TPU v7x, 32 devices: a whole 2x2x4 slice. The times are simulated.
32 devices in a mesh: bulk: 4 (over y, core), col: 8 (over z, x).
Axes of the slice: x: 2, y: 2, z: 4, core: 2. Of those that a mesh axis runs over, the one named last changes fastest.
Arguments:
- parent_front: float32 [16384, 16384], P('bulk', 'col'), may hold values from -4 to 4
- child_blocks: bfloat16 [4096, 128, 128], P(('bulk', 'col')), may hold values from -4 to 4
- child_owner: int32 [4096, 1], P(('bulk', 'col')), may hold values from 0 to 31; in each aligned block of 128 rows (0 to 127, 128 to 255, ...) at most 8 rows name the same one
- child_slot: int32 [4096], P(('bulk', 'col')), may hold values from 0 to 511
- pivot_inverse: float32 [512, 512], replicated, may hold values from -0.25 to 0.25
Outputs:
- factored_front: float32 [16384, 16384], P('bulk', 'col')
Inputs may be any that keep to these rules, and one draw needn't show every extreme that they name: `child_owner`: of the 128 child blocks of one device, at most 8 name the same owner; in every draw some device sends exactly 8 to some owner.
All inputs are finite; a program needn't handle non-finite values.
Results may differ from a plain program's by a relative error of at most 0.0003.
Values may be sent and summed in bfloat16 or wider, within the bound.
No kernel may reach another device: no remote copies, remote signals or barrier semaphores. Data moves between devices by JAX's collectives and lax.ppermute only.
A program may use at most 192 MiB of HBM per device.

v0:
```python
import jax
import jax.numpy as jnp
from jax import lax
from jax.sharding import PartitionSpec as P

PW = 512


def broadcast(block, axis, holder):
    block = jnp.where(lax.axis_index(axis) == holder, block, jnp.zeros_like(block))
    return lax.psum(block, axis)


def per_device(parent_front, child_blocks, child_owner, child_slot, pivot_inverse):
    bulk_count = lax.axis_size("bulk")
    column_count = lax.axis_size("col")
    devices = bulk_count * column_count
    row_total, column_total = parent_front.shape
    child_count, block_order, _ = child_blocks.shape
    capacity = max(2, 2 * child_count // devices)
    slots_total = devices * capacity
    highest = lax.Precision.HIGHEST
    target = child_owner[:, 0]
    owner_hits = (target[:, None] == jnp.arange(devices, dtype=jnp.int32)[None, :]).astype(
        jnp.int32
    )
    earlier = jnp.sum((jnp.cumsum(owner_hits, axis=0) - 1) * owner_hits, axis=1)
    position = target * capacity + earlier
    chosen = position[None, :] == jnp.arange(slots_total, dtype=jnp.int32)[:, None]
    filled = jnp.any(chosen, axis=1)
    source = jnp.sum(
        chosen.astype(jnp.int32) * jnp.arange(child_count, dtype=jnp.int32)[None, :], axis=1
    )
    flat_blocks = child_blocks.reshape(child_count, block_order * block_order)
    outgoing = jnp.where(filled[:, None], flat_blocks[source], jnp.zeros((), jnp.bfloat16))
    outgoing_slot = jnp.where(filled, child_slot[source], -1)
    arrived, arrived_slot = (
        lax.all_to_all(
            outgoing.reshape(devices, capacity, block_order * block_order),
            ("bulk", "col"),
            split_axis=0,
            concat_axis=0,
            tiled=True,
        ),
        lax.all_to_all(
            outgoing_slot.reshape(devices, capacity),
            ("bulk", "col"),
            split_axis=0,
            concat_axis=0,
            tiled=True,
        ),
    )
    arrived = arrived.reshape(slots_total, block_order * block_order)
    arrived_slot = arrived_slot.reshape(slots_total)
    tile_rows = row_total // block_order
    tile_columns = column_total // block_order
    placement = (
        arrived_slot[None, :] == jnp.arange(tile_rows * tile_columns, dtype=jnp.int32)[:, None]
    ).astype(jnp.bfloat16)
    assembled = jnp.dot(placement, arrived, preferred_element_type=jnp.float32)
    assembled = assembled.reshape(tile_rows, tile_columns, block_order, block_order).transpose(
        0, 2, 1, 3
    )
    extended = parent_front + assembled.reshape(row_total, column_total)
    bulk_index = lax.axis_index("bulk")
    column_index = lax.axis_index("col")
    row_global = bulk_index * row_total + jnp.arange(row_total, dtype=jnp.int32)
    column_global = column_index * column_total + jnp.arange(column_total, dtype=jnp.int32)
    below = (row_global >= PW)[:, None]
    right_side = (column_global >= PW)[None, :]
    pivot_rows = broadcast(extended[:PW, :], "bulk", 0)
    upper_masked = jnp.where(right_side, pivot_rows, 0.0)
    lower_local = jnp.where(below, jnp.dot(extended[:, :PW], pivot_inverse, precision=highest), 0.0)
    lower_factor = broadcast(lower_local, "col", 0)
    update = jnp.dot(lower_factor, upper_masked, precision=highest)
    result = extended - update
    panel_zone = below & (column_global[:PW] < PW)[None, :]
    leading = jnp.where(panel_zone, lower_factor, result[:, :PW])
    return jnp.concatenate([leading, result[:, PW:]], axis=1)


def solution(mesh):
    in_specs = (
        P("bulk", "col"),
        P(("bulk", "col"), None, None),
        P(("bulk", "col"), None),
        P(("bulk", "col")),
        P(),
    )
    out_specs = P("bulk", "col")
    return jax.shard_map(
        per_device, mesh=mesh, in_specs=in_specs, out_specs=out_specs, check_vma=False
    )
```

profile of v0, /device:TPU:0, one launch (start us, length us, event | category | flops | bytes accessed | tf_op | source)
XLA Modules:
  0.0 777.6 jit_solution(2080358833146444149)
XLA Ops:
  6.5 0.0 copy-start
  6.5 0.8 fusion.13
  7.4 0.2 reduce_window_sum.11
  7.5 0.8 select_reduce_fusion.1
  8.4 0.7 multiply_add_fusion.1
  9.0 0.1 select_reduce_fusion
  9.2 0.1 fusion.12
  9.3 1.9 gather_fusion
  11.2 0.7 select_n.62
  11.9 7.3 all-to-all-start
  19.2 0.1 broadcast_in_dim.54
  19.3 7.7 copy.22
  27.0 19.5 %gather_fusion.1 = bf16[256,16384]{1,0:T(8,128)(2,1)} fusion(bf16[128,16384]{1,0:T(8,128)(2,1)} %bitcast.31, s32[1024]{0:T(1024)S(1)} %pad_clamp_fusion), kind=kCustom, calls=%fused_computation.1 | custom fusion | bytes 16778240 | tf_op jit(solution)/shard_map/gather | solution.py:35
  46.5 7.2 bitcast_select_fusion
  53.7 0.0 all-to-all-done
  53.7 6.0 all-to-all-start.1
  59.6 0.0 all-reduce.5.cloned.1.call-start
  59.7 0.5 broadcast.100
  60.2 0.7 reduce.3
  60.9 0.1 eq.65
  61.0 184.5 %all-to-all-done.1 = bf16[32,8,16384]{2,1,0:T(8,128)(2,1)} async-done(((bf16[32,8,16384]{2,1,0:T(8,128)(2,1)}), bf16[32,8,16384]{2,1,0:T(8,128)(2,1)}, u32[]{:S(2)}, u32[]{:S(2)}) %all-to-all-start.1) | async-done | bytes 8388640 | tf_op jit(solution)/shard_map/all_to_all | solution.py:38
  245.5 11.9 %copy.14 = bf16[16384,256]{1,0:T(8,128)(2,1)} copy(bf16[16384,256]{0,1:T(8,128)(2,1)} %bitcast.8) | data formatting | bytes 16777216 | tf_op jit(solution)/shard_map/dot_general | solution.py:60
  257.3 17.4 %fusion.7 = f32[32,16,128,128]{3,1,2,0:T(8,128)} fusion(bf16[128,128,256,1]{2,1,0,3:T(8,128)(2,1)} %bitcast.33, s32[32,16]{1,0:T(8,128)S(1)} %multiply_add_fusion, s32[256]{0:T(256)S(1)} %eq.65), kind=kOutput, calls=%fused_computation.15 | convolution fusion | flops 4295098368 | bytes 41946112 | tf_op jit(solution)/shard_map/dot_general | solution.py:60
  274.8 37.1 %bitcast_add_fusion = f32[4096,2048]{1,0:T(8,128)} fusion(f32[4096,2048]{1,0:T(8,128)} %param.5, f32[512,8,16,128]{3,2,1,0:T(8,128)} %bitcast.32), kind=kLoop, calls=%fused_computation.2 | loop fusion | flops 8388608 | bytes 100663296 | tf_op jit(solution)/shard_map/add | solution.py:64
  311.9 4.7 slice_select_fusion.1
  316.6 0.0 all-reduce.5.cloned.1.call-update
  316.6 0.0 all-reduce.3.cloned.1.call-start
  316.7 0.0 copy-done
  316.7 28.1 %select_select_fusion = f32[4096,512]{1,0:T(8,128)} fusion(f32[512,512]{1,0:T(8,128)S(1)} %copy-done, f32[4096,2048]{1,0:T(8,128)} %bitcast_add_fusion, pred[]{:T(512)S(6)} %eq.58, pred[4096]{0:T(1024)(128)(4,1)S(1)} %add_compare_fusion), kind=kOutput, calls=%fused_computation.9 | convolution fusion | flops 12889096192 | bytes 17829888 | tf_op jit(solution)/shard_map/dot_general | solution.py:73
  344.8 0.0 all-reduce.3.cloned.1.call-update
  344.9 58.4 %all-reduce.5.cloned.1.call-done = f32[512,2048]{1,0:T(8,128)} async-done(((f32[512,2048]{1,0:T(8,128)}), f32[512,2048]{1,0:T(8,128)}) %all-reduce.5.cloned.1.call-update) | async-done | bytes 4194320 | tf_op jit(solution)/shard_map/psum | solution.py:11
  403.3 275.0 %all-reduce.3.cloned.1.call-done = f32[4096,512]{1,0:T(8,128)} async-done(((f32[4096,512]{1,0:T(8,128)}), f32[4096,512]{1,0:T(8,128)}) %all-reduce.3.cloned.1.call-update) | async-done | bytes 8388624 | tf_op jit(solution)/shard_map/psum | solution.py:11
  678.2 61.8 %convolution_subtract_fusion = f32[4096,2048]{1,0:T(8,128)} fusion(f32[4096,2048]{1,0:T(8,128)} %bitcast_add_fusion, f32[4096,512]{1,0:T(8,128)} %all-reduce.3.cloned.1.call-done, f32[512,2048]{1,0:T(8,128)} %all-reduce.5.cloned.1.call-done, pred[2048]{0:T(1024)(128)(4,1)S(1)} %broadcast_compare_fusion), kind=kOutput, calls=%fused_computation.4 | convolution fusion | flops 51549044736 | bytes 79693824 | tf_op jit(solution)/shard_map/dot_general | solution.py:75
  740.0 0.0 slice-start
  740.0 10.2 %slice_select_fusion = f32[4096,512]{1,0:T(8,128)} fusion(f32[4096,512]{1,0:T(8,128)} %all-reduce.3.cloned.1.call-done, f32[4096,2048]{1,0:T(8,128)} %convolution_subtract_fusion, pred[512]{0:T(512)(128)(4,1)S(1)} %slice_compare_fusion, pred[4096]{0:T(1024)(128)(4,1)S(1)} %add_compare_fusion), kind=kLoop, calls=%fused_computation.5 | loop fusion | flops 4194304 | bytes 25170432 | tf_op jit(solution)/shard_map/jit(_where)/select_n | solution.py:78
  750.1 5.9 slice-done
  756.0 0.0 copy-start.1
  756.1 14.5 %pad_maximum_fusion = f32[4096,2048]{1,0:T(8,128)} fusion(f32[4096,1536]{1,0:T(8,128)S(1)} %slice-done, f32[4096,512]{1,0:T(8,128)} %slice_select_fusion), kind=kLoop, calls=%fused_computation.3 | loop fusion | flops 8388608 | bytes 67108864 | tf_op jit(solution)/shard_map/concatenate | solution.py:79
  770.5 0.0 copy-done.1
  (8 shorter events, 0.0 us)
Async XLA Ops:
  6.5 310.1 %copy-start = (f32[512,512]{1,0:T(8,128)S(1)}, f32[512,512]{1,0:T(8,128)}, u32[]{:S(2)}) copy-start(f32[512,512]{1,0:T(8,128)} %param.9) | copy-start | bytes 3145732
  11.9 41.8 %all-to-all-start = ((s32[32,1,8]{2,1,0:T(1,128)}), s32[32,1,8]{2,1,0:T(1,128)S(1)}, u32[]{:S(2)}, u32[]{:S(2)}) async-start(s32[32,1,8]{2,1,0:T(1,128)} %bitcast.3), calls=%async_computation | async-start | bytes 32768 | tf_op jit(solution)/shard_map/all_to_all | solution.py:45
  53.7 191.8 %all-to-all-start.1 = ((bf16[32,8,16384]{2,1,0:T(8,128)(2,1)}), bf16[32,8,16384]{2,1,0:T(8,128)(2,1)}, u32[]{:S(2)}, u32[]{:S(2)}) async-start(bf16[32,8,16384]{2,1,0:T(8,128)(2,1)} %bitcast_select_fusion), calls=%async_computation.1 | async-start | bytes 16777216 | tf_op jit(solution)/shard_map/all_to_all | solution.py:38
  59.6 343.6 %all-reduce.5.cloned.1.call-start = ((), (), s32[]{:S(2)}) async-start(), calls=%async_computation.3 | async-start | bytes 8388608 | tf_op jit(solution)/shard_map/psum | solution.py:11
  316.6 361.6 %all-reduce.3.cloned.1.call-start = ((), (), s32[]{:S(2)}) async-start(), calls=%async_computation.2 | async-start | bytes 16777216 | tf_op jit(solution)/shard_map/psum | solution.py:11
  740.0 16.1 %slice-start = ((f32[4096,2048]{1,0:T(8,128)}), f32[4096,1536]{1,0:T(8,128)S(1)}, s32[]{:S(2)}) async-start(f32[4096,2048]{1,0:T(8,128)} %convolution_subtract_fusion), calls=%async_computation.4 | async-start | bytes 50331648 | tf_op jit(solution)/shard_map/slice | solution.py:79
  756.0 14.5 %copy-start.1 = (f32[512,512]{1,0:T(8,128)S(1)}, f32[512,512]{1,0:T(8,128)}, u32[]{:S(2)}) copy-start(f32[512,512]{1,0:T(8,128)} %param.9) | copy-start | bytes 3145732
Sparse Core Ops, SparseCore 0:
  316.7 86.5 all-reduce.4
  407.7 270.5 all-reduce.2
where the time goes:
time: 788 us; the launch traced here: 778 us
  waiting for transfers between devices  518 us (66%)
  matrix products  107 us (14%)
  other arithmetic  77.1 us (10%)
  local copies, waits for them, and re-layouts  48.2 us (6%)
  between operations  13.7 us (2%)
  starting transfers between devices  13.3 us (2%)
    psum x2, waiting for transfers between devices, broadcast(): return lax.psum(block, axis)  333 us
    all_to_all x1, waiting for transfers between devices, per_device(): lax.all_to_all(outgoing.reshape(devices, capacity, block_order * block_or...  184 us
    dot_general x1, matrix products, per_device(): update = jnp.dot(lower_factor, upper_masked, precision=highest)  61.8 us
    add x1, other arithmetic, per_device(): extended = parent_front + assembled.reshape(row_total, column_total)  37.1 us
    dot_general x1, matrix products, per_device(): jnp.dot(extended[:, :PW], pivot_inverse, precision=highest)  28.1 us
    gather x1, local copies, waits for them, and re-layouts, per_device(): flat_blocks[source]  19.5 us
    dot_general x1, matrix products, per_device(): assembled = jnp.dot(placement, arrived, preferred_element_type=jnp.float32)  17.4 us
  transfers between devices with their start and end apart: 4, of which 3 were waited for; matrix products, arithmetic and copies ran while one was open for 8% of the time, Pallas kernels for 0%

commit v1 on v0

v1 whole, which is shorter than its diff:
```python
import functools

import jax
import jax.numpy as jnp
from jax import lax
from jax.experimental import pallas as pl
from jax.experimental.pallas import tpu as pltpu
from jax.sharding import PartitionSpec as P

PW = 512
TILE = 128
META = 16
CODE_TOP = 32600.0
VMEM_LIMIT = 56 * 1024 * 1024

F32 = jnp.float32
BF16 = jnp.bfloat16
I32 = jnp.int32


def compiler_params(semantics=None):
    return pltpu.CompilerParams(dimension_semantics=semantics, vmem_limit_bytes=VMEM_LIMIT)


def pack_kernel(devices, capacity, owner_ref, slot_ref, child_ref, out_ref, filled, slots, meta, sem, meta_sem):
    child_count = owner_ref.shape[0]

    def clear(d, _):
        filled[d] = 0
        return 0

    lax.fori_loop(0, devices, clear, 0)

    def clear_slot(i, _):
        slots[i] = -1
        return 0

    lax.fori_loop(0, devices * capacity, clear_slot, 0)

    def place(i, _):
        d = owner_ref[i]
        k = filled[d]
        filled[d] = k + 1
        slots[d * capacity + k] = slot_ref[i]
        pltpu.make_async_copy(
            child_ref.at[i], out_ref.at[d, pl.ds(pl.multiple_of(k * TILE, TILE), TILE)], sem
        ).start()
        return 0

    lax.fori_loop(0, child_count, place, 0)
    lane = lax.broadcasted_iota(I32, (META, TILE), 1)
    row = lax.broadcasted_iota(I32, (META, TILE), 0)

    def write_meta(d, _):
        value = jnp.full((META, TILE), -1, I32)
        for k in range(capacity):
            value = jnp.where(lane == k, slots[d * capacity + k], value)
        coded = jnp.where(row == 0, value >> 4, value & 15)
        meta[d] = coded.astype(F32).astype(BF16)
        return 0

    lax.fori_loop(0, devices, write_meta, 0)
    copy = pltpu.make_async_copy(meta, out_ref.at[:, pl.ds(capacity * TILE, META)], meta_sem)
    copy.start()
    pltpu.make_async_copy(child_ref, child_ref, sem).wait()
    copy.wait()


def pack(owner, slot, child, devices, capacity):
    rows = capacity * TILE + META
    return pl.pallas_call(
        functools.partial(pack_kernel, devices, capacity),
        out_shape=jax.ShapeDtypeStruct((devices, rows, TILE), BF16),
        in_specs=[
            pl.BlockSpec(memory_space=pltpu.SMEM),
            pl.BlockSpec(memory_space=pltpu.SMEM),
            pl.BlockSpec(memory_space=pl.ANY),
        ],
        out_specs=pl.BlockSpec(memory_space=pl.ANY),
        scratch_shapes=[
            pltpu.SMEM((devices,), I32),
            pltpu.SMEM((devices * capacity,), I32),
            pltpu.VMEM((devices, META, TILE), BF16),
            pltpu.SemaphoreType.DMA,
            pltpu.SemaphoreType.DMA,
        ],
        compiler_params=compiler_params(),
        name="pack_children",
    )(owner, slot, child)


def read_slots(arrived, capacity):
    coded = arrived[:, capacity * TILE : capacity * TILE + 2, :capacity].astype(I32)
    return (coded[:, 0] * 16 + coded[:, 1]).reshape(-1)


def build_lists(key_ref, head, following, width):
    def clear(i, _):
        head[i] = -1
        return 0

    lax.fori_loop(0, head.shape[0], clear, 0)

    def add(i, _):
        key = key_ref[i]

        @pl.when(key >= 0)
        def _():
            strip = key // width
            following[i] = head[strip]
            head[strip] = i

        return 0

    lax.fori_loop(0, key_ref.shape[0], add, 0)


def add_strip(key_ref, arrived_ref, out, head, following, strip, width, capacity, row):
    def body(i):
        column = pl.multiple_of((key_ref[i] % width) * TILE, TILE)
        start = pl.multiple_of((i % capacity) * TILE, TILE)
        block = arrived_ref[i // capacity, pl.ds(start, TILE), :]
        spot = (pl.ds(row, TILE), pl.ds(column, TILE))
        out[spot] = out[spot] + block.astype(F32)
        return following[i]

    lax.while_loop(lambda i: i >= 0, body, head[strip])


def extend_kernel(width, capacity, key_ref, base_ref, arrived_ref, out_ref, head, following):
    step = pl.program_id(0)

    @pl.when(step == 0)
    def _():
        build_lists(key_ref, head, following, width)

    out_ref[...] = base_ref[...]
    strips = base_ref.shape[0] // TILE
    for s in range(strips):
        add_strip(
            key_ref, arrived_ref, out_ref, head, following, step * strips + s, width, capacity, s * TILE
        )


def extend(base, arrived, key, width, capacity, rows, columns, alias=False):
    return pl.pallas_call(
        functools.partial(extend_kernel, width, capacity),
        out_shape=jax.ShapeDtypeStruct((rows, columns), F32),
        grid_spec=pltpu.PrefetchScalarGridSpec(
            num_scalar_prefetch=1,
            grid=(rows // TILE,),
            in_specs=[
                pl.BlockSpec((TILE, columns), lambda i, k: (i, 0)),
                pl.BlockSpec(memory_space=pltpu.VMEM),
            ],
            out_specs=pl.BlockSpec((TILE, columns), lambda i, k: (i, 0)),
            scratch_shapes=[
                pltpu.SMEM((rows // TILE,), I32),
                pltpu.SMEM((key.shape[0],), I32),
            ],
        ),
        input_output_aliases={1: 0} if alias else {},
        compiler_params=compiler_params(("arbitrary",)),
        name="extend_add",
    )(key, base, arrived)


def code_rows(values):
    top = jnp.maximum(jnp.max(jnp.abs(values), axis=1, keepdims=True), 1e-30)
    exponent = jnp.ceil(jnp.log2(top) * 64.0)
    code = jnp.round(values * (CODE_TOP * jnp.exp2(exponent * (-1.0 / 64.0))))
    return code.astype(I32), exponent


def diagonal(n):
    return lax.broadcasted_iota(I32, (n, n), 0) == lax.broadcasted_iota(I32, (n, n), 1)


def panel_kernel(width, capacity, key_ref, base_ref, arrived_ref, out_ref, work, head, following):
    step = pl.program_id(0)

    @pl.when(step == 0)
    def _():
        build_lists(key_ref, head, following, width)

    work[...] = base_ref[...]
    rows = base_ref.shape[0]
    strips = rows // TILE
    eye = diagonal(TILE)
    out_ref[0, pl.ds(rows, META), :] = jnp.zeros((META, out_ref.shape[2]), jnp.int16)
    for s in range(strips):
        add_strip(
            key_ref, arrived_ref, work, head, following, step * strips + s, width, capacity, s * TILE
        )
        code, exponent = code_rows(work[pl.ds(s * TILE, TILE), :])
        out_ref[0, pl.ds(s * TILE, TILE), :] = code.astype(jnp.int16)
        line = jnp.sum(jnp.where(eye, exponent, 0.0), axis=0, keepdims=True)
        out_ref[0, pl.ds(rows, META), pl.ds(s * TILE, TILE)] = (
            jnp.broadcast_to(line, (META, TILE)).astype(I32).astype(jnp.int16)
        )


def code_panel(base, arrived, key, capacity, slices):
    rows = base.shape[0] // slices
    width = PW // TILE
    return pl.pallas_call(
        functools.partial(panel_kernel, width, capacity),
        out_shape=jax.ShapeDtypeStruct((slices, rows + META, PW), jnp.int16),
        grid_spec=pltpu.PrefetchScalarGridSpec(
            num_scalar_prefetch=1,
            grid=(slices,),
            in_specs=[
                pl.BlockSpec((rows, PW), lambda i, k: (i, 0)),
                pl.BlockSpec(memory_space=pltpu.VMEM),
            ],
            out_specs=pl.BlockSpec((1, rows + META, PW), lambda i, k: (i, 0, 0)),
            scratch_shapes=[
                pltpu.VMEM((rows, PW), F32),
                pltpu.SMEM((base.shape[0] // TILE,), I32),
                pltpu.SMEM((key.shape[0],), I32),
            ],
        ),
        compiler_params=compiler_params(("arbitrary",)),
        name="code_panel",
    )(key, base, arrived)


def right_kernel(flag_ref, pivot_ref, upper_ref, high_ref, low_ref):
    step = pl.program_id(0)
    columns = upper_ref.shape[1]
    row = lax.broadcasted_iota(I32, (PW, columns), 0)
    column = lax.broadcasted_iota(I32, (PW, columns), 1) + step * columns
    in_panel = jnp.logical_and(column < PW, flag_ref[1] == 0)
    upper = jnp.where(in_panel, jnp.where(row == column, -1.0, 0.0), upper_ref[...])
    right = jnp.dot(pivot_ref[...], upper, precision=lax.Precision.HIGHEST, preferred_element_type=F32)
    high = right.astype(BF16)
    high_ref[...] = high
    low_ref[...] = (right - high.astype(F32)).astype(BF16)


def right_factor(flags, pivot_inverse, upper):
    columns = upper.shape[1]
    block = min(512, columns)
    spec = pl.BlockSpec((PW, block), lambda i, f: (0, i))
    return pl.pallas_call(
        right_kernel,
        out_shape=[jax.ShapeDtypeStruct((PW, columns), BF16)] * 2,
        grid_spec=pltpu.PrefetchScalarGridSpec(
            num_scalar_prefetch=1,
            grid=(columns // block,),
            in_specs=[pl.BlockSpec((PW, PW), lambda i, f: (0, 0)), spec],
            out_specs=[spec, spec],
        ),
        compiler_params=compiler_params(("arbitrary",)),
        name="right_factor",
    )(flags, pivot_inverse, upper)


def update_kernel(block, per_slice, flag_ref, slice_ref, base_ref, code_ref, scale_ref, high_ref, low_ref, out_ref):
    step = pl.program_id(0)
    row_block = slice_ref[step // per_slice] * per_slice + lax.rem(step, per_slice)
    above = jnp.logical_and(flag_ref[0] == 0, row_block < PW // block)

    @pl.when(above)
    def _():
        out_ref[...] = base_ref[...]

    @pl.when(jnp.logical_not(above))
    def _():
        code = code_ref[0].astype(I32)
        upper_part = (code + 128) >> 8
        lower_part = (code - upper_part * 256).astype(F32).astype(BF16)
        upper_part = (upper_part * 256).astype(F32).astype(BF16)
        high, low = high_ref[...], low_ref[...]
        product = (
            jnp.dot(lower_part, high, preferred_element_type=F32)
            + jnp.dot(upper_part, low, preferred_element_type=F32)
        ) + jnp.dot(upper_part, high, preferred_element_type=F32)
        eye = diagonal(TILE)
        for s in range(block // TILE):
            line = scale_ref[0, :, pl.ds(s * TILE, TILE)].astype(I32).astype(F32)[:1]
            exponent = jnp.sum(jnp.where(eye, line, 0.0), axis=1, keepdims=True)
            scale = jnp.exp2(exponent * (1.0 / 64.0)) * (1.0 / CODE_TOP)
            rows = slice(s * TILE, (s + 1) * TILE)
            update = scale * product[rows]
            out_ref[pl.ds(s * TILE, TILE), pl.ds(PW, out_ref.shape[1] - PW)] = (
                base_ref[pl.ds(s * TILE, TILE), pl.ds(PW, out_ref.shape[1] - PW)] - update[:, PW:]
            )
            kept = jnp.where(flag_ref[1] == 0, 0.0, 1.0)
            out_ref[pl.ds(s * TILE, TILE), pl.ds(0, PW)] = (
                base_ref[pl.ds(s * TILE, TILE), pl.ds(0, PW)] * kept - update[:, :PW]
            )


def update_rows(flags, slice_ids, base, codes, high, low):
    rows, columns = base.shape
    slices, slice_rows, _ = codes.shape
    slice_rows -= META
    block = min(256, slice_rows)
    per_slice = slice_rows // block

    def base_map(i, f, s):
        return (s[i // per_slice] * per_slice + lax.rem(i, per_slice), 0)

    return pl.pallas_call(
        functools.partial(update_kernel, block, per_slice),
        out_shape=jax.ShapeDtypeStruct((rows, columns), F32),
        grid_spec=pltpu.PrefetchScalarGridSpec(
            num_scalar_prefetch=2,
            grid=(slices * per_slice,),
            in_specs=[
                pl.BlockSpec((block, columns), base_map),
                pl.BlockSpec((1, block, PW), lambda i, f, s: (i // per_slice, lax.rem(i, per_slice), 0)),
                pl.BlockSpec(
                    (1, META, block),
                    lambda i, f, s: (i // per_slice, slice_rows // META, lax.rem(i, per_slice)),
                ),
                pl.BlockSpec((PW, columns), lambda i, f, s: (0, 0)),
                pl.BlockSpec((PW, columns), lambda i, f, s: (0, 0)),
            ],
            out_specs=pl.BlockSpec((block, columns), base_map),
        ),
        compiler_params=compiler_params(("arbitrary",)),
        name="update_rows",
    )(flags, slice_ids, base, codes, codes, high, low)


def ring_order(count):
    return list(range(0, count, 2)) + list(range(count - 1, 0, -2))


def ring_gather(own, axis):
    count = lax.axis_size(axis)
    order = ring_order(count)
    ahead = [(order[i], order[(i + 1) % count]) for i in range(count)]
    back = [(b, a) for a, b in ahead]
    place = jnp.zeros((), I32)
    index = lax.axis_index(axis)
    for p, d in enumerate(order):
        place = jnp.where(index == d, p, place)
    table = jnp.array(order, I32)
    pieces, whose = [own], [index]
    left = right = own
    for step in range(1, count // 2):
        left, right = lax.ppermute(left, axis, ahead), lax.ppermute(right, axis, back)
        pieces += [left, right]
        whose += [table[(place + count - step) % count], table[(place + step) % count]]
    half = own.shape[0] // 2
    pieces.append(
        jnp.concatenate([lax.ppermute(left[:half], axis, ahead), lax.ppermute(right[half:], axis, back)], 0)
    )
    whose.append(table[(place + count // 2) % count])
    return pieces, jnp.stack(whose)


def scatter_first(parts, axis):
    count = lax.axis_size(axis)
    mine = jnp.where(lax.axis_index(axis) == 0, parts[0], jnp.zeros((), parts.dtype))
    for k in range(1, count):
        mine = mine + lax.ppermute(parts[k], axis, [(0, k)])
    return mine


def tree_broadcast(block, axis):
    count = lax.axis_size(axis)
    index = lax.axis_index(axis)
    reach = count // 2
    while reach >= 1:
        sent = lax.ppermute(block, axis, [(i, i + reach) for i in range(0, count, 2 * reach)])
        block = jnp.where(index % (2 * reach) == reach, sent, block)
        reach //= 2
    return block


def per_device(parent, child, owner, slot, pivot_inverse):
    bulk_count, column_count = lax.axis_size("bulk"), lax.axis_size("col")
    devices = bulk_count * column_count
    rows, columns = parent.shape
    child_count = child.shape[0]
    capacity = max(2, 2 * child_count // devices)
    width = columns // TILE
    bulk_index, column_index = lax.axis_index("bulk"), lax.axis_index("col")
    flags = jnp.stack([bulk_index, column_index]).astype(I32)

    outgoing = pack(owner[:, 0], slot, child, devices, capacity)
    arrived = lax.all_to_all(outgoing, ("bulk", "col"), split_axis=0, concat_axis=0, tiled=True)
    slots = read_slots(arrived, capacity)
    strip, tile_column = slots // width, slots % width
    valid = slots >= 0
    pivot_tiles = PW // TILE
    in_panel = valid & (tile_column < pivot_tiles)
    in_pivot = valid & (strip < pivot_tiles)
    panel_key = jnp.where(in_panel, strip * pivot_tiles + tile_column, -1)
    pivot_key = jnp.where(in_pivot, slots, -1)
    taken = in_panel & (column_index == 0) & ~(in_pivot & (bulk_index == 0))
    rest_key = jnp.where(valid & ~taken, slots, -1)

    codes = code_panel(parent, arrived, panel_key, capacity, column_count)
    upper = extend(parent, arrived, pivot_key, width, capacity, PW, columns)
    upper = tree_broadcast(upper, "bulk")
    high, low = right_factor(flags, pivot_inverse, upper)
    pieces, whose = ring_gather(scatter_first(codes, "col"), "col")
    result = update_rows(flags, whose, parent, jnp.stack(pieces), high, low)
    return extend(result, arrived, rest_key, width, capacity, rows, columns, alias=True)


def solution(mesh):
    in_specs = (
        P("bulk", "col"),
        P(("bulk", "col"), None, None),
        P(("bulk", "col"), None),
        P(("bulk", "col")),
        P(),
    )
    return jax.shard_map(
        per_device, mesh=mesh, in_specs=in_specs, out_specs=P("bulk", "col"), check_vma=False
    )
```

time: 788 us -> 591 us (0.75)
  waiting for transfers between devices: 518 us -> 95 us
  Pallas kernels: 0 us -> 243 us
  blocking collectives: 0 us -> 195 us
  matrix products: 107 us -> 0 us
  other arithmetic: 77.1 us -> 12.5 us
  local copies, waits for them, and re-layouts: 48.2 us -> 14.4 us
  starting transfers between devices: 13.3 us -> 28.2 us
  between operations: 13.7 us -> 0.14 us
    psum x2 -> x0, waiting for transfers between devices: 333 us -> none  [broadcast(): return lax.psum(block, axis)]
    pallas_call x0 -> x6, Pallas kernels: none -> 243 us  [the longest x1 131 us: pack(): pl.pallas_call(functools.partial(pack_kernel, devices, capacity), out_sha...]
    all_to_all x0 -> x1, blocking collectives: none -> 195 us  [per_device(): lax.all_to_all(outgoing, ('bulk', 'col'), split_axis=0, concat_axis=0, ti...]
    all_to_all x2 -> x0, waiting for transfers between devices: 184 us -> none  [the longest x1 184 us: per_device(): lax.all_to_all(outgoing.reshape(devices, capacity, block_order * block_or...]
    dot_general x3 -> x0, matrix products: 107 us -> none  [the longest x1 61.8 us: per_device(): update = jnp.dot(lower_factor, upper_masked, precision=highest)]
    ppermute x0 -> x17, waiting for transfers between devices: none -> 95 us  [the longest x7 49.6 us: scatter_first(): mine = mine + lax.ppermute(parts[k], axis, [(0, k)])]
    add x3 -> x1, other arithmetic: 37.8 us -> 0.06 us  [read_slots(): return (coded[:, 0] * 16 + coded[:, 1]).reshape(-1)]
    ppermute x0 -> x17, starting transfers between devices: none -> 28.2 us  [the longest x7 11 us: scatter_first(): mine = mine + lax.ppermute(parts[k], axis, [(0, k)])]
  transfers between devices with their start and end apart: 4 -> 17, of which waited for: 3 -> 12; matrix products, arithmetic and copies ran while one was open for 8% -> 2% of each run, Pallas kernels for 0% -> 2%
where the time goes in v1:
time: 591 us; the launch traced here: 588 us
  Pallas kernels  243 us (41%)
  blocking collectives  195 us (33%)
  waiting for transfers between devices  95 us (16%)
  starting transfers between devices  28.2 us (5%)
  local copies, waits for them, and re-layouts  14.4 us (2%)
  other arithmetic  12.5 us (2%)
    all_to_all x1, blocking collectives, per_device(): lax.all_to_all(outgoing, ('bulk', 'col'), split_axis=0, concat_axis=0, ti...  195 us
    pallas_call x1, Pallas kernels, pack(): pl.pallas_call(functools.partial(pack_kernel, devices, capacity), out_sha...  131 us
    ppermute x7, waiting for transfers between devices, scatter_first(): mine = mine + lax.ppermute(parts[k], axis, [(0, k)])  49.6 us
    pallas_call x2, Pallas kernels, extend(): pl.pallas_call(functools.partial(extend_kernel, width, capacity), out_sha...  48.6 us
    pallas_call x1, Pallas kernels, update_rows(): pl.pallas_call(functools.partial(update_kernel, block, per_slice), out_sh...  37.8 us
    ppermute x2, waiting for transfers between devices, tree_broadcast(): lax.ppermute(block, axis, [(i, i + reach) for i in range(0, count, 2 * re...  29.2 us
    pallas_call x1, Pallas kernels, code_panel(): pl.pallas_call(functools.partial(panel_kernel, width, capacity), out_shap...  14.5 us
  transfers between devices with their start and end apart: 17, of which 12 were waited for; matrix products, arithmetic and copies ran while one was open for 2% of the time, Pallas kernels for 2%

profile of v1, /device:TPU:0, one launch (start us, length us, event | category | flops | bytes accessed | tf_op | source)
XLA Modules:
  0.0 587.8 jit_solution(5694418686031426716)
XLA Ops:
  0.0 130.7 %pack_children.1 = bf16[32,1040,128]{2,1,0:T(8,128)(2,1)} custom-call(s32[128]{0:T(128)} %bitcast.52, s32[128]{0:T(128)} %slot_ref.1, bf16[128,128,128]{2,1,0:T(8,128)(2,1)} %child_ref.1), custom_call_target="tpu_custom_call" | custom-call | tf_op jit(solution)/shard_map/pack_children/pallas_call | solution.py:71
  130.7 195.0 %all_to_all.5.arrived_ref = bf16[32,1040,128]{2,1,0:T(8,128)(2,1)S(1)} all-to-all(bf16[32,1040,128]{2,1,0:T(8,128)(2,1)} %pack_children.1), channel_id=1, replica_groups=mesh['bulk'=4,'col'=8] {'bulk','col'}, dimensions={0} | all-to-all | bytes 17039360 | tf_op jit(solution)/shard_map/all_to_all | solution.py:386
  325.7 3.3 copy-done
  329.0 0.1 fusion.9
  329.1 0.1 add.112
  329.2 0.6 broadcast_select_fusion.2
  329.7 8.7 %extend_add.2 = f32[512,2048]{1,0:T(8,128)} custom-call(s32[256]{0:T(256)} %get-tuple-element.9.key_ref, f32[4096,2048]{1,0:T(8,128)} %base_ref.5, bf16[32,1040,128]{2,1,0:T(8,128)(2,1)} %copy-done), custom_call_target="tpu_custom_call" | custom-call | tf_op jit(solution)/shard_map/extend_add/pallas_call | solution.py:146
  338.5 4.3 collective-permute-start.15
  342.8 0.6 add_select_fusion
  343.4 14.5 %code_panel.1 = s16[8,528,512]{2,1,0:T(8,128)(2,1)} custom-call(s32[256]{0:T(256)} %get-tuple-element.20.key_ref, f32[4096,2048]{1,0:T(8,128)} %base_ref.5, bf16[32,1040,128]{2,1,0:T(8,128)(2,1)} %copy-done), custom_call_target="tpu_custom_call" | custom-call | tf_op jit(solution)/shard_map/code_panel/pallas_call | solution.py:206
  358.0 29.2 %collective-permute-done.15 = f32[512,2048]{1,0:T(8,128)} collective-permute-done((f32[512,2048]{1,0:T(8,128)}, f32[512,2048]{1,0:T(8,128)}, u32[]{:S(2)}, u32[]{:S(2)}) %collective-permute-start.15) | collective-permute-done | bytes 4194336 | tf_op jit(solution)/shard_map/ppermute | solution.py:369
  387.1 0.0 copy-done.2
  387.1 3.0 broadcast_select_fusion
  390.2 3.3 collective-permute-start.16
  393.4 0.0 copy-done.1
  393.4 0.3 slice_bitcast_fusion.6
  393.7 0.0 copy-start.3
  393.7 2.9 collective-permute-start
  396.6 1.5 collective-permute-start.6
  398.1 1.3 collective-permute-start.5
  399.5 1.3 collective-permute-start.4
  400.8 2.6 collective-permute-done
  403.5 1.3 collective-permute-start.3
  404.8 2.1 collective-permute-done.6
  406.9 1.3 collective-permute-start.2
  408.2 8.5 %collective-permute-done.5 = s16[528,512]{1,0:T(8,128)(2,1)S(1)} collective-permute-done((s16[528,512]{1,0:T(8,128)(2,1)S(1)}, s16[528,512]{1,0:T(8,128)(2,1)S(1)}, u32[]{:S(2)}, u32[]{:S(2)}) %collective-permute-start.5) | collective-permute-done | bytes 540704 | tf_op jit(solution)/shard_map/ppermute | solution.py:360
  416.8 1.3 collective-permute-start.1
  418.1 9.5 %collective-permute-done.4 = s16[528,512]{1,0:T(8,128)(2,1)S(1)} collective-permute-done((s16[528,512]{1,0:T(8,128)(2,1)S(1)}, s16[528,512]{1,0:T(8,128)(2,1)S(1)}, u32[]{:S(2)}, u32[]{:S(2)}) %collective-permute-start.4) | collective-permute-done | bytes 540704 | tf_op jit(solution)/shard_map/ppermute | solution.py:360
  427.6 9.1 %collective-permute-done.3 = s16[528,512]{1,0:T(8,128)(2,1)S(1)} collective-permute-done((s16[528,512]{1,0:T(8,128)(2,1)S(1)}, s16[528,512]{1,0:T(8,128)(2,1)S(1)}, u32[]{:S(2)}, u32[]{:S(2)}) %collective-permute-start.3) | collective-permute-done | bytes 540704 | tf_op jit(solution)/shard_map/ppermute | solution.py:360
  436.7 9.0 %collective-permute-done.2 = s16[528,512]{1,0:T(8,128)(2,1)S(1)} collective-permute-done((s16[528,512]{1,0:T(8,128)(2,1)S(1)}, s16[528,512]{1,0:T(8,128)(2,1)S(1)}, u32[]{:S(2)}, u32[]{:S(2)}) %collective-permute-start.2) | collective-permute-done | bytes 540704 | tf_op jit(solution)/shard_map/ppermute | solution.py:360
  445.7 8.7 %collective-permute-done.1 = s16[528,512]{1,0:T(8,128)(2,1)S(1)} collective-permute-done((s16[528,512]{1,0:T(8,128)(2,1)S(1)}, s16[528,512]{1,0:T(8,128)(2,1)S(1)}, u32[]{:S(2)}, u32[]{:S(2)}) %collective-permute-start.1) | collective-permute-done | bytes 540704 | tf_op jit(solution)/shard_map/ppermute | solution.py:360
  454.4 1.4 bitcast_dynamic-update-slice_fusion.6
  455.9 2.5 collective-permute-start.7
  458.3 0.0 collective-permute-start.8
  458.3 6.9 %collective-permute-done.7 = s16[528,512]{1,0:T(8,128)(2,1)S(1)} collective-permute-done((s16[528,512]{1,0:T(8,128)(2,1)S(1)}, s16[528,512]{1,0:T(8,128)(2,1)S(1)}, u32[]{:S(2)}, u32[]{:S(2)}) %collective-permute-start.7) | collective-permute-done | bytes 540704 | tf_op jit(solution)/shard_map/ppermute | solution.py:345
  465.2 2.5 collective-permute-start.9
  467.7 0.0 collective-permute-done.8
  467.7 0.0 collective-permute-start.10
  467.7 0.0 copy-done.3
  467.7 0.7 fusion.11
  468.4 4.9 stack.43.slice_ref
  473.3 0.6 pad_add_fusion.flag_ref
  473.9 0.8 bitcast_dynamic-update-slice_fusion.5
  474.8 0.0 collective-permute-done.9
  474.8 2.3 collective-permute-start.11
  477.1 0.0 collective-permute-done.10
  477.1 0.0 collective-permute-start.12
  477.1 0.8 bitcast_dynamic-update-slice_fusion.4
  477.9 0.8 bitcast_dynamic-update-slice_fusion.3
  478.7 0.8 bitcast_dynamic-update-slice_fusion.2
  479.6 4.5 collective-permute-done.11
  484.1 2.4 collective-permute-start.13
  486.5 0.0 collective-permute-done.12
  486.5 0.1 collective-permute-start.14
  486.6 0.8 bitcast_dynamic-update-slice_fusion.1
  487.4 0.8 bitcast_dynamic-update-slice_fusion
  488.2 2.4 collective-permute-done.13
  490.7 2.4 collective-permute-done.14
  493.0 0.9 fusion.8.code_ref.scale_ref
  493.9 0.0 collective-permute-done.16
  493.9 5.3 broadcast_select_fusion.1.upper_ref
  499.2 10.9 %right_factor.1 = (bf16[512,2048]{1,0:T(8,128)(2,1)}, bf16[512,2048]{1,0:T(8,128)(2,1)}) custom-call(s32[2]{0:T(128)} %pad_add_fusion.flag_ref, f32[512,512]{1,0:T(8,128)} %pivot_ref.1, f32[512,2048]{1,0:T(8,128)} %broadcast_select_fusion.1.upper_ref), custom_call_target="tpu_custom_call" | custom-call | tf_op jit(solution)/shard_map/right_factor/pallas_call | solution.py:245
  510.1 37.8 %update_rows.1.base_ref = f32[4096,2048]{1,0:T(8,128)} custom-call(s32[2]{0:T(128)} %pad_add_fusion.flag_ref, s32[8]{0:T(128)} %stack.43.slice_ref, f32[4096,2048]{1,0:T(8,128)} %base_ref.5, s16[8,528,512]{2,1,0:T(8,128)(2,1)} %fusion.8.code_ref.scale_ref, s16[8,528,512]{2,1,0:T(8,128)(2,1)} %fusion.8.code_ref.scale_ref, ...), custom_call_target="tpu_custom_call" | custom-call | tf_op jit(solution)/shard_map/update_rows/pallas_call | solution.py:305
  547.9 39.9 %extend_add.3 = f32[4096,2048]{1,0:T(8,128)} custom-call(s32[256]{0:T(256)} %get-tuple-element.21.key_ref, f32[4096,2048]{1,0:T(8,128)} %update_rows.1.base_ref, bf16[32,1040,128]{2,1,0:T(8,128)(2,1)} %copy-done), custom_call_target="tpu_custom_call", output_to_operand_aliasing={{}: (1, {})} | custom-call | tf_op jit(solution)/shard_map/extend_add/pallas_call | solution.py:146
  (6 shorter events, 0.1 us)
Async XLA Ops:
  325.7 3.3 copy-start
  338.5 48.7 %collective-permute-start.15 = (f32[512,2048]{1,0:T(8,128)}, f32[512,2048]{1,0:T(8,128)}, u32[]{:S(2)}, u32[]{:S(2)}) collective-permute-start(f32[512,2048]{1,0:T(8,128)} %extend_add.2), channel_id=1, source_target_pairs={{0,16},{1,17},{2,18},{3,19},{4,20},{5,21},{6,22},{7,23}} | collective-permute-start | bytes 12582920 | tf_op jit(solution)/shard_map/ppermute | solution.py:369
  343.4 43.7 %copy-start.2 = (f32[512,2048]{1,0:T(8,128)S(1)}, f32[512,2048]{1,0:T(8,128)}, u32[]{:S(2)}) copy-start(f32[512,2048]{1,0:T(8,128)} %extend_add.2) | copy-start | bytes 12582916
  358.0 35.5 %copy-start.1 = (s16[8,528,512]{2,1,0:T(8,128)(2,1)S(1)}, s16[8,528,512]{2,1,0:T(8,128)(2,1)}, u32[]{:S(2)}) copy-start(s16[8,528,512]{2,1,0:T(8,128)(2,1)} %code_panel.1) | copy-start | bytes 12976132
  390.2 103.7 %collective-permute-start.16 = (f32[512,2048]{1,0:T(8,128)}, f32[512,2048]{1,0:T(8,128)}, u32[]{:S(2)}, u32[]{:S(2)}) collective-permute-start(f32[512,2048]{1,0:T(8,128)} %broadcast_select_fusion), channel_id=1, source_target_pairs={{0,8},{16,24},{1,9},{17,25},{2,10},{18,26},{3,11},{19,27},{4,12},{... | collective-permute-start | bytes 12582920 | tf_op jit(solution)/shard_map/ppermute | solution.py:369
  393.7 74.0 %copy-start.3 = (s32[8]{0:T(128)S(1)}, s32[8]{0:T(128)}, u32[]{:S(2)}) copy-start(s32[8]{0:T(128)} %constant.112.clone) | copy-start | bytes 100
  393.7 9.7 %collective-permute-start = (s16[528,512]{1,0:T(8,128)(2,1)S(1)}, s16[528,512]{1,0:T(8,128)(2,1)S(1)}, u32[]{:S(2)}, u32[]{:S(2)}) collective-permute-start(s16[528,512]{1,0:T(8,128)(2,1)S(1)} %get-tuple-element.13), channel_id=1, source_target_pairs={{0,1},{8,9},{16,17},{24,25}} | collective-permute-start | bytes 1622024 | tf_op jit(solution)/shard_map/ppermute | solution.py:360
  396.6 10.3 %collective-permute-start.6 = (s16[528,512]{1,0:T(8,128)(2,1)S(1)}, s16[528,512]{1,0:T(8,128)(2,1)S(1)}, u32[]{:S(2)}, u32[]{:S(2)}) collective-permute-start(s16[528,512]{1,0:T(8,128)(2,1)S(1)} %get-tuple-element.14), channel_id=1, source_target_pairs={{0,7},{8,15},{16,23},{24,31}} | collective-permute-start | bytes 1622024 | tf_op jit(solution)/shard_map/ppermute | solution.py:360
  398.1 18.6 %collective-permute-start.5 = (s16[528,512]{1,0:T(8,128)(2,1)S(1)}, s16[528,512]{1,0:T(8,128)(2,1)S(1)}, u32[]{:S(2)}, u32[]{:S(2)}) collective-permute-start(s16[528,512]{1,0:T(8,128)(2,1)S(1)} %get-tuple-element.15), channel_id=1, source_target_pairs={{0,6},{8,14},{16,22},{24,30}} | collective-permute-start | bytes 1622024 | tf_op jit(solution)/shard_map/ppermute | solution.py:360
  399.5 28.1 %collective-permute-start.4 = (s16[528,512]{1,0:T(8,128)(2,1)S(1)}, s16[528,512]{1,0:T(8,128)(2,1)S(1)}, u32[]{:S(2)}, u32[]{:S(2)}) collective-permute-start(s16[528,512]{1,0:T(8,128)(2,1)S(1)} %get-tuple-element.16), channel_id=1, source_target_pairs={{0,5},{8,13},{16,21},{24,29}} | collective-permute-start | bytes 1622024 | tf_op jit(solution)/shard_map/ppermute | solution.py:360
  403.5 33.2 %collective-permute-start.3 = (s16[528,512]{1,0:T(8,128)(2,1)S(1)}, s16[528,512]{1,0:T(8,128)(2,1)S(1)}, u32[]{:S(2)}, u32[]{:S(2)}) collective-permute-start(s16[528,512]{1,0:T(8,128)(2,1)S(1)} %get-tuple-element.17), channel_id=1, source_target_pairs={{0,4},{8,12},{16,20},{24,28}} | collective-permute-start | bytes 1622024 | tf_op jit(solution)/shard_map/ppermute | solution.py:360
  406.9 38.8 %collective-permute-start.2 = (s16[528,512]{1,0:T(8,128)(2,1)S(1)}, s16[528,512]{1,0:T(8,128)(2,1)S(1)}, u32[]{:S(2)}, u32[]{:S(2)}) collective-permute-start(s16[528,512]{1,0:T(8,128)(2,1)S(1)} %get-tuple-element.18), channel_id=1, source_target_pairs={{0,3},{8,11},{16,19},{24,27}} | collective-permute-start | bytes 1622024 | tf_op jit(solution)/shard_map/ppermute | solution.py:360
  416.8 37.7 %collective-permute-start.1 = (s16[528,512]{1,0:T(8,128)(2,1)S(1)}, s16[528,512]{1,0:T(8,128)(2,1)S(1)}, u32[]{:S(2)}, u32[]{:S(2)}) collective-permute-start(s16[528,512]{1,0:T(8,128)(2,1)S(1)} %get-tuple-element.19), channel_id=1, source_target_pairs={{0,2},{8,10},{16,18},{24,26}} | collective-permute-start | bytes 1622024 | tf_op jit(solution)/shard_map/ppermute | solution.py:360
  455.9 9.4 %collective-permute-start.7 = (s16[528,512]{1,0:T(8,128)(2,1)S(1)}, s16[528,512]{1,0:T(8,128)(2,1)S(1)}, u32[]{:S(2)}, u32[]{:S(2)}) collective-permute-start(s16[528,512]{1,0:T(8,128)(2,1)S(1)} %get-tuple-element.12), channel_id=1, source_target_pairs={{0,2},{2,4},{4,6},{6,7},{7,5},{5,3},{3,1},{1,0},{8,10},{10,12},{12... | collective-permute-start | bytes 1622024 | tf_op jit(solution)/shard_map/ppermute | solution.py:345
  458.3 9.4 %collective-permute-start.8 = (s16[528,512]{1,0:T(8,128)(2,1)S(1)}, s16[528,512]{1,0:T(8,128)(2,1)S(1)}, u32[]{:S(2)}, u32[]{:S(2)}) collective-permute-start(s16[528,512]{1,0:T(8,128)(2,1)S(1)} %get-tuple-element.12), channel_id=1, source_target_pairs={{2,0},{4,2},{6,4},{7,6},{5,7},{3,5},{1,3},{0,1},{10,8},{12,10},{14... | collective-permute-start | bytes 1622024 | tf_op jit(solution)/shard_map/ppermute | solution.py:345
  465.2 9.5 %collective-permute-start.9 = (s16[528,512]{1,0:T(8,128)(2,1)S(1)}, s16[528,512]{1,0:T(8,128)(2,1)S(1)}, u32[]{:S(2)}, u32[]{:S(2)}) collective-permute-start(s16[528,512]{1,0:T(8,128)(2,1)S(1)} %collective-permute-done.7), channel_id=1, source_target_pairs={{0,2},{2,4},{4,6},{6,7},{7,5},{5,3},{3,1},{1,0},{8,10},{10,12},{12... | collective-permute-start | bytes 1622024 | tf_op jit(solution)/shard_map/ppermute | solution.py:345
  467.7 9.4 %collective-permute-start.10 = (s16[528,512]{1,0:T(8,128)(2,1)S(1)}, s16[528,512]{1,0:T(8,128)(2,1)S(1)}, u32[]{:S(2)}, u32[]{:S(2)}) collective-permute-start(s16[528,512]{1,0:T(8,128)(2,1)S(1)} %collective-permute-done.8), channel_id=1, source_target_pairs={{2,0},{4,2},{6,4},{7,6},{5,7},{3,5},{1,3},{0,1},{10,8},{12,10},{14... | collective-permute-start | bytes 1622024 | tf_op jit(solution)/shard_map/ppermute | solution.py:345
  474.8 9.4 %collective-permute-start.11 = (s16[528,512]{1,0:T(8,128)(2,1)S(1)}, s16[528,512]{1,0:T(8,128)(2,1)S(1)}, u32[]{:S(2)}, u32[]{:S(2)}) collective-permute-start(s16[528,512]{1,0:T(8,128)(2,1)S(1)} %collective-permute-done.9), channel_id=1, source_target_pairs={{0,2},{2,4},{4,6},{6,7},{7,5},{5,3},{3,1},{1,0},{8,10},{10,12},{12... | collective-permute-start | bytes 1622024 | tf_op jit(solution)/shard_map/ppermute | solution.py:345
  477.1 9.4 %collective-permute-start.12 = (s16[528,512]{1,0:T(8,128)(2,1)S(1)}, s16[528,512]{1,0:T(8,128)(2,1)S(1)}, u32[]{:S(2)}, u32[]{:S(2)}) collective-permute-start(s16[528,512]{1,0:T(8,128)(2,1)S(1)} %collective-permute-done.10), channel_id=1, source_target_pairs={{2,0},{4,2},{6,4},{7,6},{5,7},{3,5},{1,3},{0,1},{10,8},{12,10},{14... | collective-permute-start | bytes 1622024 | tf_op jit(solution)/shard_map/ppermute | solution.py:345
  484.1 6.5 %collective-permute-start.13 = (s16[264,512]{1,0:T(8,128)(2,1)S(1)}, s16[264,512]{1,0:T(8,128)(2,1)S(1)}, u32[]{:S(2)}, u32[]{:S(2)}) collective-permute-start(s16[264,512]{1,0:T(8,128)(2,1)S(1)} %slice.63), channel_id=1, source_target_pairs={{0,2},{2,4},{4,6},{6,7},{7,5},{5,3},{3,1},{1,0},{8,10},{10,12},{12... | collective-permute-start | bytes 811016 | tf_op jit(solution)/shard_map/ppermute | solution.py:350
  486.5 6.5 %collective-permute-start.14 = (s16[264,512]{1,0:T(8,128)(2,1)S(1)}, s16[264,512]{1,0:T(8,128)(2,1)S(1)}, u32[]{:S(2)}, u32[]{:S(2)}) collective-permute-start(s16[264,512]{1,0:T(8,128)(2,1)S(1)} %slice.64), channel_id=1, source_target_pairs={{2,0},{4,2},{6,4},{7,6},{5,7},{3,5},{1,3},{0,1},{10,8},{12,10},{14... | collective-permute-start | bytes 811016 | tf_op jit(solution)/shard_map/ppermute | solution.py:350

commit v2 on v1

--- a/solution.py
+++ b/solution.py
@@ -74,7 +74,7 @@
         in_specs=[
             pl.BlockSpec(memory_space=pltpu.SMEM),
             pl.BlockSpec(memory_space=pltpu.SMEM),
-            pl.BlockSpec(memory_space=pl.ANY),
+            pl.BlockSpec(memory_space=pltpu.VMEM),
         ],
         out_specs=pl.BlockSpec(memory_space=pl.ANY),
         scratch_shapes=[
@@ -142,7 +142,7 @@
         )
 
 
-def extend(base, arrived, key, width, capacity, rows, columns, alias=False):
+def extend(base, arrived, key, width, capacity, rows, columns):
     return pl.pallas_call(
         functools.partial(extend_kernel, width, capacity),
         out_shape=jax.ShapeDtypeStruct((rows, columns), F32),
@@ -159,8 +159,8 @@
                 pltpu.SMEM((key.shape[0],), I32),
             ],
         ),
-        input_output_aliases={1: 0} if alias else {},
         compiler_params=compiler_params(("arbitrary",)),
+        cost_estimate=pl.CostEstimate(flops=rows * columns, bytes_accessed=12 * rows * columns, transcendentals=0),
         name="extend_add",
     )(key, base, arrived)
 
@@ -320,6 +320,7 @@
             ],
             out_specs=pl.BlockSpec((block, columns), base_map),
         ),
+        input_output_aliases={2: 0},
         compiler_params=compiler_params(("arbitrary",)),
         name="update_rows",
     )(flags, slice_ids, base, codes, codes, high, low)
@@ -392,16 +393,14 @@
     in_pivot = valid & (strip < pivot_tiles)
     panel_key = jnp.where(in_panel, strip * pivot_tiles + tile_column, -1)
     pivot_key = jnp.where(in_pivot, slots, -1)
-    taken = in_panel & (column_index == 0) & ~(in_pivot & (bulk_index == 0))
-    rest_key = jnp.where(valid & ~taken, slots, -1)
 
     codes = code_panel(parent, arrived, panel_key, capacity, column_count)
     upper = extend(parent, arrived, pivot_key, width, capacity, PW, columns)
     upper = tree_broadcast(upper, "bulk")
     high, low = right_factor(flags, pivot_inverse, upper)
     pieces, whose = ring_gather(scatter_first(codes, "col"), "col")
-    result = update_rows(flags, whose, parent, jnp.stack(pieces), high, low)
-    return extend(result, arrived, rest_key, width, capacity, rows, columns, alias=True)
+    extended = extend(parent, arrived, slots, width, capacity, rows, columns)
+    return update_rows(flags, whose, extended, jnp.stack(pieces), high, low)
 
 
 def solution(mesh):

time: 591 us -> 461 us (0.78)
  Pallas kernels: 243 us -> 117 us
    pallas_call x1, Pallas kernels: 131 us -> 6.59 us  [pack(): pl.pallas_call(functools.partial(pack_kernel, devices, capacity), out_sha...]
    ppermute x7, waiting for transfers between devices: 49.6 us -> 40.6 us  [scatter_first(): mine = mine + lax.ppermute(parts[k], axis, [(0, k)])]
  transfers between devices with their start and end apart: 17 -> 17, of which waited for: 12 -> 12; matrix products, arithmetic and copies ran while one was open for 2% -> 2% of each run, Pallas kernels for 2% -> 12%
where the time goes in v2:
time: 461 us; the launch traced here: 457 us
  blocking collectives  195 us (42%)
  Pallas kernels  117 us (25%)
  waiting for transfers between devices  90.6 us (20%)
  starting transfers between devices  29 us (6%)
  other arithmetic  14.4 us (3%)
  local copies, waits for them, and re-layouts  10.9 us (2%)
    all_to_all x1, blocking collectives, per_device(): lax.all_to_all(outgoing, ('bulk', 'col'), split_axis=0, concat_axis=0, ti...  195 us
    pallas_call x2, Pallas kernels, extend(): pl.pallas_call(functools.partial(extend_kernel, width, capacity), out_sha...  48 us
    ppermute x7, waiting for transfers between devices, scatter_first(): mine = mine + lax.ppermute(parts[k], axis, [(0, k)])  40.6 us
    pallas_call x1, Pallas kernels, update_rows(): pl.pallas_call(functools.partial(update_kernel, block, per_slice), out_sh...  37.8 us
    ppermute x2, waiting for transfers between devices, tree_broadcast(): lax.ppermute(block, axis, [(i, i + reach) for i in range(0, count, 2 * re...  29.6 us
    pallas_call x1, Pallas kernels, code_panel(): pl.pallas_call(functools.partial(panel_kernel, width, capacity), out_shap...  14.1 us
    ppermute x3, waiting for transfers between devices, ring_gather(): lax.ppermute(left, axis, ahead)  14 us
    ppermute x7, starting transfers between devices, scatter_first(): mine = mine + lax.ppermute(parts[k], axis, [(0, k)])  11.9 us
  transfers between devices with their start and end apart: 17, of which 12 were waited for; matrix products, arithmetic and copies ran while one was open for 2% of the time, Pallas kernels for 12%

profile of v2, /device:TPU:0, one launch (start us, length us, event | category | flops | bytes accessed | tf_op | source)
XLA Modules:
  0.0 457.5 jit_solution(13346150957976330063)
XLA Ops:
  0.0 6.6 %pack_children.1 = bf16[32,1040,128]{2,1,0:T(8,128)(2,1)} custom-call(s32[128]{0:T(128)} %bitcast.52, s32[128]{0:T(128)} %slot_ref.1, bf16[128,128,128]{2,1,0:T(8,128)(2,1)} %child_ref.1), custom_call_target="tpu_custom_call" | custom-call | tf_op jit(solution)/shard_map/pack_children/pallas_call | solution.py:71
  6.6 195.0 %all_to_all.5.arrived_ref = bf16[32,1040,128]{2,1,0:T(8,128)(2,1)S(1)} all-to-all(bf16[32,1040,128]{2,1,0:T(8,128)(2,1)} %pack_children.1), channel_id=1, replica_groups=mesh['bulk'=4,'col'=8] {'bulk','col'}, dimensions={0} | all-to-all | bytes 17039360 | tf_op jit(solution)/shard_map/all_to_all | solution.py:387
  201.6 0.0 copy-start
  201.6 3.3 copy-done
  204.9 0.1 fusion.9
  205.0 0.1 add.130.key_ref
  205.1 0.0 copy-start.6
  205.1 0.6 and_select_fusion
  205.7 8.5 %extend_add.3 = f32[512,2048]{1,0:T(8,128)} custom-call(s32[256]{0:T(256)} %get-tuple-element.9.key_ref, f32[4096,2048]{1,0:T(8,128)} %base_ref.5, bf16[32,1040,128]{2,1,0:T(8,128)(2,1)} %copy-done), custom_call_target="tpu_custom_call" | custom-call | flops 1048576 | bytes 12582912 | tf_op jit(solution)/shard_map/extend_add/pallas_call | solution.py:146
  214.2 4.5 collective-permute-start.15
  218.8 0.0 copy-done.6
  218.8 0.6 and_select_fusion.2.key_ref
  219.3 0.0 copy-start.4
  219.3 14.1 %code_panel.1 = s16[8,528,512]{2,1,0:T(8,128)(2,1)} custom-call(s32[256]{0:T(256)} %and_select_fusion.2.key_ref, f32[4096,2048]{1,0:T(8,128)} %base_ref.5, bf16[32,1040,128]{2,1,0:T(8,128)(2,1)} %copy-done), custom_call_target="tpu_custom_call" | custom-call | tf_op jit(solution)/shard_map/code_panel/pallas_call | solution.py:206
  233.5 0.0 copy-start.3
  233.5 29.6 %collective-permute-done.15 = f32[512,2048]{1,0:T(8,128)} collective-permute-done((f32[512,2048]{1,0:T(8,128)}, f32[512,2048]{1,0:T(8,128)}, u32[]{:S(2)}, u32[]{:S(2)}) %collective-permute-start.15) | collective-permute-done | bytes 4194336 | tf_op jit(solution)/shard_map/ppermute | solution.py:370
  263.1 0.0 copy-done.4
  263.1 3.0 broadcast_select_fusion
  266.1 3.3 collective-permute-start.16
  269.4 0.0 copy-done.3
  269.4 1.6 slice_bitcast_fusion.6
  270.9 2.9 collective-permute-start
  273.9 1.7 collective-permute-start.6
  275.5 1.3 collective-permute-start.5
  276.9 1.3 collective-permute-start.4
  278.2 2.5 collective-permute-done
  280.7 1.3 collective-permute-start.3
  282.0 1.0 collective-permute-done.6
  283.0 1.3 collective-permute-start.2
  284.3 10.2 %collective-permute-done.5 = s16[528,512]{1,0:T(8,128)(2,1)S(1)} collective-permute-done((s16[528,512]{1,0:T(8,128)(2,1)S(1)}, s16[528,512]{1,0:T(8,128)(2,1)S(1)}, u32[]{:S(2)}, u32[]{:S(2)}) %collective-permute-start.5) | collective-permute-done | bytes 540704 | tf_op jit(solution)/shard_map/ppermute | solution.py:361
  294.5 2.1 collective-permute-start.1
  296.6 7.2 %collective-permute-done.4 = s16[528,512]{1,0:T(8,128)(2,1)S(1)} collective-permute-done((s16[528,512]{1,0:T(8,128)(2,1)}, s16[528,512]{1,0:T(8,128)(2,1)S(1)}, u32[]{:S(2)}, u32[]{:S(2)}) %collective-permute-start.4) | collective-permute-done | bytes 540704 | tf_op jit(solution)/shard_map/ppermute | solution.py:361
  303.8 8.2 %collective-permute-done.3 = s16[528,512]{1,0:T(8,128)(2,1)S(1)} collective-permute-done((s16[528,512]{1,0:T(8,128)(2,1)}, s16[528,512]{1,0:T(8,128)(2,1)S(1)}, u32[]{:S(2)}, u32[]{:S(2)}) %collective-permute-start.3) | collective-permute-done | bytes 540704 | tf_op jit(solution)/shard_map/ppermute | solution.py:361
  312.0 5.8 %collective-permute-done.2 = s16[528,512]{1,0:T(8,128)(2,1)S(1)} collective-permute-done((s16[528,512]{1,0:T(8,128)(2,1)}, s16[528,512]{1,0:T(8,128)(2,1)S(1)}, u32[]{:S(2)}, u32[]{:S(2)}) %collective-permute-start.2) | collective-permute-done | bytes 540704 | tf_op jit(solution)/shard_map/ppermute | solution.py:361
  317.8 5.8 %collective-permute-done.1 = s16[528,512]{1,0:T(8,128)(2,1)} collective-permute-done((s16[528,512]{1,0:T(8,128)(2,1)}, s16[528,512]{1,0:T(8,128)(2,1)}, u32[]{:S(2)}, u32[]{:S(2)}) %collective-permute-start.1) | collective-permute-done | bytes 540704 | tf_op jit(solution)/shard_map/ppermute | solution.py:361
  323.6 2.6 bitcast_dynamic-update-slice_fusion.6
  326.2 2.5 collective-permute-start.7
  328.7 0.0 collective-permute-start.8
  328.7 6.9 %collective-permute-done.7 = s16[528,512]{1,0:T(8,128)(2,1)S(1)} collective-permute-done((s16[528,512]{1,0:T(8,128)(2,1)S(1)}, s16[528,512]{1,0:T(8,128)(2,1)S(1)}, u32[]{:S(2)}, u32[]{:S(2)}) %collective-permute-start.7) | collective-permute-done | bytes 540704 | tf_op jit(solution)/shard_map/ppermute | solution.py:346
  335.6 2.5 collective-permute-start.9
  338.0 0.0 collective-permute-done.8
  338.0 0.0 collective-permute-start.10
  338.1 0.0 copy-done.5
  338.1 0.7 fusion.11
  338.7 5.0 %stack.43.slice_ref = s32[8]{0:T(128)} concatenate(s32[1]{0:T(128)} %bitcast.1, s32[1]{0:T(128)} %get-tuple-element.25, s32[1]{0:T(128)} %get-tuple-element.24, s32[1]{0:T(128)} %get-tuple-element.23, s32[1]{0:T(128)} %get-tuple-element.22, s32[1]{0:T(128)} %get-tuple-element.21, s32[1]{0:T(128)} %get-tuple-element.26, s32[1]{0:T(128)} %get-tuple-element.20), dimensions={0} | concatenate | bytes 64 | tf_op jit(solution)/shard_map/stack | solution.py:354
  343.7 0.7 pad_add_fusion.flag_ref
  344.4 39.4 %extend_add.2.base_ref = f32[4096,2048]{1,0:T(8,128)} custom-call(s32[256]{0:T(256)} %copy-done.6, f32[4096,2048]{1,0:T(8,128)} %base_ref.5, bf16[32,1040,128]{2,1,0:T(8,128)(2,1)} %copy-done), custom_call_target="tpu_custom_call" | custom-call | flops 8388608 | bytes 100663296 | tf_op jit(solution)/shard_map/extend_add/pallas_call | solution.py:146
  383.8 0.0 copy-done.1
  383.8 0.0 collective-permute-done.9
  383.8 2.1 collective-permute-start.11
  385.9 0.0 collective-permute-done.10
  385.9 0.0 collective-permute-start.12
  386.1 7.2 %collective-permute-done.11 = s16[528,512]{1,0:T(8,128)(2,1)S(1)} collective-permute-done((s16[528,512]{1,0:T(8,128)(2,1)S(1)}, s16[528,512]{1,0:T(8,128)(2,1)S(1)}, u32[]{:S(2)}, u32[]{:S(2)}) %collective-permute-start.11) | collective-permute-done | bytes 540704 | tf_op jit(solution)/shard_map/ppermute | solution.py:346
  393.3 2.1 collective-permute-start.13
  395.4 0.0 collective-permute-done.12
  395.4 0.1 collective-permute-start.14
  395.6 4.2 collective-permute-done.13
  399.8 2.1 collective-permute-done.14
  402.0 0.0 copy-start.2
  402.0 0.0 collective-permute-done.16
  402.0 6.8 %broadcast_select_fusion.1.upper_ref = f32[512,2048]{1,0:T(8,128)} fusion(f32[512,2048]{1,0:T(8,128)} %collective-permute-done.16, f32[512,2048]{1,0:T(8,128)} %broadcast_select_fusion, pred[]{:T(512)S(6)} %eq.51), kind=kLoop, calls=%fused_computation.1 | loop fusion | flops 1048576 | bytes 12582913 | tf_op jit(solution)/shard_map/jit(_where)/select_n | solution.py:371
  408.7 0.0 copy-done.2
  408.7 10.9 %right_factor.1 = (bf16[512,2048]{1,0:T(8,128)(2,1)}, bf16[512,2048]{1,0:T(8,128)(2,1)}) custom-call(s32[2]{0:T(128)} %pad_add_fusion.flag_ref, f32[512,512]{1,0:T(8,128)} %pivot_ref.1, f32[512,2048]{1,0:T(8,128)} %broadcast_select_fusion.1.upper_ref), custom_call_target="tpu_custom_call" | custom-call | tf_op jit(solution)/shard_map/right_factor/pallas_call | solution.py:245
  419.7 37.8 %update_rows.1 = f32[4096,2048]{1,0:T(8,128)} custom-call(s32[2]{0:T(128)} %pad_add_fusion.flag_ref, s32[8]{0:T(128)} %stack.43.slice_ref, f32[4096,2048]{1,0:T(8,128)} %extend_add.2.base_ref, s16[8,528,512]{2,1,0:T(8,128)(2,1)} %copy-done.2, s16[8,528,512]{2,1,0:T(8,128)(2,1)} %copy-done.2, ...), custom_call_target="tpu_custom_call", output_to_operand_aliasing={{}: (2, {})} | custom-call | tf_op jit(solution)/shard_map/update_rows/pallas_call | solution.py:305
  (12 shorter events, 0.3 us)
Async XLA Ops:
  201.6 3.3 copy-start
  205.1 13.7 %copy-start.6 = (s32[256]{0:T(256)}, s32[256]{0:T(256)S(1)}, u32[]{:S(2)}) copy-start(s32[256]{0:T(256)S(1)} %add.130.key_ref) | copy-start | bytes 3076
  214.2 48.9 %collective-permute-start.15 = (f32[512,2048]{1,0:T(8,128)}, f32[512,2048]{1,0:T(8,128)}, u32[]{:S(2)}, u32[]{:S(2)}) collective-permute-start(f32[512,2048]{1,0:T(8,128)} %extend_add.3), channel_id=1, source_target_pairs={{0,16},{1,17},{2,18},{3,19},{4,20},{5,21},{6,22},{7,23}} | collective-permute-start | bytes 12582920 | tf_op jit(solution)/shard_map/ppermute | solution.py:370
  219.3 43.7 %copy-start.4 = (f32[512,2048]{1,0:T(8,128)S(1)}, f32[512,2048]{1,0:T(8,128)}, u32[]{:S(2)}) copy-start(f32[512,2048]{1,0:T(8,128)} %extend_add.3) | copy-start | bytes 12582916
  233.5 35.9 %copy-start.3 = (s16[8,528,512]{2,1,0:T(8,128)(2,1)S(1)}, s16[8,528,512]{2,1,0:T(8,128)(2,1)}, u32[]{:S(2)}) copy-start(s16[8,528,512]{2,1,0:T(8,128)(2,1)} %code_panel.1) | copy-start | bytes 12976132
  266.1 135.9 %collective-permute-start.16 = (f32[512,2048]{1,0:T(8,128)}, f32[512,2048]{1,0:T(8,128)}, u32[]{:S(2)}, u32[]{:S(2)}) collective-permute-start(f32[512,2048]{1,0:T(8,128)} %broadcast_select_fusion), channel_id=1, source_target_pairs={{0,8},{16,24},{1,9},{17,25},{2,10},{18,26},{3,11},{19,27},{4,12},{... | collective-permute-start | bytes 12582920 | tf_op jit(solution)/shard_map/ppermute | solution.py:370
  270.9 67.1 %copy-start.5 = (s32[8]{0:T(128)S(1)}, s32[8]{0:T(128)}, u32[]{:S(2)}) copy-start(s32[8]{0:T(128)} %constant.112.clone) | copy-start | bytes 100
  270.9 9.7 %collective-permute-start = (s16[528,512]{1,0:T(8,128)(2,1)S(1)}, s16[528,512]{1,0:T(8,128)(2,1)S(1)}, u32[]{:S(2)}, u32[]{:S(2)}) collective-permute-start(s16[528,512]{1,0:T(8,128)(2,1)S(1)} %get-tuple-element.13), channel_id=1, source_target_pairs={{0,1},{8,9},{16,17},{24,25}} | collective-permute-start | bytes 1622024 | tf_op jit(solution)/shard_map/ppermute | solution.py:361
  273.9 9.1 %collective-permute-start.6 = (s16[528,512]{1,0:T(8,128)(2,1)S(1)}, s16[528,512]{1,0:T(8,128)(2,1)S(1)}, u32[]{:S(2)}, u32[]{:S(2)}) collective-permute-start(s16[528,512]{1,0:T(8,128)(2,1)S(1)} %get-tuple-element.14), channel_id=1, source_target_pairs={{0,7},{8,15},{16,23},{24,31}} | collective-permute-start | bytes 1622024 | tf_op jit(solution)/shard_map/ppermute | solution.py:361
  275.5 18.9 %collective-permute-start.5 = (s16[528,512]{1,0:T(8,128)(2,1)S(1)}, s16[528,512]{1,0:T(8,128)(2,1)S(1)}, u32[]{:S(2)}, u32[]{:S(2)}) collective-permute-start(s16[528,512]{1,0:T(8,128)(2,1)S(1)} %get-tuple-element.15), channel_id=1, source_target_pairs={{0,6},{8,14},{16,22},{24,30}} | collective-permute-start | bytes 1622024 | tf_op jit(solution)/shard_map/ppermute | solution.py:361
  276.9 26.9 %collective-permute-start.4 = (s16[528,512]{1,0:T(8,128)(2,1)}, s16[528,512]{1,0:T(8,128)(2,1)S(1)}, u32[]{:S(2)}, u32[]{:S(2)}) collective-permute-start(s16[528,512]{1,0:T(8,128)(2,1)} %get-tuple-element.16), channel_id=1, source_target_pairs={{0,5},{8,13},{16,21},{24,29}} | collective-permute-start | bytes 1622024 | tf_op jit(solution)/shard_map/ppermute | solution.py:361
  280.7 31.3 %collective-permute-start.3 = (s16[528,512]{1,0:T(8,128)(2,1)}, s16[528,512]{1,0:T(8,128)(2,1)S(1)}, u32[]{:S(2)}, u32[]{:S(2)}) collective-permute-start(s16[528,512]{1,0:T(8,128)(2,1)} %get-tuple-element.17), channel_id=1, source_target_pairs={{0,4},{8,12},{16,20},{24,28}} | collective-permute-start | bytes 1622024 | tf_op jit(solution)/shard_map/ppermute | solution.py:361
  283.0 34.8 %collective-permute-start.2 = (s16[528,512]{1,0:T(8,128)(2,1)}, s16[528,512]{1,0:T(8,128)(2,1)S(1)}, u32[]{:S(2)}, u32[]{:S(2)}) collective-permute-start(s16[528,512]{1,0:T(8,128)(2,1)} %get-tuple-element.18), channel_id=1, source_target_pairs={{0,3},{8,11},{16,19},{24,27}} | collective-permute-start | bytes 1622024 | tf_op jit(solution)/shard_map/ppermute | solution.py:361
  294.5 29.1 %collective-permute-start.1 = (s16[528,512]{1,0:T(8,128)(2,1)}, s16[528,512]{1,0:T(8,128)(2,1)}, u32[]{:S(2)}, u32[]{:S(2)}) collective-permute-start(s16[528,512]{1,0:T(8,128)(2,1)} %get-tuple-element.19), channel_id=1, source_target_pairs={{0,2},{8,10},{16,18},{24,26}} | collective-permute-start | bytes 1622024 | tf_op jit(solution)/shard_map/ppermute | solution.py:361
  326.2 9.4 %collective-permute-start.7 = (s16[528,512]{1,0:T(8,128)(2,1)S(1)}, s16[528,512]{1,0:T(8,128)(2,1)S(1)}, u32[]{:S(2)}, u32[]{:S(2)}) collective-permute-start(s16[528,512]{1,0:T(8,128)(2,1)S(1)} %get-tuple-element.12), channel_id=1, source_target_pairs={{0,2},{2,4},{4,6},{6,7},{7,5},{5,3},{3,1},{1,0},{8,10},{10,12},{12... | collective-permute-start | bytes 1622024 | tf_op jit(solution)/shard_map/ppermute | solution.py:346
  328.7 9.4 %collective-permute-start.8 = (s16[528,512]{1,0:T(8,128)(2,1)S(1)}, s16[528,512]{1,0:T(8,128)(2,1)S(1)}, u32[]{:S(2)}, u32[]{:S(2)}) collective-permute-start(s16[528,512]{1,0:T(8,128)(2,1)S(1)} %get-tuple-element.12), channel_id=1, source_target_pairs={{2,0},{4,2},{6,4},{7,6},{5,7},{3,5},{1,3},{0,1},{10,8},{12,10},{14... | collective-permute-start | bytes 1622024 | tf_op jit(solution)/shard_map/ppermute | solution.py:346
  335.6 48.3 %collective-permute-start.9 = (s16[528,512]{1,0:T(8,128)(2,1)S(1)}, s16[528,512]{1,0:T(8,128)(2,1)S(1)}, u32[]{:S(2)}, u32[]{:S(2)}) collective-permute-start(s16[528,512]{1,0:T(8,128)(2,1)S(1)} %collective-permute-done.7), channel_id=1, source_target_pairs={{0,2},{2,4},{4,6},{6,7},{7,5},{5,3},{3,1},{1,0},{8,10},{10,12},{12... | collective-permute-start | bytes 1622024 | tf_op jit(solution)/shard_map/ppermute | solution.py:346
  338.0 47.9 %collective-permute-start.10 = (s16[528,512]{1,0:T(8,128)(2,1)S(1)}, s16[528,512]{1,0:T(8,128)(2,1)S(1)}, u32[]{:S(2)}, u32[]{:S(2)}) collective-permute-start(s16[528,512]{1,0:T(8,128)(2,1)S(1)} %collective-permute-done.8), channel_id=1, source_target_pairs={{2,0},{4,2},{6,4},{7,6},{5,7},{3,5},{1,3},{0,1},{10,8},{12,10},{14... | collective-permute-start | bytes 1622024 | tf_op jit(solution)/shard_map/ppermute | solution.py:346
  344.4 39.4 %copy-start.1 = (s16[8,528,512]{2,1,0:T(8,128)(2,1)S(1)}, s16[8,528,512]{2,1,0:T(8,128)(2,1)}, u32[]{:S(2)}) copy-start(s16[8,528,512]{2,1,0:T(8,128)(2,1)} %get-tuple-element.11) | copy-start | bytes 12976132
  383.8 9.4 %collective-permute-start.11 = (s16[528,512]{1,0:T(8,128)(2,1)S(1)}, s16[528,512]{1,0:T(8,128)(2,1)S(1)}, u32[]{:S(2)}, u32[]{:S(2)}) collective-permute-start(s16[528,512]{1,0:T(8,128)(2,1)S(1)} %collective-permute-done.9), channel_id=1, source_target_pairs={{0,2},{2,4},{4,6},{6,7},{7,5},{5,3},{3,1},{1,0},{8,10},{10,12},{12... | collective-permute-start | bytes 1622024 | tf_op jit(solution)/shard_map/ppermute | solution.py:346
  385.9 9.4 %collective-permute-start.12 = (s16[528,512]{1,0:T(8,128)(2,1)S(1)}, s16[528,512]{1,0:T(8,128)(2,1)S(1)}, u32[]{:S(2)}, u32[]{:S(2)}) collective-permute-start(s16[528,512]{1,0:T(8,128)(2,1)S(1)} %collective-permute-done.10), channel_id=1, source_target_pairs={{2,0},{4,2},{6,4},{7,6},{5,7},{3,5},{1,3},{0,1},{10,8},{12,10},{14... | collective-permute-start | bytes 1622024 | tf_op jit(solution)/shard_map/ppermute | solution.py:346
  393.3 6.5 %collective-permute-start.13 = (s16[264,512]{1,0:T(8,128)(2,1)S(1)}, s16[264,512]{1,0:T(8,128)(2,1)S(1)}, u32[]{:S(2)}, u32[]{:S(2)}) collective-permute-start(s16[264,512]{1,0:T(8,128)(2,1)S(1)} %slice.63), channel_id=1, source_target_pairs={{0,2},{2,4},{4,6},{6,7},{7,5},{5,3},{3,1},{1,0},{8,10},{10,12},{12... | collective-permute-start | bytes 811016 | tf_op jit(solution)/shard_map/ppermute | solution.py:351
  395.4 6.5 %collective-permute-start.14 = (s16[264,512]{1,0:T(8,128)(2,1)S(1)}, s16[264,512]{1,0:T(8,128)(2,1)S(1)}, u32[]{:S(2)}, u32[]{:S(2)}) collective-permute-start(s16[264,512]{1,0:T(8,128)(2,1)S(1)} %slice.64), channel_id=1, source_target_pairs={{2,0},{4,2},{6,4},{7,6},{5,7},{3,5},{1,3},{0,1},{10,8},{12,10},{14... | collective-permute-start | bytes 811016 | tf_op jit(solution)/shard_map/ppermute | solution.py:351
  402.0 6.8 %copy-start.2 = (s16[8,528,512]{2,1,0:T(8,128)(2,1)}, s16[8,528,512]{2,1,0:T(8,128)(2,1)S(1)}, u32[]{:S(2)}) copy-start(s16[8,528,512]{2,1,0:T(8,128)(2,1)S(1)} %fusion.8.code_ref.scale_ref) | copy-start | bytes 12976132

commit v3 on v2

--- a/solution.py
+++ b/solution.py
@@ -12,6 +12,8 @@
 META = 16
 CODE_TOP = 32600.0
 VMEM_LIMIT = 56 * 1024 * 1024
+
+SHORT = pl.CostEstimate(flops=0, bytes_accessed=4096, transcendentals=0)
 
 F32 = jnp.float32
 BF16 = jnp.bfloat16
@@ -87,6 +89,253 @@
         compiler_params=compiler_params(),
         name="pack_children",
     )(owner, slot, child)
+
+
+def lanes(values, count, fallback=-1):
+    lane = lax.broadcasted_iota(I32, (META, TILE), 1)
+    out = jnp.full((META, TILE), fallback, I32)
+    for k in range(count):
+        out = jnp.where(lane == k, values(k), out)
+    return out
+
+
+def coded_lines(code, third):
+    row = lax.broadcasted_iota(I32, (META, TILE), 0)
+    lines = jnp.where(row == 0, code >> 4, jnp.where(row == 1, code & 15, third))
+    return lines.astype(F32).astype(BF16)
+
+
+def fill(ref, count, value):
+    def step(i, _):
+        ref[i] = value
+        return 0
+
+    lax.fori_loop(0, count, step, 0, unroll=8 if count % 8 == 0 else 1)
+
+
+def sort_kernel(
+    plan, kind_ref, dest_ref, code_ref, child_ref,
+    early_ref, near_ref, far_ref, over_ref,
+    filled, early_code, list_code, list_dest, early_meta, list_meta, sem, meta_sem,
+):
+    devices, share, size, half = plan["devices"], plan["early"], plan["listed"], plan["half"]
+    columns = plan["columns"]
+    lists = (near_ref, far_ref)
+    fill(filled, devices + 2, 0)
+    fill(early_code, devices * share, -1)
+    fill(list_code, 2 * size, -1)
+    fill(list_dest, 2 * size, -1)
+    over_ref[0] = 0
+
+    def send_early(i, dest, k):
+        early_code[dest * share + k] = code_ref[i]
+        rows = pl.ds(pl.multiple_of(k * TILE, TILE), TILE)
+        pltpu.make_async_copy(child_ref.at[i], early_ref.at[dest, rows], sem).start()
+
+    def place_special(i, _):
+        @pl.when(kind_ref[i] == 2)
+        def _():
+            dest = dest_ref[i]
+            k = filled[dest]
+            filled[dest] = k + 1
+
+            @pl.when(k >= share)
+            def _():
+                over_ref[0] = 1
+
+            send_early(i, dest, jnp.minimum(k, share - 1))
+
+        return 0
+
+    def place_plain(i, _):
+        kind, dest = kind_ref[i], dest_ref[i]
+
+        @pl.when(kind < 2)
+        def _():
+            k = filled[dest]
+            filled[dest] = k + 1
+
+            @pl.when(k < share)
+            def _():
+                send_early(i, dest, k)
+
+            @pl.when(k >= share)
+            def _():
+                spot = filled[devices + kind]
+                filled[devices + kind] = spot + 1
+
+                @pl.when(spot >= size)
+                def _():
+                    over_ref[0] = 1
+
+                spot = jnp.minimum(spot, size - 1)
+                list_code[kind * size + spot] = code_ref[i]
+                list_dest[kind * size + spot] = (dest // columns) * half + lax.rem(dest, half)
+                rows = pl.ds(pl.multiple_of(spot * TILE, TILE), TILE)
+                for which in range(2):
+
+                    @pl.when(kind == which)
+                    def _(which=which):
+                        pltpu.make_async_copy(child_ref.at[i], lists[which].at[rows], sem).start()
+
+        return 0
+
+    lax.fori_loop(0, kind_ref.shape[0], place_special, 0)
+    lax.fori_loop(0, kind_ref.shape[0], place_plain, 0)
+    copies = []
+    for which in range(2):
+        code = lanes(lambda k: list_code[which * size + k], size)
+        dest = lanes(lambda k: list_dest[which * size + k], size)
+        list_meta[which] = coded_lines(code, dest)
+        copies.append(
+            pltpu.make_async_copy(
+                list_meta.at[which], lists[which].at[pl.ds(size * TILE, META)], meta_sem.at[which]
+            )
+        )
+        copies[-1].start()
+
+    def write_meta(d, _):
+        early_meta[d] = coded_lines(lanes(lambda k: early_code[d * share + k], share), 0)
+        return 0
+
+    lax.fori_loop(0, devices, write_meta, 0)
+    copies.append(
+        pltpu.make_async_copy(early_meta, early_ref.at[:, pl.ds(share * TILE, META)], meta_sem.at[2])
+    )
+    copies[-1].start()
+    pltpu.make_async_copy(child_ref, child_ref, sem).wait()
+    for copy in copies:
+        copy.wait()
+
+
+def sort_children(plan, owner, slot, flags, child):
+    devices, share, listed = plan["devices"], plan["early"], plan["listed"]
+    bulk, col = owner // plan["columns"], owner % plan["columns"]
+    strip, tile = slot // plan["width"], slot % plan["width"]
+    pivot = (bulk == 0) & (strip < plan["pivot"])
+    panel = (col == 0) & (tile < plan["pivot"])
+    pivot, panel = pivot & ~panel, panel & ~pivot
+    bulk = jnp.where(pivot, strip // plan["pivot_strips"], bulk)
+    col = jnp.where(panel, strip // plan["panel_strips"], col)
+    code = jnp.where(panel, plan["panel_code"] + (strip % plan["panel_strips"]) * plan["pivot"] + tile, slot)
+    code = jnp.where(pivot, plan["pivot_code"] + (strip % plan["pivot_strips"]) * plan["width"] + tile, code)
+    here = col // plan["half"] == flags[1] // plan["half"]
+    kind = jnp.where(pivot | panel, 2, jnp.where(here, 0, 1))
+    dest = bulk * plan["columns"] + col
+    anywhere = pl.BlockSpec(memory_space=pl.ANY)
+    scalars = pl.BlockSpec(memory_space=pltpu.SMEM)
+    in_list = jax.ShapeDtypeStruct((listed * TILE + META, TILE), BF16)
+    return pl.pallas_call(
+        functools.partial(sort_kernel, plan),
+        out_shape=[
+            jax.ShapeDtypeStruct((devices, share * TILE + META, TILE), BF16),
+            in_list,
+            in_list,
+            jax.ShapeDtypeStruct((1,), I32),
+        ],
+        in_specs=[scalars, scalars, scalars, pl.BlockSpec(memory_space=pltpu.VMEM)],
+        out_specs=[anywhere, anywhere, anywhere, scalars],
+        scratch_shapes=[
+            pltpu.SMEM((devices + 2,), I32),
+            pltpu.SMEM((devices * share,), I32),
+            pltpu.SMEM((2 * listed,), I32),
+            pltpu.SMEM((2 * listed,), I32),
+            pltpu.VMEM((devices, META, TILE), BF16),
+            pltpu.VMEM((2, META, TILE), BF16),
+            pltpu.SemaphoreType.DMA,
+            pltpu.SemaphoreType.DMA((3,)),
+        ],
+        compiler_params=compiler_params(),
+        cost_estimate=SHORT,
+        name="sort_children",
+    )(kind, dest, code, child)
+
+
+def read_list(listed):
+    count = (listed.shape[0] - META) // TILE
+    lines = listed[count * TILE : count * TILE + 3, :count].astype(I32)
+    return lines[0] * 16 + lines[1], lines[2]
+
+
+def distribute_kernel(groups, capacity, sizes, *refs):
+    n = len(sizes)
+    code_refs, dest_refs, block_refs = refs[:n], refs[n : 2 * n], refs[2 * n : 3 * n]
+    over_in, out_ref, over_ref, filled, codes, meta, spare, sem, meta_sem = refs[3 * n :]
+    fill(filled, groups, 0)
+    fill(codes, groups * capacity, -1)
+    over_ref[0] = over_in[0]
+    for code_ref, dest_ref, block_ref, size in zip(code_refs, dest_refs, block_refs, sizes):
+
+        def place(i, _, code_ref=code_ref, dest_ref=dest_ref, block_ref=block_ref):
+            dest = dest_ref[i]
+            block = block_ref.at[pl.ds(pl.multiple_of(i * TILE, TILE), TILE)]
+
+            @pl.when(dest >= 0)
+            def _():
+                k = filled[dest]
+                filled[dest] = k + 1
+
+                @pl.when(k >= capacity)
+                def _():
+                    over_ref[0] = 1
+
+                k = jnp.minimum(k, capacity - 1)
+                codes[dest * capacity + k] = code_ref[i]
+                pltpu.make_async_copy(
+                    block, out_ref.at[dest, pl.ds(pl.multiple_of(k * TILE, TILE), TILE)], sem
+                ).start()
+
+            @pl.when(dest < 0)
+            def _():
+                pltpu.make_async_copy(block, spare, sem).start()
+
+            return 0
+
+        lax.fori_loop(0, size, place, 0)
+
+    def write_meta(g, _):
+        meta[g] = coded_lines(lanes(lambda k: codes[g * capacity + k], capacity), over_ref[0])
+        return 0
+
+    lax.fori_loop(0, groups, write_meta, 0)
+    copy = pltpu.make_async_copy(meta, out_ref.at[:, pl.ds(capacity * TILE, META)], meta_sem)
+    copy.start()
+    for block_ref, size in zip(block_refs, sizes):
+        blocks = block_ref.at[pl.ds(0, size * TILE)]
+        pltpu.make_async_copy(blocks, blocks, sem).wait()
+    copy.wait()
+
+
+def distribute(lists, over, groups, capacity):
+    sizes = [(x.shape[0] - META) // TILE for x in lists]
+    codes, dests = zip(*[read_list(x) for x in lists])
+    n = len(lists)
+    return pl.pallas_call(
+        functools.partial(distribute_kernel, groups, capacity, sizes),
+        out_shape=[
+            jax.ShapeDtypeStruct((groups, capacity * TILE + META, TILE), BF16),
+            jax.ShapeDtypeStruct((1,), I32),
+        ],
+        in_specs=[pl.BlockSpec(memory_space=pltpu.SMEM)] * (2 * n)
+        + [pl.BlockSpec(memory_space=pltpu.VMEM)] * n
+        + [pl.BlockSpec(memory_space=pltpu.SMEM)],
+        out_specs=[pl.BlockSpec(memory_space=pl.ANY), pl.BlockSpec(memory_space=pltpu.SMEM)],
+        scratch_shapes=[
+            pltpu.SMEM((groups,), I32),
+            pltpu.SMEM((groups * capacity,), I32),
+            pltpu.VMEM((groups, META, TILE), BF16),
+            pltpu.VMEM((TILE, TILE), BF16),
+            pltpu.SemaphoreType.DMA,
+            pltpu.SemaphoreType.DMA,
+        ],
+        compiler_params=compiler_params(),
+        cost_estimate=SHORT,
+        name="distribute",
+    )(*codes, *dests, *lists, over)[0]
+
+
+def read_over(arrived, capacity):
+    return jnp.max(arrived[:, capacity * TILE + 2, 0].astype(I32))
 
 
 def read_slots(arrived, capacity):
@@ -165,6 +414,109 @@
     )(key, base, arrived)
 
 
+AHEAD = 8
+BUFFERS = 16
+
+
+def touch_kernel(
+    width, capacity, key_ref, base_ref, arrived_ref, out_ref,
+    tiles, head, following, active, read_sem, write_sem,
+):
+    del base_ref
+    fill(head, head.shape[0], -1)
+
+    def chain(i, count):
+        key = key_ref[i]
+        at = jnp.maximum(key, 0)
+        first = jnp.logical_and(key >= 0, head[at] < 0)
+
+        @pl.when(key >= 0)
+        def _():
+            following[i] = head[at]
+            head[at] = i
+
+        @pl.when(first)
+        def _():
+            active[count] = key
+
+        return count + first.astype(I32)
+
+    count = lax.fori_loop(0, key_ref.shape[0], chain, jnp.int32(0))
+
+    def copy(j, out):
+        key = active[j]
+        slot = lax.rem(j, BUFFERS)
+        place = out_ref.at[
+            pl.ds(pl.multiple_of((key // width) * TILE, TILE), TILE),
+            pl.ds(pl.multiple_of((key % width) * TILE, TILE), TILE),
+        ]
+        if out:
+            return pltpu.make_async_copy(tiles.at[slot], place, write_sem.at[slot])
+        return pltpu.make_async_copy(place, tiles.at[slot], read_sem.at[slot])
+
+    def first_reads(j, _):
+        copy(j, False).start()
+        return 0
+
+    lax.fori_loop(0, jnp.minimum(count, AHEAD), first_reads, 0)
+
+    def step(j, _):
+        later = j + AHEAD
+
+        @pl.when(later < count)
+        def _():
+            @pl.when(later >= BUFFERS)
+            def _():
+                copy(later - BUFFERS, True).wait()
+
+            copy(later, False).start()
+
+        copy(j, False).wait()
+        slot = lax.rem(j, BUFFERS)
+
+        def body(i):
+            start = pl.multiple_of((i % capacity) * TILE, TILE)
+            tiles[slot] = tiles[slot] + arrived_ref[i // capacity, pl.ds(start, TILE), :].astype(F32)
+            return following[i]
+
+        lax.while_loop(lambda i: i >= 0, body, head[active[j]])
+        copy(j, True).start()
+        return 0
+
+    lax.fori_loop(0, count, step, 0)
+
+    def last_writes(j, _):
+        copy(j, True).wait()
+        return 0
+
+    lax.fori_loop(jnp.maximum(count - BUFFERS, 0), count, last_writes, 0)
+
+
+def touch_tiles(base, arrived, key, width, capacity):
+    rows, columns = base.shape
+    return pl.pallas_call(
+        functools.partial(touch_kernel, width, capacity),
+        out_shape=jax.ShapeDtypeStruct((rows, columns), F32),
+        in_specs=[
+            pl.BlockSpec(memory_space=pltpu.SMEM),
+            pl.BlockSpec(memory_space=pl.ANY),
+            pl.BlockSpec(memory_space=pltpu.VMEM),
+        ],
+        out_specs=pl.BlockSpec(memory_space=pl.ANY),
+        scratch_shapes=[
+            pltpu.VMEM((BUFFERS, TILE, TILE), F32),
+            pltpu.SMEM((rows * columns // (TILE * TILE),), I32),
+            pltpu.SMEM((key.shape[0],), I32),
+            pltpu.SMEM((key.shape[0],), I32),
+            pltpu.SemaphoreType.DMA((BUFFERS,)),
+            pltpu.SemaphoreType.DMA((BUFFERS,)),
+        ],
+        input_output_aliases={1: 0},
+        compiler_params=compiler_params(),
+        name="touch_tiles",
+    )(key, base, arrived)
+
+
 def code_rows(values):
     top = jnp.maximum(jnp.max(jnp.abs(values), axis=1, keepdims=True), 1e-30)
     exponent = jnp.ceil(jnp.log2(top) * 64.0)
@@ -176,6 +528,77 @@
     return lax.broadcasted_iota(I32, (n, n), 0) == lax.broadcasted_iota(I32, (n, n), 1)
 
 
+def write_code(out_ref, lead, values, rows, s):
+    code, exponent = code_rows(values)
+    out_ref[(*lead, pl.ds(s * TILE, TILE), slice(None))] = code.astype(jnp.int16)
+    line = jnp.sum(jnp.where(diagonal(TILE), exponent, 0.0), axis=0, keepdims=True)
+    out_ref[(*lead, pl.ds(rows, META), pl.ds(s * TILE, TILE))] = (
+        jnp.broadcast_to(line, (META, TILE)).astype(I32).astype(jnp.int16)
+    )
+
+
+def row_scale(lines):
+    line = lines.astype(I32).astype(F32)[:1]
+    exponent = jnp.sum(jnp.where(diagonal(TILE), line, 0.0), axis=1, keepdims=True)
+    return jnp.exp2(exponent * (1.0 / 64.0)) * (1.0 / CODE_TOP)
+
+
+def encode_kernel(base_ref, out_ref):
+    rows = base_ref.shape[0]
+    out_ref[0, pl.ds(rows, META), :] = jnp.zeros((META, out_ref.shape[2]), jnp.int16)
+    for s in range(rows // TILE):
+        write_code(out_ref, (0,), base_ref[pl.ds(s * TILE, TILE), :], rows, s)
+
+
+def encode_panel(base, slices):
+    rows = base.shape[0] // slices
+    return pl.pallas_call(
+        encode_kernel,
+        out_shape=jax.ShapeDtypeStruct((slices, rows + META, PW), jnp.int16),
+        grid=(slices,),
+        in_specs=[pl.BlockSpec((rows, PW), lambda i: (i, 0))],
+        out_specs=pl.BlockSpec((1, rows + META, PW), lambda i: (i, 0, 0)),
+        compiler_params=compiler_params(("arbitrary",)),
+        cost_estimate=SHORT,
+        name="encode_panel",
+    )(base)
+
+
+def slice_kernel(width, capacity, key_ref, code_ref, arrived_ref, out_ref, work, head, following):
+    build_lists(key_ref, head, following, width)
+    rows = work.shape[0]
+    out_ref[pl.ds(rows, META), :] = jnp.zeros((META, out_ref.shape[1]), jnp.int16)
+    for s in range(rows // TILE):
+        spot = pl.ds(s * TILE, TILE)
+        work[spot, :] = code_ref[spot, :].astype(I32).astype(F32) * row_scale(
+            code_ref[pl.ds(rows, META), spot]
+        )
+        add_strip(key_ref, arrived_ref, work, head, following, s, width, capacity, s * TILE)
+        write_code(out_ref, (), work[spot, :], rows, s)
+
+
+def extend_slice(code, arrived, key, capacity):
+    rows = code.shape[0] - META
+    return pl.pallas_call(
+        functools.partial(slice_kernel, PW // TILE, capacity),
+        out_shape=jax.ShapeDtypeStruct(code.shape, jnp.int16),
+        in_specs=[
+            pl.BlockSpec(memory_space=pltpu.SMEM),
+            pl.BlockSpec(memory_space=pltpu.VMEM),
+            pl.BlockSpec(memory_space=pltpu.VMEM),
+        ],
+        out_specs=pl.BlockSpec(memory_space=pltpu.VMEM),
+        scratch_shapes=[
+            pltpu.VMEM((rows, PW), F32),
+            pltpu.SMEM((rows // TILE,), I32),
+            pltpu.SMEM((key.shape[0],), I32),
+        ],
+        compiler_params=compiler_params(),
+        cost_estimate=SHORT,
+        name="extend_slice",
+    )(key, code, arrived)
+
+
 def panel_kernel(width, capacity, key_ref, base_ref, arrived_ref, out_ref, work, head, following):
     step = pl.program_id(0)
 
@@ -186,18 +609,12 @@
     work[...] = base_ref[...]
     rows = base_ref.shape[0]
     strips = rows // TILE
-    eye = diagonal(TILE)
     out_ref[0, pl.ds(rows, META), :] = jnp.zeros((META, out_ref.shape[2]), jnp.int16)
     for s in range(strips):
         add_strip(
             key_ref, arrived_ref, work, head, following, step * strips + s, width, capacity, s * TILE
         )
-        code, exponent = code_rows(work[pl.ds(s * TILE, TILE), :])
-        out_ref[0, pl.ds(s * TILE, TILE), :] = code.astype(jnp.int16)
-        line = jnp.sum(jnp.where(eye, exponent, 0.0), axis=0, keepdims=True)
-        out_ref[0, pl.ds(rows, META), pl.ds(s * TILE, TILE)] = (
-            jnp.broadcast_to(line, (META, TILE)).astype(I32).astype(jnp.int16)
-        )
+        write_code(out_ref, (0,), work[pl.ds(s * TILE, TILE), :], rows, s)
 
 
 def code_panel(base, arrived, key, capacity, slices):
@@ -225,45 +642,64 @@
     )(key, base, arrived)
 
 
-def right_kernel(flag_ref, pivot_ref, upper_ref, high_ref, low_ref):
+def split(x):
+    high = x.astype(BF16)
+    return high, (x - high.astype(F32)).astype(BF16)
+
+
+def right_kernel(flag_ref, id_ref, pivot_ref, *refs):
+    pieces, (high_ref, low_ref, upper_ref) = refs[:-3], refs[-3:]
     step = pl.program_id(0)
-    columns = upper_ref.shape[1]
+    height, columns = pieces[0].shape
+    for p, piece in enumerate(pieces):
+        upper_ref[pl.ds(pl.multiple_of(id_ref[p] * height, 8), height), :] = piece[...]
     row = lax.broadcasted_iota(I32, (PW, columns), 0)
     column = lax.broadcasted_iota(I32, (PW, columns), 1) + step * columns
     in_panel = jnp.logical_and(column < PW, flag_ref[1] == 0)
     upper = jnp.where(in_panel, jnp.where(row == column, -1.0, 0.0), upper_ref[...])
-    right = jnp.dot(pivot_ref[...], upper, precision=lax.Precision.HIGHEST, preferred_element_type=F32)
-    high = right.astype(BF16)
-    high_ref[...] = high
-    low_ref[...] = (right - high.astype(F32)).astype(BF16)
-
-
-def right_factor(flags, pivot_inverse, upper):
-    columns = upper.shape[1]
+    a, b = split(pivot_ref[...])
+    c, d = split(upper)
+    right = (
+        jnp.dot(a, d, preferred_element_type=F32) + jnp.dot(b, c, preferred_element_type=F32)
+    ) + jnp.dot(a, c, preferred_element_type=F32)
+    high_ref[...], low_ref[...] = split(right)
+
+
+def right_factor(flags, ids, pivot_inverse, pieces):
+    height, columns = pieces[0].shape
     block = min(512, columns)
-    spec = pl.BlockSpec((PW, block), lambda i, f: (0, i))
+    spec = pl.BlockSpec((PW, block), lambda i, f, s: (0, i))
     return pl.pallas_call(
         right_kernel,
-        out_shape=[jax.ShapeDtypeStruct((PW, columns), BF16)] * 2,
+        out_shape=[jax.ShapeDtypeStruct((PW, columns), t) for t in (BF16, BF16, F32)],
         grid_spec=pltpu.PrefetchScalarGridSpec(
-            num_scalar_prefetch=1,
+            num_scalar_prefetch=2,
             grid=(columns // block,),
-            in_specs=[pl.BlockSpec((PW, PW), lambda i, f: (0, 0)), spec],
-            out_specs=[spec, spec],
+            in_specs=[pl.BlockSpec((PW, PW), lambda i, f, s: (0, 0))]
+            + [pl.BlockSpec((height, block), lambda i, f, s: (0, i))] * len(pieces),
+            out_specs=[spec, spec, spec],
         ),
         compiler_params=compiler_params(("arbitrary",)),
+        cost_estimate=SHORT,
         name="right_factor",
-    )(flags, pivot_inverse, upper)
-
-
-def update_kernel(block, per_slice, flag_ref, slice_ref, base_ref, code_ref, scale_ref, high_ref, low_ref, out_ref):
+    )(flags, ids, pivot_inverse, *pieces)
+
+
+def update_kernel(block, per_slice, flag_ref, slice_ref, base_ref, code_ref, scale_ref, high_ref, low_ref, upper_ref, *refs):
+    out_ref, token_ref = refs[-2:]
     step = pl.program_id(0)
+
+    @pl.when(step == 0)
+    def _():
+        token_ref[...] = jnp.zeros_like(token_ref)
+
     row_block = slice_ref[step // per_slice] * per_slice + lax.rem(step, per_slice)
     above = jnp.logical_and(flag_ref[0] == 0, row_block < PW // block)
 
     @pl.when(above)
     def _():
-        out_ref[...] = base_ref[...]
+        out_ref[:, pl.ds(PW, out_ref.shape[1] - PW)] = upper_ref[:, pl.ds(PW, out_ref.shape[1] - PW)]
+        out_ref[:, pl.ds(0, PW)] = jnp.where(flag_ref[1] == 0, base_ref[:, pl.ds(0, PW)], upper_ref[:, pl.ds(0, PW)])
 
     @pl.when(jnp.logical_not(above))
     def _():
@@ -276,11 +712,8 @@
             jnp.dot(lower_part, high, preferred_element_type=F32)
             + jnp.dot(upper_part, low, preferred_element_type=F32)
         ) + jnp.dot(upper_part, high, preferred_element_type=F32)
-        eye = diagonal(TILE)
         for s in range(block // TILE):
-            line = scale_ref[0, :, pl.ds(s * TILE, TILE)].astype(I32).astype(F32)[:1]
-            exponent = jnp.sum(jnp.where(eye, line, 0.0), axis=1, keepdims=True)
-            scale = jnp.exp2(exponent * (1.0 / 64.0)) * (1.0 / CODE_TOP)
+            scale = row_scale(scale_ref[0, :, pl.ds(s * TILE, TILE)])
             rows = slice(s * TILE, (s + 1) * TILE)
             update = scale * product[rows]
             out_ref[pl.ds(s * TILE, TILE), pl.ds(PW, out_ref.shape[1] - PW)] = (
@@ -292,19 +725,26 @@
             )
 
 
-def update_rows(flags, slice_ids, base, codes, high, low):
+def update_rows(flags, slice_ids, base, codes, high, low, upper, into=None):
     rows, columns = base.shape
     slices, slice_rows, _ = codes.shape
     slice_rows -= META
     block = min(256, slice_rows)
     per_slice = slice_rows // block
 
+    if into is None:
+        extra, aliases = [], {}
+    elif into is base:
+        extra, aliases = [], {2: 0}
+    else:
+        extra, aliases = [into], {8: 0}
+
     def base_map(i, f, s):
         return (s[i // per_slice] * per_slice + lax.rem(i, per_slice), 0)
 
     return pl.pallas_call(
         functools.partial(update_kernel, block, per_slice),
-        out_shape=jax.ShapeDtypeStruct((rows, columns), F32),
+        out_shape=[jax.ShapeDtypeStruct((rows, columns), F32), jax.ShapeDtypeStruct((8, TILE), F32)],
         grid_spec=pltpu.PrefetchScalarGridSpec(
             num_scalar_prefetch=2,
             grid=(slices * per_slice,),
@@ -317,48 +757,78 @@
                 ),
                 pl.BlockSpec((PW, columns), lambda i, f, s: (0, 0)),
                 pl.BlockSpec((PW, columns), lambda i, f, s: (0, 0)),
+                pl.BlockSpec(
+                    (block, columns), lambda i, f, s: (jnp.minimum(base_map(i, f, s)[0], PW // block - 1), 0)
+                ),
+            ]
+            + [pl.BlockSpec(memory_space=pl.ANY)] * len(extra),
+            out_specs=[
+                pl.BlockSpec((block, columns), base_map),
+                pl.BlockSpec((8, TILE), lambda i, f, s: (0, 0)),
             ],
-            out_specs=pl.BlockSpec((block, columns), base_map),
         ),
-        input_output_aliases={2: 0},
+        input_output_aliases=aliases,
+        cost_estimate=pl.CostEstimate(
+            flops=6 * slices * slice_rows * PW * columns,
+            bytes_accessed=8 * slices * slice_rows * columns,
+            transcendentals=0,
+        ),
         compiler_params=compiler_params(("arbitrary",)),
         name="update_rows",
-    )(flags, slice_ids, base, codes, codes, high, low)
+    )(flags, slice_ids, base, codes, codes, high, low, upper, *extra)
+
+
+def gate(x, *earlier):
+    anywhere = pl.BlockSpec(memory_space=pl.ANY)
+    return pl.pallas_call(
+        lambda *refs: None,
+        out_shape=jax.ShapeDtypeStruct(x.shape, x.dtype),
+        in_specs=[anywhere] * (1 + len(earlier)),
+        out_specs=anywhere,
+        input_output_aliases={0: 0},
+        cost_estimate=pl.CostEstimate(flops=0, bytes_accessed=0, transcendentals=0),
+        name="gate",
+    )(x, *earlier)
 
 
 def ring_order(count):
     return list(range(0, count, 2)) + list(range(count - 1, 0, -2))
 
 
-def ring_gather(own, axis):
+def ring_gather(own, axis, before=()):
     count = lax.axis_size(axis)
     order = ring_order(count)
     ahead = [(order[i], order[(i + 1) % count]) for i in range(count)]
     back = [(b, a) for a, b in ahead]
-    place = jnp.zeros((), I32)
-    index = lax.axis_index(axis)
-    for p, d in enumerate(order):
-        place = jnp.where(index == d, p, place)
-    table = jnp.array(order, I32)
-    pieces, whose = [own], [index]
+    place = {d: p for p, d in enumerate(order)}
+    steps = [0] + [s for t in range(1, count // 2) for s in (-t, t)] + [count // 2]
+    whose = jnp.array([[order[(place[d] + s) % count] for s in steps] for d in range(count)], I32)
+    whose = lax.dynamic_index_in_dim(whose, lax.axis_index(axis), keepdims=False)
+    pieces = [own]
     left = right = own
     for step in range(1, count // 2):
+        if step in before:
+            left = gate(left, before[step])
         left, right = lax.ppermute(left, axis, ahead), lax.ppermute(right, axis, back)
         pieces += [left, right]
-        whose += [table[(place + count - step) % count], table[(place + step) % count]]
     half = own.shape[0] // 2
+    if count // 2 in before:
+        left = gate(left, before[count // 2])
     pieces.append(
         jnp.concatenate([lax.ppermute(left[:half], axis, ahead), lax.ppermute(right[half:], axis, back)], 0)
     )
-    whose.append(table[(place + count // 2) % count])
-    return pieces, jnp.stack(whose)
+    return pieces, whose
 
 
 def scatter_first(parts, axis):
     count = lax.axis_size(axis)
-    mine = jnp.where(lax.axis_index(axis) == 0, parts[0], jnp.zeros((), parts.dtype))
-    for k in range(1, count):
-        mine = mine + lax.ppermute(parts[k], axis, [(0, k)])
+    index = lax.axis_index(axis)
+    odd = lax.ppermute(jnp.concatenate([parts[k : k + 1] for k in range(1, count, 2)]), axis, [(0, 1)])
+    sent = [lax.ppermute(parts[k], axis, [(0, k)]) for k in range(2, count, 2)]
+    sent += [lax.ppermute(odd[k // 2], axis, [(1, k)]) for k in range(3, count, 2)]
+    mine = jnp.where(index == 0, parts[0], odd[0])
+    for x in sent:
+        mine = mine + x
     return mine
 
 
@@ -373,34 +843,132 @@
     return block
 
 
-def per_device(parent, child, owner, slot, pivot_inverse):
+def spread_pivots(parent, axis):
+    count = lax.axis_size(axis)
+    height = PW // count
+    mine = parent[:height]
+    index = lax.axis_index(axis)
+    received = mine
+    for k in range(1, count):
+        sent = lax.ppermute(parent[k * height : (k + 1) * height], axis, [(0, k)])
+        received = jnp.where(index == k, sent, received)
+    return received
+
+
+def gather_pieces(piece, axis):
+    count = lax.axis_size(axis)
+    pieces, ids = [piece], [lax.axis_index(axis)]
+    reach = count // 2
+    while reach >= 1:
+        pairs = [(i, i ^ reach) for i in range(count)]
+        pieces = pieces + [lax.ppermute(x, axis, pairs) for x in pieces]
+        ids = ids + [i ^ reach for i in ids]
+        reach //= 2
+    return pieces, jnp.stack(ids)
+
+
+def plain_path(flags, parent, child, owner, slot, pivot_inverse):
     bulk_count, column_count = lax.axis_size("bulk"), lax.axis_size("col")
     devices = bulk_count * column_count
     rows, columns = parent.shape
-    child_count = child.shape[0]
-    capacity = max(2, 2 * child_count // devices)
+    capacity = max(2, 2 * child.shape[0] // devices)
     width = columns // TILE
-    bulk_index, column_index = lax.axis_index("bulk"), lax.axis_index("col")
-    flags = jnp.stack([bulk_index, column_index]).astype(I32)
-
-    outgoing = pack(owner[:, 0], slot, child, devices, capacity)
+    outgoing = pack(owner, slot, child, devices, capacity)
     arrived = lax.all_to_all(outgoing, ("bulk", "col"), split_axis=0, concat_axis=0, tiled=True)
     slots = read_slots(arrived, capacity)
     strip, tile_column = slots // width, slots % width
-    valid = slots >= 0
     pivot_tiles = PW // TILE
-    in_panel = valid & (tile_column < pivot_tiles)
-    in_pivot = valid & (strip < pivot_tiles)
-    panel_key = jnp.where(in_panel, strip * pivot_tiles + tile_column, -1)
-    pivot_key = jnp.where(in_pivot, slots, -1)
+    panel_key = jnp.where((slots >= 0) & (tile_column < pivot_tiles), strip * pivot_tiles + tile_column, -1)
+    pivot_key = jnp.where((slots >= 0) & (strip < pivot_tiles), slots, -1)
 
     codes = code_panel(parent, arrived, panel_key, capacity, column_count)
-    upper = extend(parent, arrived, pivot_key, width, capacity, PW, columns)
-    upper = tree_broadcast(upper, "bulk")
-    high, low = right_factor(flags, pivot_inverse, upper)
+    upper = tree_broadcast(extend(parent, arrived, pivot_key, width, capacity, PW, columns), "bulk")
+    high, low, upper = right_factor(flags, jnp.zeros((1,), I32), pivot_inverse, [upper])
     pieces, whose = ring_gather(scatter_first(codes, "col"), "col")
     extended = extend(parent, arrived, slots, width, capacity, rows, columns)
-    return update_rows(flags, whose, extended, jnp.stack(pieces), high, low)
+    return update_rows(flags, whose, extended, jnp.stack(pieces), high, low, upper, into=extended)[0]
+
+
+def quick_path(plan, flags, parent, child, owner, slot, pivot_inverse):
+    bulk_count, column_count = lax.axis_size("bulk"), lax.axis_size("col")
+    width, half, groups, share = plan["width"], plan["half"], plan["groups"], plan["early"]
+    swap = [(i, i ^ half) for i in range(column_count)]
+    halves = [
+        [b * column_count + h * half + c for b in range(bulk_count) for c in range(half)] for h in range(2)
+    ]
+
+    def exchange(blocks, groups=None):
+        return lax.all_to_all(
+            blocks, ("bulk", "col"), split_axis=0, concat_axis=0, axis_index_groups=groups, tiled=True
+        )
+
+    early, near, far, over = sort_children(plan, owner, slot, flags, child)
+    far = lax.ppermute(far, "col", swap)
+    early = exchange(early)
+    code = scatter_first(encode_panel(parent, column_count), "col")
+    pivots = spread_pivots(parent, "bulk")
+
+    codes = read_slots(early, share)
+    panel_key = jnp.where((codes >= plan["panel_code"]) & (codes < plan["pivot_code"]), codes - plan["panel_code"], -1)
+    pivot_key = jnp.where(codes >= plan["pivot_code"], codes - plan["pivot_code"], -1)
+    plain_key = jnp.where(codes < plan["panel_code"], codes, -1)
+    code = extend_slice(gate(code, pivots, far), early, panel_key, share)
+    pivots = extend(pivots, early, pivot_key, width, share, *pivots.shape)
+    uppers, ids = gather_pieces(pivots, "bulk")
+    high, low, upper = right_factor(flags, ids, pivot_inverse, uppers)
+    pieces, whose = ring_gather(code, "col", {column_count // 2 - 1: high})
+    cut = len(pieces) - 3
+    result, done = update_rows(flags, whose[:cut], parent, jnp.stack(pieces[:cut]), high, low, upper)
+
+    late = distribute([near, far], over, groups, plan["late"])
+    late = exchange(gate(late, *pieces[-3:]), halves)
+    result, _ = update_rows(flags, whose[cut:], parent, jnp.stack(pieces[cut:]), high, low, upper, into=result)
+    result = touch_tiles(result, early, plain_key, width, share)
+
+    over = jnp.full((8, TILE), read_over(late, plan["late"]), I32)
+    over = jnp.max(jnp.maximum(over, lax.ppermute(over, "col", swap)))
+    return touch_tiles(result, late, read_slots(late, plan["late"]), width, plan["late"]), over
+
+
+def make_plan(bulk_count, column_count, rows, columns, child_count):
+    strips, width, pivot = rows // TILE, columns // TILE, PW // TILE
+    if pivot % bulk_count or strips % column_count or column_count % 4:
+        return None
+    half = column_count // 2
+    share = child_count // 2
+    panel_strips, pivot_strips = strips // column_count, pivot // bulk_count
+    panel_code = strips * width
+    return dict(
+        devices=bulk_count * column_count,
+        columns=column_count,
+        width=width,
+        pivot=pivot,
+        half=half,
+        groups=bulk_count * half,
+        early=max(2, child_count // (bulk_count * column_count)),
+        listed=max(8, share * 7 // 16),
+        late=12,
+        panel_strips=panel_strips,
+        pivot_strips=pivot_strips,
+        panel_code=panel_code,
+        pivot_code=panel_code + panel_strips * pivot,
+    )
+
+
+def per_device(parent, child, owner, slot, pivot_inverse):
+    flags = jnp.stack([lax.axis_index("bulk"), lax.axis_index("col")]).astype(I32)
+    owner = owner[:, 0]
+    plan = make_plan(
+        lax.axis_size("bulk"), lax.axis_size("col"), parent.shape[0], parent.shape[1], child.shape[0]
+    )
+    if plan is None:
+        return plain_path(flags, parent, child, owner, slot, pivot_inverse)
+    result, over = quick_path(plan, flags, parent, child, owner, slot, pivot_inverse)
+
+    def again(state):
+        return jnp.int32(0), plain_path(flags, parent, child, owner, slot, pivot_inverse)
+
+    return lax.while_loop(lambda state: state[0] > 0, again, (over, result))[1]
 
 
 def solution(mesh):

time: 461 us -> 375 us (0.81)
  the two profiles are of different devices: /device:TPU:0 before, /device:TPU:15 now
where the time goes in v3:
time: 375 us; the launch traced here: 371 us
  Pallas kernels  127 us (34%)
  waiting for transfers between devices  122 us (33%)
  starting transfers between devices  78.2 us (21%)
  local copies, waits for them, and re-layouts  22.2 us (6%)
  other arithmetic  19.1 us (5%)
    all_to_all x2, waiting for transfers between devices, exchange(): lax.all_to_all(blocks, ('bulk', 'col'), split_axis=0, concat_axis=0, axis...  74.8 us
    pallas_call x2, Pallas kernels, update_rows(): pl.pallas_call(functools.partial(update_kernel, block, per_slice), out_sh...  45.4 us
    ppermute x3, starting transfers between devices, ring_gather(): lax.ppermute(left, axis, ahead)  37 us
    pallas_call x2, Pallas kernels, touch_tiles(): pl.pallas_call(functools.partial(touch_kernel, width, capacity), out_shap...  36.6 us
    ppermute x3, waiting for transfers between devices, ring_gather(): lax.ppermute(left, axis, ahead)  24.7 us
    all_to_all x2, starting transfers between devices, exchange(): lax.all_to_all(blocks, ('bulk', 'col'), split_axis=0, concat_axis=0, axis...  15.5 us
    ppermute x3, waiting for transfers between devices, spread_pivots(): sent = lax.ppermute(parent[k * height:(k + 1) * height], axis, [(0, k)])  15 us
    pallas_call x1, Pallas kernels, sort_children(): pl.pallas_call(functools.partial(sort_kernel, plan), out_shape=[jax.Shape...  11.4 us
  transfers between devices with their start and end apart: 25, of which 7 were waited for; matrix products, arithmetic and copies ran while one was open for 8% of the time, Pallas kernels for 31%

profile of v3, /device:TPU:15, one launch (start us, length us, event | category | flops | bytes accessed | tf_op | source)
XLA Modules:
  0.0 370.7 jit_solution(13446612178732219859)
XLA Ops:
  0.0 1.2 add_select_fusion
  2.3 11.4 %sort_children.1 = (bf16[32,528,128]{2,1,0:T(8,128)(2,1)}, bf16[3600,128]{1,0:T(8,128)(2,1)}, bf16[3600,128]{1,0:T(8,128)(2,1)}, s32[1]{0:T(128)}) custom-call(s32[128]{0:T(128)} %or_select_fusion.kind_ref, s32[128]{0:T(128)} %get-tuple-element.131.dest_ref, s32[128]{0:T(128)} %get-tuple-element.126.code_ref, bf16[128,128,128]{2,1,0:T(8,128)(2,1)} %child_ref.1), custom_call_target="tpu_custom_call" | custom-call | bytes 4096 | tf_op jit(solution)/shard_map/sort_children/pallas_call | solution.py:228
  13.7 6.3 %all-to-all-start.1 = ((bf16[32,528,128]{2,1,0:T(8,128)(2,1)}), bf16[32,528,128]{2,1,0:T(8,128)(2,1)}, u32[]{:S(2)}, u32[]{:S(2)}) async-start(bf16[32,528,128]{2,1,0:T(8,128)(2,1)} %get-tuple-element.68), calls=%async_computation.1 | async-start | bytes 8650752 | tf_op jit(solution)/shard_map/all_to_all | solution.py:901
  20.1 8.4 %encode_panel.1 = s16[8,528,512]{2,1,0:T(8,128)(2,1)} custom-call(f32[4096,2048]{1,0:T(8,128)} %base_ref.5), custom_call_target="tpu_custom_call" | custom-call | bytes 4096 | tf_op jit(solution)/shard_map/encode_panel/pallas_call | solution.py:555
  28.5 3.3 slice_bitcast_fusion.11
  31.8 1.5 pad_add_fusion.1
  33.3 2.0 collective-permute-start.18
  35.4 3.5 fusion.26
  38.8 1.3 collective-permute-start.25
  40.1 1.7 collective-permute-start.26
  41.8 1.7 collective-permute-start.27
  43.4 2.2 collective-permute-start.17
  45.6 15.0 %collective-permute-done.25 = f32[128,2048]{1,0:T(8,128)S(1)} collective-permute-done((f32[128,2048]{1,0:T(8,128)}, f32[128,2048]{1,0:T(8,128)S(1)}, u32[]{:S(2)}, u32[]{:S(2)}) %collective-permute-start.25) | collective-permute-done | bytes 1048608 | tf_op jit(solution)/shard_map/ppermute | solution.py:853
  60.6 1.5 collective-permute-start.19
  62.1 1.5 collective-permute-start.20
  63.5 2.5 select_select_fusion.refs_1_.base_ref
  66.0 0.7 collective-permute-start.21
  66.7 2.5 slice_bitcast_fusion.8
  69.2 64.3 %all-to-all-done.1.arrived_ref = bf16[32,528,128]{2,1,0:T(8,128)(2,1)} async-done(((bf16[32,528,128]{2,1,0:T(8,128)(2,1)}), bf16[32,528,128]{2,1,0:T(8,128)(2,1)}, u32[]{:S(2)}, u32[]{:S(2)}) %all-to-all-start.1) | async-done | bytes 4325408 | tf_op jit(solution)/shard_map/all_to_all | solution.py:901
  133.5 0.9 slice_convert_fusion.1
  134.4 1.3 collective-permute-start.22
  135.7 1.5 collective-permute-start.23
  137.2 1.5 collective-permute-start.24
  139.4 4.3 %extend_add.3.refs_0_ = f32[128,2048]{1,0:T(8,128)} custom-call(s32[128]{0:T(128)} %get-tuple-element.161.key_ref, f32[128,2048]{1,0:T(8,128)} %select_select_fusion.refs_1_.base_ref, bf16[32,528,128]{2,1,0:T(8,128)(2,1)} %all-to-all-done.1.arrived_ref), custom_call_target="tpu_custom_call" | custom-call | flops 262144 | bytes 3145728 | tf_op jit(solution)/shard_map/extend_add/pallas_call | solution.py:395
  144.1 7.9 %collective-permute-done.22 = s16[528,512]{1,0:T(8,128)(2,1)S(1)} collective-permute-done((s16[528,512]{1,0:T(8,128)(2,1)}, s16[528,512]{1,0:T(8,128)(2,1)S(1)}, u32[]{:S(2)}, u32[]{:S(2)}) %collective-permute-start.22) | collective-permute-done | bytes 540704 | tf_op jit(solution)/shard_map/ppermute | solution.py:828
  152.0 3.2 fusion.15.refs_0_
  155.2 1.0 copy-done.5
  156.2 6.3 %extend_slice.1 = s16[528,512]{1,0:T(8,128)(2,1)} custom-call(s32[128]{0:T(128)} %get-tuple-element.162.key_ref, s16[528,512]{1,0:T(8,128)(2,1)} %gate.3.code_ref, bf16[32,528,128]{2,1,0:T(8,128)(2,1)} %all-to-all-done.1.arrived_ref), custom_call_target="tpu_custom_call" | custom-call | bytes 4096 | tf_op jit(solution)/shard_map/extend_slice/pallas_call | solution.py:582
  162.5 34.7 %collective-permute-start.28 = (s16[528,512]{1,0:T(8,128)(2,1)}, s16[528,512]{1,0:T(8,128)(2,1)}, u32[]{:S(2)}, u32[]{:S(2)}) collective-permute-start(s16[528,512]{1,0:T(8,128)(2,1)} %extend_slice.1), channel_id=1, source_target_pairs={{0,2},{2,4},{4,6},{6,7},{7,5},{5,3},{3,1},{1,0},{8,10},{10,12},{12... | collective-permute-start | bytes 1622024 | tf_op jit(solution)/shard_map/ppermute | solution.py:812
  197.3 1.6 collective-permute-start.31
  199.6 8.2 %collective-permute-done.28 = s16[528,512]{1,0:T(8,128)(2,1)} collective-permute-done((s16[528,512]{1,0:T(8,128)(2,1)}, s16[528,512]{1,0:T(8,128)(2,1)}, u32[]{:S(2)}, u32[]{:S(2)}) %collective-permute-start.28) | collective-permute-done | bytes 540704 | tf_op jit(solution)/shard_map/ppermute | solution.py:812
  207.8 2.2 collective-permute-start.29
  210.0 1.1 bitcast_dynamic-update-slice_fusion.11
  211.1 2.2 collective-permute-start.35
  213.3 1.1 bitcast_dynamic-update-slice_fusion.10
  214.4 1.1 bitcast_dynamic-update-slice_fusion.9
  215.5 7.6 %collective-permute-done.29.refs_0_ = s16[528,512]{1,0:T(8,128)(2,1)S(1)} collective-permute-done((s16[528,512]{1,0:T(8,128)(2,1)}, s16[528,512]{1,0:T(8,128)(2,1)S(1)}, u32[]{:S(2)}, u32[]{:S(2)}) %collective-permute-start.29) | collective-permute-done | bytes 540704 | tf_op jit(solution)/shard_map/ppermute | solution.py:812
  223.2 1.5 copy-done.18
  224.7 1.1 copy-done.15
  225.8 1.0 copy-done.16
  226.8 8.7 %right_factor.2 = (bf16[512,2048]{1,0:T(8,128)(2,1)}, bf16[512,2048]{1,0:T(8,128)(2,1)}, f32[512,2048]{1,0:T(8,128)}) custom-call(s32[2]{0:T(128)S(1)} %pad_add_fusion.3.flag_ref, s32[4]{0:T(128)} %pad_add_fusion.4.id_ref, f32[512,512]{1,0:T(8,128)S(1)} %copy-done.1, f32[128,2048]{1,0:T(8,128)} %extend_add.3.refs_0_, ...), custom_call_target="tpu_custom_call" | custom-call | bytes 4096 | tf_op jit(solution)/shard_map/right_factor/pallas_call | solution.py:672
  235.5 1.4 collective-permute-start.36
  238.1 8.8 %collective-permute-done.33.refs_1_ = s16[528,512]{1,0:T(8,128)(2,1)S(1)} collective-permute-done((s16[528,512]{1,0:T(8,128)(2,1)}, s16[528,512]{1,0:T(8,128)(2,1)S(1)}, u32[]{:S(2)}, u32[]{:S(2)}) %collective-permute-start.33) | collective-permute-done | bytes 540704 | tf_op jit(solution)/shard_map/ppermute | solution.py:812
  247.3 0.7 slice_convert_fusion.4
  248.0 1.2 collective-permute-start.38
  249.8 6.4 %distribute.1 = (bf16[16,1552,128]{2,1,0:T(8,128)(2,1)}, s32[1]{0:T(128)}) custom-call(s32[28]{0:T(128)} %get-tuple-element.159.refs_0_, s32[28]{0:T(128)} %get-tuple-element.157.refs_1_, s32[28]{0:T(128)} %get-tuple-element.158.refs_2_, s32[28]{0:T(128)} %get-tuple-element.156.refs_3_, bf16[3600,128]{1,0:T(8,128)(2,1)} %get-tuple-element.64.refs_4_, ...), custom_call_target="tpu_custom_call" | custom-call | bytes 4096 | tf_op jit(solution)/shard_map/distribute/pallas_call | solution.py:313
  256.4 0.8 copy-done.10
  257.2 9.2 %all-to-all-start.2 = ((bf16[16,1552,128]{2,1,0:T(8,128)(2,1)}), bf16[16,1552,128]{2,1,0:T(8,128)(2,1)}, u32[]{:S(2)}, u32[]{:S(2)}) async-start(bf16[16,1552,128]{2,1,0:T(8,128)(2,1)} %gate.5), calls=%async_computation.2 | async-start | bytes 12713984 | tf_op jit(solution)/shard_map/all_to_all | solution.py:901
  266.4 0.7 constant_dynamic-slice_fusion
  267.6 0.6 slice_bitcast_fusion.13.slice_ref
  268.2 0.8 bitcast_dynamic-update-slice_fusion.7.code_ref.scale_ref
  269.1 27.5 %update_rows.3 = (f32[4096,2048]{1,0:T(8,128)}, f32[8,128]{1,0:T(8,128)}) custom-call(s32[2]{0:T(128)S(1)} %pad_add_fusion.3.flag_ref, s32[5]{0:T(128)} %slice_bitcast_fusion.12.slice_ref, f32[4096,2048]{1,0:T(8,128)} %base_ref.5, s16[5,528,512]{2,1,0:T(8,128)(2,1)} %bitcast_dynamic-update-slice_fusion.7.code_ref.scale_ref, ...), custom_call_target="tpu_custom_call" | custom-call | flops 16106127360 | bytes 41943040 | tf_op jit(solution)/shard_map/update_rows/pallas_call | solution.py:745
  296.6 1.3 pad_add_fusion.2.code_ref.scale_ref
  297.8 18.0 %update_rows.4 = (f32[4096,2048]{1,0:T(8,128)}, f32[8,128]{1,0:T(8,128)}) custom-call(s32[2]{0:T(128)S(1)} %pad_add_fusion.3.flag_ref, s32[3]{0:T(128)} %slice_bitcast_fusion.13.slice_ref, f32[4096,2048]{1,0:T(8,128)} %base_ref.5, s16[3,528,512]{2,1,0:T(8,128)(2,1)} %pad_add_fusion.2.code_ref.scale_ref, ...), custom_call_target="tpu_custom_call", output_to_operand_aliasing={{0}: (8, {})} | custom-call | flops 9663676416 | bytes 25165824 | tf_op jit(solution)/shard_map/update_rows/pallas_call | solution.py:745
  315.8 17.1 %touch_tiles.2.base_ref = f32[4096,2048]{1,0:T(8,128)} custom-call(s32[128]{0:T(128)} %get-tuple-element.160.key_ref, f32[4096,2048]{1,0:T(8,128)} %get-tuple-element.73.base_ref, bf16[32,528,128]{2,1,0:T(8,128)(2,1)} %all-to-all-done.1.arrived_ref), custom_call_target="tpu_custom_call", output_to_operand_aliasing={{}: (1, {})} | custom-call | tf_op jit(solution)/shard_map/touch_tiles/pallas_call | solution.py:497
  332.9 10.5 %all-to-all-done.2.arrived_ref = bf16[16,1552,128]{2,1,0:T(8,128)(2,1)} async-done(((bf16[16,1552,128]{2,1,0:T(8,128)(2,1)}), bf16[16,1552,128]{2,1,0:T(8,128)(2,1)}, u32[]{:S(2)}, u32[]{:S(2)}) %all-to-all-start.2) | async-done | bytes 6357024 | tf_op jit(solution)/shard_map/all_to_all | solution.py:901
  343.5 1.5 fusion.18
  345.0 0.7 broadcast_in_dim.19
  345.7 1.7 collective-permute-start.39
  347.3 0.8 slice_convert_fusion.2
  348.2 0.7 add.150.key_ref
  348.8 19.4 %touch_tiles.3 = f32[4096,2048]{1,0:T(8,128)} custom-call(s32[192]{0:T(256)} %add.150.key_ref, f32[4096,2048]{1,0:T(8,128)} %touch_tiles.2.base_ref, bf16[16,1552,128]{2,1,0:T(8,128)(2,1)} %all-to-all-done.2.arrived_ref), custom_call_target="tpu_custom_call", output_to_operand_aliasing={{}: (1, {})} | custom-call | tf_op jit(solution)/shard_map/touch_tiles/pallas_call | solution.py:497
  368.3 1.4 maximum_reduce_fusion
  369.7 0.9 while.10
  (68 shorter events, 5.8 us)
Async XLA Ops:
  13.7 119.8 %all-to-all-start.1 = ((bf16[32,528,128]{2,1,0:T(8,128)(2,1)}), bf16[32,528,128]{2,1,0:T(8,128)(2,1)}, u32[]{:S(2)}, u32[]{:S(2)}) async-start(bf16[32,528,128]{2,1,0:T(8,128)(2,1)} %get-tuple-element.68), calls=%async_computation.1 | async-start | bytes 8650752 | tf_op jit(solution)/shard_map/all_to_all | solution.py:901
  33.3 33.4 %collective-permute-start.18 = (s16[4,528,512]{2,1,0:T(8,128)(2,1)}, s16[4,528,512]{2,1,0:T(8,128)(2,1)}, u32[]{:S(2)}, u32[]{:S(2)}) collective-permute-start(s16[4,528,512]{2,1,0:T(8,128)(2,1)} %pad_add_fusion.1), channel_id=1, source_target_pairs={{0,1},{8,9},{16,17},{24,25}} | collective-permute-start | bytes 6488072 | tf_op jit(solution)/shard_map/ppermute | solution.py:826
  38.8 21.8 %collective-permute-start.25 = (f32[128,2048]{1,0:T(8,128)}, f32[128,2048]{1,0:T(8,128)S(1)}, u32[]{:S(2)}, u32[]{:S(2)}) collective-permute-start(f32[128,2048]{1,0:T(8,128)} %get-tuple-element.145), channel_id=1, source_target_pairs={{0,24},{1,25},{2,26},{3,27},{4,28},{5,29},{6,30},{7,31}} | collective-permute-start | bytes 3145736 | tf_op jit(solution)/shard_map/ppermute | solution.py:853
  40.1 22.0 %collective-permute-start.26 = (f32[128,2048]{1,0:T(8,128)}, f32[128,2048]{1,0:T(8,128)}, u32[]{:S(2)}, u32[]{:S(2)}) collective-permute-start(f32[128,2048]{1,0:T(8,128)} %get-tuple-element.144), channel_id=1, source_target_pairs={{0,16},{1,17},{2,18},{3,19},{4,20},{5,21},{6,22},{7,23}} | collective-permute-start | bytes 3145736 | tf_op jit(solution)/shard_map/ppermute | solution.py:853
  41.8 21.8 %collective-permute-start.27 = (f32[128,2048]{1,0:T(8,128)S(1)}, f32[128,2048]{1,0:T(8,128)}, u32[]{:S(2)}, u32[]{:S(2)}) collective-permute-start(f32[128,2048]{1,0:T(8,128)S(1)} %get-tuple-element.143), channel_id=1, source_target_pairs={{0,8},{1,9},{2,10},{3,11},{4,12},{5,13},{6,14},{7,15}} | collective-permute-start | bytes 3145736 | tf_op jit(solution)/shard_map/ppermute | solution.py:853
  43.4 111.8 %collective-permute-start.17 = (bf16[3600,128]{1,0:T(8,128)(2,1)}, bf16[3600,128]{1,0:T(8,128)(2,1)S(1)}, u32[]{:S(2)}, u32[]{:S(2)}) collective-permute-start(bf16[3600,128]{1,0:T(8,128)(2,1)} %get-tuple-element.65), channel_id=1, source_target_pairs={{0,4},{1,5},{2,6},{3,7},{4,0},{5,1},{6,2},{7,3},{8,12},{9,13},{10,... | collective-permute-start | bytes 2764808 | tf_op jit(solution)/shard_map/ppermute | solution.py:906
  60.6 75.1 %collective-permute-start.19 = (s16[528,512]{1,0:T(8,128)(2,1)}, s16[528,512]{1,0:T(8,128)(2,1)}, u32[]{:S(2)}, u32[]{:S(2)}) collective-permute-start(s16[528,512]{1,0:T(8,128)(2,1)} %get-tuple-element.146), channel_id=1, source_target_pairs={{0,2},{8,10},{16,18},{24,26}} | collective-permute-start | bytes 1622024 | tf_op jit(solution)/shard_map/ppermute | solution.py:827
  62.1 75.1 %collective-permute-start.20 = (s16[528,512]{1,0:T(8,128)(2,1)}, s16[528,512]{1,0:T(8,128)(2,1)}, u32[]{:S(2)}, u32[]{:S(2)}) collective-permute-start(s16[528,512]{1,0:T(8,128)(2,1)} %get-tuple-element.148), channel_id=1, source_target_pairs={{0,4},{8,12},{16,20},{24,28}} | collective-permute-start | bytes 1622024 | tf_op jit(solution)/shard_map/ppermute | solution.py:827
  66.0 77.7 %collective-permute-start.21 = (s16[528,512]{1,0:T(8,128)(2,1)}, s16[528,512]{1,0:T(8,128)(2,1)S(1)}, u32[]{:S(2)}, u32[]{:S(2)}) collective-permute-start(s16[528,512]{1,0:T(8,128)(2,1)} %get-tuple-element.147), channel_id=1, source_target_pairs={{0,6},{8,14},{16,22},{24,30}} | collective-permute-start | bytes 1622024 | tf_op jit(solution)/shard_map/ppermute | solution.py:827
  134.4 17.6 %collective-permute-start.22 = (s16[528,512]{1,0:T(8,128)(2,1)}, s16[528,512]{1,0:T(8,128)(2,1)S(1)}, u32[]{:S(2)}, u32[]{:S(2)}) collective-permute-start(s16[528,512]{1,0:T(8,128)(2,1)} %get-tuple-element.153), channel_id=1, source_target_pairs={{1,3},{9,11},{17,19},{25,27}} | collective-permute-start | bytes 1622024 | tf_op jit(solution)/shard_map/ppermute | solution.py:828
  135.7 16.3 %collective-permute-start.23 = (s16[528,512]{1,0:T(8,128)(2,1)}, s16[528,512]{1,0:T(8,128)(2,1)}, u32[]{:S(2)}, u32[]{:S(2)}) collective-permute-start(s16[528,512]{1,0:T(8,128)(2,1)} %get-tuple-element.155), channel_id=1, source_target_pairs={{1,5},{9,13},{17,21},{25,29}} | collective-permute-start | bytes 1622024 | tf_op jit(solution)/shard_map/ppermute | solution.py:828
  137.2 14.8 %collective-permute-start.24 = (s16[528,512]{1,0:T(8,128)(2,1)S(1)}, s16[528,512]{1,0:T(8,128)(2,1)}, u32[]{:S(2)}, u32[]{:S(2)}) collective-permute-start(s16[528,512]{1,0:T(8,128)(2,1)S(1)} %get-tuple-element.154), channel_id=1, source_target_pairs={{1,7},{9,15},{17,23},{25,31}} | collective-permute-start | bytes 1622024 | tf_op jit(solution)/shard_map/ppermute | solution.py:828
  143.7 55.3 %collective-permute-start.30 = (f32[128,2048]{1,0:T(8,128)}, f32[128,2048]{1,0:T(8,128)}, u32[]{:S(2)}, u32[]{:S(2)}) collective-permute-start(f32[128,2048]{1,0:T(8,128)} %extend_add.3.refs_0_), channel_id=1, source_target_pairs={{0,16},{8,24},{16,0},{24,8},{1,17},{9,25},{17,1},{25,9},{2,18},{10... | collective-permute-start | bytes 3145736 | tf_op jit(solution)/shard_map/ppermute | solution.py:864
  155.2 42.1 %copy-start.4 = (f32[128,2048]{1,0:T(8,128)S(1)}, f32[128,2048]{1,0:T(8,128)}, u32[]{:S(2)}) copy-start(f32[128,2048]{1,0:T(8,128)} %extend_add.3.refs_0_) | copy-start | bytes 3145732
  155.2 1.0 copy-start.5
  156.2 70.6 %copy-start.1 = (f32[512,512]{1,0:T(8,128)S(1)}, f32[512,512]{1,0:T(8,128)}, u32[]{:S(2)}) copy-start(f32[512,512]{1,0:T(8,128)} %pivot_ref.1) | copy-start | bytes 3145732
  162.5 45.3 %collective-permute-start.28 = (s16[528,512]{1,0:T(8,128)(2,1)}, s16[528,512]{1,0:T(8,128)(2,1)}, u32[]{:S(2)}, u32[]{:S(2)}) collective-permute-start(s16[528,512]{1,0:T(8,128)(2,1)} %extend_slice.1), channel_id=1, source_target_pairs={{0,2},{2,4},{4,6},{6,7},{7,5},{5,3},{3,1},{1,0},{8,10},{10,12},{12... | collective-permute-start | bytes 1622024 | tf_op jit(solution)/shard_map/ppermute | solution.py:812
  197.3 13.8 %collective-permute-start.34 = (s16[528,512]{1,0:T(8,128)(2,1)}, s16[528,512]{1,0:T(8,128)(2,1)}, u32[]{:S(2)}, u32[]{:S(2)}) collective-permute-start(s16[528,512]{1,0:T(8,128)(2,1)} %extend_slice.1), channel_id=1, source_target_pairs={{2,0},{4,2},{6,4},{7,6},{5,7},{3,5},{1,3},{0,1},{10,8},{12,10},{14... | collective-permute-start | bytes 1622024 | tf_op jit(solution)/shard_map/ppermute | solution.py:812
  197.3 25.8 %collective-permute-start.31 = (f32[128,2048]{1,0:T(8,128)S(1)}, f32[128,2048]{1,0:T(8,128)S(1)}, u32[]{:S(2)}, u32[]{:S(2)}) collective-permute-start(f32[128,2048]{1,0:T(8,128)S(1)} %copy-done.4), channel_id=1, source_target_pairs={{0,8},{8,0},{16,24},{24,16},{1,9},{9,1},{17,25},{25,17},{2,10},{10... | collective-permute-start | bytes 3145736 | tf_op jit(solution)/shard_map/ppermute | solution.py:864
  199.0 25.8 %collective-permute-start.32 = (f32[128,2048]{1,0:T(8,128)}, f32[128,2048]{1,0:T(8,128)S(1)}, u32[]{:S(2)}, u32[]{:S(2)}) collective-permute-start(f32[128,2048]{1,0:T(8,128)} %collective-permute-done.30.refs_1_), channel_id=1, source_target_pairs={{0,8},{8,0},{16,24},{24,16},{1,9},{9,1},{17,25},{25,17},{2,10},{10... | collective-permute-start | bytes 3145736 | tf_op jit(solution)/shard_map/ppermute | solution.py:864
  207.8 15.3 %collective-permute-start.29 = (s16[528,512]{1,0:T(8,128)(2,1)}, s16[528,512]{1,0:T(8,128)(2,1)S(1)}, u32[]{:S(2)}, u32[]{:S(2)}) collective-permute-start(s16[528,512]{1,0:T(8,128)(2,1)} %collective-permute-done.28), channel_id=1, source_target_pairs={{0,2},{2,4},{4,6},{6,7},{7,5},{5,3},{3,1},{1,0},{8,10},{10,12},{12... | collective-permute-start | bytes 1622024 | tf_op jit(solution)/shard_map/ppermute | solution.py:812
  211.1 24.4 %collective-permute-start.35 = (s16[528,512]{1,0:T(8,128)(2,1)}, s16[528,512]{1,0:T(8,128)(2,1)S(1)}, u32[]{:S(2)}, u32[]{:S(2)}) collective-permute-start(s16[528,512]{1,0:T(8,128)(2,1)} %collective-permute-done.34), channel_id=1, source_target_pairs={{2,0},{4,2},{6,4},{7,6},{5,7},{3,5},{1,3},{0,1},{10,8},{12,10},{14... | collective-permute-start | bytes 1622024 | tf_op jit(solution)/shard_map/ppermute | solution.py:812
  223.1 12.3 %copy-start.12 = (s16[528,512]{1,0:T(8,128)(2,1)}, s16[528,512]{1,0:T(8,128)(2,1)S(1)}, u32[]{:S(2)}) copy-start(s16[528,512]{1,0:T(8,128)(2,1)S(1)} %collective-permute-done.29.refs_0_) | copy-start | bytes 1622020
  223.2 1.6 copy-start.18
  224.7 1.1 copy-start.15
  225.8 1.0 copy-start.16
  235.5 11.5 %collective-permute-start.33 = (s16[528,512]{1,0:T(8,128)(2,1)}, s16[528,512]{1,0:T(8,128)(2,1)S(1)}, u32[]{:S(2)}, u32[]{:S(2)}) collective-permute-start(s16[528,512]{1,0:T(8,128)(2,1)} %gate.4), channel_id=1, source_target_pairs={{0,2},{2,4},{4,6},{6,7},{7,5},{5,3},{3,1},{1,0},{8,10},{10,12},{12... | collective-permute-start | bytes 1622024 | tf_op jit(solution)/shard_map/ppermute | solution.py:812
  235.5 12.5 %collective-permute-start.36 = (s16[528,512]{1,0:T(8,128)(2,1)S(1)}, s16[528,512]{1,0:T(8,128)(2,1)S(1)}, u32[]{:S(2)}, u32[]{:S(2)}) collective-permute-start(s16[528,512]{1,0:T(8,128)(2,1)S(1)} %collective-permute-done.35), channel_id=1, source_target_pairs={{2,0},{4,2},{6,4},{7,6},{5,7},{3,5},{1,3},{0,1},{10,8},{12,10},{14... | collective-permute-start | bytes 1622024 | tf_op jit(solution)/shard_map/ppermute | solution.py:812
  247.0 9.4 %copy-start.6 = (s16[528,512]{1,0:T(8,128)(2,1)}, s16[528,512]{1,0:T(8,128)(2,1)S(1)}, u32[]{:S(2)}) copy-start(s16[528,512]{1,0:T(8,128)(2,1)S(1)} %collective-permute-done.33.refs_1_) | copy-start | bytes 1622020
  247.0 9.2 %collective-permute-start.37 = (s16[264,512]{1,0:T(8,128)(2,1)S(1)}, s16[264,512]{1,0:T(8,128)(2,1)S(1)}, u32[]{:S(2)}, u32[]{:S(2)}) collective-permute-start(s16[264,512]{1,0:T(8,128)(2,1)S(1)} %slice.266), channel_id=1, source_target_pairs={{0,2},{2,4},{4,6},{6,7},{7,5},{5,3},{3,1},{1,0},{8,10},{10,12},{12... | collective-permute-start | bytes 811016 | tf_op jit(solution)/shard_map/ppermute | solution.py:818
  248.0 8.3 %copy-start.8 = (s16[528,512]{1,0:T(8,128)(2,1)}, s16[528,512]{1,0:T(8,128)(2,1)S(1)}, u32[]{:S(2)}) copy-start(s16[528,512]{1,0:T(8,128)(2,1)S(1)} %collective-permute-done.36.refs_2_) | copy-start | bytes 1622020
  248.0 8.3 %collective-permute-start.38 = (s16[264,512]{1,0:T(8,128)(2,1)S(1)}, s16[264,512]{1,0:T(8,128)(2,1)S(1)}, u32[]{:S(2)}, u32[]{:S(2)}) collective-permute-start(s16[264,512]{1,0:T(8,128)(2,1)S(1)} %slice.267), channel_id=1, source_target_pairs={{2,0},{4,2},{6,4},{7,6},{5,7},{3,5},{1,3},{0,1},{10,8},{12,10},{14... | collective-permute-start | bytes 811016 | tf_op jit(solution)/shard_map/ppermute | solution.py:818
  256.3 0.8 copy-start.10
  257.2 86.3 %all-to-all-start.2 = ((bf16[16,1552,128]{2,1,0:T(8,128)(2,1)}), bf16[16,1552,128]{2,1,0:T(8,128)(2,1)}, u32[]{:S(2)}, u32[]{:S(2)}) async-start(bf16[16,1552,128]{2,1,0:T(8,128)(2,1)} %gate.5), calls=%async_computation.2 | async-start | bytes 12713984 | tf_op jit(solution)/shard_map/all_to_all | solution.py:901
  269.1 27.5 %copy-start.7 = (s16[528,512]{1,0:T(8,128)(2,1)S(1)}, s16[528,512]{1,0:T(8,128)(2,1)}, u32[]{:S(2)}) copy-start(s16[528,512]{1,0:T(8,128)(2,1)} %copy-done.6) | copy-start | bytes 1622020
  269.1 27.5 %copy-start.9 = (s16[528,512]{1,0:T(8,128)(2,1)S(1)}, s16[528,512]{1,0:T(8,128)(2,1)}, u32[]{:S(2)}) copy-start(s16[528,512]{1,0:T(8,128)(2,1)} %copy-done.8) | copy-start | bytes 1622020
  269.1 27.5 %copy-start.11 = (s16[528,512]{1,0:T(8,128)(2,1)S(1)}, s16[528,512]{1,0:T(8,128)(2,1)}, u32[]{:S(2)}) copy-start(s16[528,512]{1,0:T(8,128)(2,1)} %copy-done.10) | copy-start | bytes 1622020
  345.7 22.6 %collective-permute-start.39 = (s32[8,128]{1,0:T(8,128)S(1)}, s32[8,128]{1,0:T(8,128)S(1)}, u32[]{:S(2)}, u32[]{:S(2)}) collective-permute-start(s32[8,128]{1,0:T(8,128)S(1)} %broadcast_in_dim.19), channel_id=1, source_target_pairs={{0,4},{1,5},{2,6},{3,7},{4,0},{5,1},{6,2},{7,3},{8,12},{9,13},{10,... | collective-permute-start | bytes 12296 | tf_op jit(solution)/shard_map/ppermute | solution.py:929
  348.8 20.9 %copy-start.21 = (s32[128]{0:T(128)S(1)}, s32[128]{0:T(128)}, u32[]{:S(2)}) copy-start(s32[128]{0:T(128)} %param.12) | copy-start | bytes 1540
  348.8 20.9 %copy-start.22 = (s32[128,1]{0,1:T(1,128)S(1)}, s32[128,1]{0,1:T(1,128)}, u32[]{:S(2)}) copy-start(s32[128,1]{0,1:T(1,128)} %param.11) | copy-start | bytes 1540

commit v4 on v3

--- a/solution.py
+++ b/solution.py
@@ -414,8 +414,8 @@
     )(key, base, arrived)
 
 
-AHEAD = 8
-BUFFERS = 16
+AHEAD = 24
+BUFFERS = 48
 
 
 def touch_kernel(
@@ -820,10 +820,12 @@
     return pieces, whose
 
 
-def scatter_first(parts, axis):
+def scatter_first(parts, axis, before=()):
     count = lax.axis_size(axis)
     index = lax.axis_index(axis)
     odd = lax.ppermute(jnp.concatenate([parts[k : k + 1] for k in range(1, count, 2)]), axis, [(0, 1)])
+    if before:
+        odd = gate(odd, *before)
     sent = [lax.ppermute(parts[k], axis, [(0, k)]) for k in range(2, count, 2)]
     sent += [lax.ppermute(odd[k // 2], axis, [(1, k)]) for k in range(3, count, 2)]
     mine = jnp.where(index == 0, parts[0], odd[0])
@@ -903,25 +905,25 @@
         )
 
     early, near, far, over = sort_children(plan, owner, slot, flags, child)
-    far = lax.ppermute(far, "col", swap)
     early = exchange(early)
     code = scatter_first(encode_panel(parent, column_count), "col")
     pivots = spread_pivots(parent, "bulk")
+    early = gate(early, code, pivots)
 
     codes = read_slots(early, share)
     panel_key = jnp.where((codes >= plan["panel_code"]) & (codes < plan["pivot_code"]), codes - plan["panel_code"], -1)
     pivot_key = jnp.where(codes >= plan["pivot_code"], codes - plan["pivot_code"], -1)
     plain_key = jnp.where(codes < plan["panel_code"], codes, -1)
-    code = extend_slice(gate(code, pivots, far), early, panel_key, share)
+    code = extend_slice(code, early, panel_key, share)
     pivots = extend(pivots, early, pivot_key, width, share, *pivots.shape)
     uppers, ids = gather_pieces(pivots, "bulk")
     high, low, upper = right_factor(flags, ids, pivot_inverse, uppers)
-    pieces, whose = ring_gather(code, "col", {column_count // 2 - 1: high})
+    far = lax.ppermute(far, "col", swap)
+    pieces, whose = ring_gather(code, "col", {2: far})
     cut = len(pieces) - 3
-    result, done = update_rows(flags, whose[:cut], parent, jnp.stack(pieces[:cut]), high, low, upper)
-
     late = distribute([near, far], over, groups, plan["late"])
-    late = exchange(gate(late, *pieces[-3:]), halves)
+    late = exchange(gate(late, high, *pieces[-3:]), halves)
+    result, _ = update_rows(flags, whose[:cut], parent, jnp.stack(pieces[:cut]), high, low, upper)
     result, _ = update_rows(flags, whose[cut:], parent, jnp.stack(pieces[cut:]), high, low, upper, into=result)
     result = touch_tiles(result, early, plain_key, width, share)
 

time: 375 us -> 346 us (0.923)
  the two profiles are of different devices: /device:TPU:15 before, /device:TPU:5 now
where the time goes in v4:
time: 346 us; the launch traced here: 343 us
  Pallas kernels  117 us (34%)
  waiting for transfers between devices  117 us (34%)
  starting transfers between devices  71.4 us (21%)
  other arithmetic  18.8 us (5%)
  local copies, waits for them, and re-layouts  17.7 us (5%)
    ppermute x1, waiting for transfers between devices, scatter_first(): lax.ppermute(jnp.concatenate([parts[k:k + 1] for k in range(1, count, 2)]...  60.6 us
    pallas_call x2, Pallas kernels, update_rows(): pl.pallas_call(functools.partial(update_kernel, block, per_slice), out_sh...  44.5 us
    ppermute x3, starting transfers between devices, ring_gather(): lax.ppermute(left, axis, ahead)  34.9 us
    pallas_call x2, Pallas kernels, touch_tiles(): pl.pallas_call(functools.partial(touch_kernel, width, capacity), out_shap...  27.3 us
    ppermute x3, waiting for transfers between devices, ring_gather(): lax.ppermute(left, axis, ahead)  25 us
    all_to_all x2, waiting for transfers between devices, exchange(): lax.all_to_all(blocks, ('bulk', 'col'), split_axis=0, concat_axis=0, axis...  14.5 us
    ppermute x3, waiting for transfers between devices, scatter_first(): sent = [lax.ppermute(parts[k], axis, [(0, k)]) for k in range(2, count, 2)]  13.7 us
    all_to_all x2, starting transfers between devices, exchange(): lax.all_to_all(blocks, ('bulk', 'col'), split_axis=0, concat_axis=0, axis...  12.9 us
  transfers between devices with their start and end apart: 25, of which 9 were waited for; matrix products, arithmetic and copies ran while one was open for 9% of the time, Pallas kernels for 28%

profile of v4, /device:TPU:5, one launch (start us, length us, event | category | flops | bytes accessed | tf_op | source)
XLA Modules:
  0.0 342.9 jit_solution(3845443992134168411)
XLA Ops:
  0.0 1.3 add_select_fusion
  1.3 0.6 multiply_add_fusion
  2.4 11.4 %sort_children.1 = (bf16[32,528,128]{2,1,0:T(8,128)(2,1)}, bf16[3600,128]{1,0:T(8,128)(2,1)}, bf16[3600,128]{1,0:T(8,128)(2,1)}, s32[1]{0:T(128)}) custom-call(s32[128]{0:T(128)} %or_select_fusion.kind_ref, s32[128]{0:T(128)} %get-tuple-element.131.dest_ref, s32[128]{0:T(128)} %get-tuple-element.126.code_ref, bf16[128,128,128]{2,1,0:T(8,128)(2,1)} %child_ref.1), custom_call_target="tpu_custom_call" | custom-call | bytes 4096 | tf_op jit(solution)/shard_map/sort_children/pallas_call | solution.py:228
  13.8 6.5 %all-to-all-start.1 = ((bf16[32,528,128]{2,1,0:T(8,128)(2,1)}), bf16[32,528,128]{2,1,0:T(8,128)(2,1)}, u32[]{:S(2)}, u32[]{:S(2)}) async-start(bf16[32,528,128]{2,1,0:T(8,128)(2,1)} %get-tuple-element.68), calls=%async_computation.1 | async-start | bytes 8650752 | tf_op jit(solution)/shard_map/all_to_all | solution.py:903
  20.3 8.4 %encode_panel.1 = s16[8,528,512]{2,1,0:T(8,128)(2,1)} custom-call(f32[4096,2048]{1,0:T(8,128)} %base_ref.5), custom_call_target="tpu_custom_call" | custom-call | bytes 4096 | tf_op jit(solution)/shard_map/encode_panel/pallas_call | solution.py:555
  28.7 3.3 slice_bitcast_fusion.11
  32.0 1.5 pad_add_fusion.1
  33.5 3.2 collective-permute-start.18
  36.7 3.6 %fusion.26 = (f32[128,2048]{1,0:T(8,128)}, f32[128,2048]{1,0:T(8,128)}, f32[128,2048]{1,0:T(8,128)}) fusion(f32[4096,2048]{1,0:T(8,128)} %base_ref.5), kind=kLoop, calls=%fused_computation.122 | loop fusion | bytes 6291456 | tf_op jit(solution)/shard_map/slice | solution.py:855
  40.3 1.3 collective-permute-start.25
  41.6 1.7 collective-permute-start.26
  43.3 1.6 collective-permute-start.27
  45.0 2.1 collective-permute-start.19
  47.1 60.6 %collective-permute-done.18 = s16[4,528,512]{2,1,0:T(8,128)(2,1)S(1)} collective-permute-done((s16[4,528,512]{2,1,0:T(8,128)(2,1)}, s16[4,528,512]{2,1,0:T(8,128)(2,1)S(1)}, u32[]{:S(2)}, u32[]{:S(2)}) %collective-permute-start.18) | collective-permute-done | bytes 2162720 | tf_op jit(solution)/shard_map/ppermute | solution.py:826
  107.8 1.3 collective-permute-start.20
  109.2 1.3 collective-permute-start.21
  110.5 0.7 collective-permute-start.22
  111.2 0.7 collective-permute-start.23
  111.9 0.7 collective-permute-start.24
  112.7 2.6 select_select_fusion.refs_2_.base_ref
  115.2 5.1 %collective-permute-done.20 = s16[528,512]{1,0:T(8,128)(2,1)S(1)} collective-permute-done((s16[528,512]{1,0:T(8,128)(2,1)}, s16[528,512]{1,0:T(8,128)(2,1)S(1)}, u32[]{:S(2)}, u32[]{:S(2)}) %collective-permute-start.20) | collective-permute-done | bytes 540704 | tf_op jit(solution)/shard_map/ppermute | solution.py:829
  120.3 3.0 collective-permute-start.17
  123.3 8.6 %collective-permute-done.21 = s16[528,512]{1,0:T(8,128)(2,1)S(1)} collective-permute-done((s16[528,512]{1,0:T(8,128)(2,1)}, s16[528,512]{1,0:T(8,128)(2,1)S(1)}, u32[]{:S(2)}, u32[]{:S(2)}) %collective-permute-start.21) | collective-permute-done | bytes 540704 | tf_op jit(solution)/shard_map/ppermute | solution.py:829
  131.9 2.8 fusion.15.refs_1_.code_ref
  134.6 2.8 all-to-all-done.1.refs_0_
  137.5 0.9 slice_convert_fusion.1
  138.5 0.6 compare_select_fusion
  139.1 6.2 %extend_slice.1 = s16[528,512]{1,0:T(8,128)(2,1)} custom-call(s32[128]{0:T(128)} %get-tuple-element.161.key_ref, s16[528,512]{1,0:T(8,128)(2,1)} %fusion.15.refs_1_.code_ref, bf16[32,528,128]{2,1,0:T(8,128)(2,1)} %gate.3.arrived_ref), custom_call_target="tpu_custom_call" | custom-call | bytes 4096 | tf_op jit(solution)/shard_map/extend_slice/pallas_call | solution.py:582
  145.4 20.9 %collective-permute-start.31 = (s16[528,512]{1,0:T(8,128)(2,1)}, s16[528,512]{1,0:T(8,128)(2,1)S(1)}, u32[]{:S(2)}, u32[]{:S(2)}) collective-permute-start(s16[528,512]{1,0:T(8,128)(2,1)} %extend_slice.1), channel_id=1, source_target_pairs={{0,2},{2,4},{4,6},{6,7},{7,5},{5,3},{3,1},{1,0},{8,10},{10,12},{12... | collective-permute-start | bytes 1622024 | tf_op jit(solution)/shard_map/ppermute | solution.py:812
  166.3 4.3 %extend_add.3.refs_0_ = f32[128,2048]{1,0:T(8,128)} custom-call(s32[128]{0:T(128)} %get-tuple-element.162.key_ref, f32[128,2048]{1,0:T(8,128)} %select_select_fusion.refs_2_.base_ref, bf16[32,528,128]{2,1,0:T(8,128)(2,1)} %gate.3.arrived_ref), custom_call_target="tpu_custom_call" | custom-call | flops 262144 | bytes 3145728 | tf_op jit(solution)/shard_map/extend_add/pallas_call | solution.py:395
  170.6 0.8 bitcast_dynamic-update-slice_fusion.11
  171.4 6.5 %collective-permute-done.31.refs_0_ = s16[528,512]{1,0:T(8,128)(2,1)S(1)} collective-permute-done((s16[528,512]{1,0:T(8,128)(2,1)}, s16[528,512]{1,0:T(8,128)(2,1)S(1)}, u32[]{:S(2)}, u32[]{:S(2)}) %collective-permute-start.31) | collective-permute-done | bytes 540704 | tf_op jit(solution)/shard_map/ppermute | solution.py:812
  177.9 0.9 bitcast_dynamic-update-slice_fusion.10
  178.9 0.9 copy-done.4
  179.8 11.8 %collective-permute-start.32 = (s16[528,512]{1,0:T(8,128)(2,1)}, s16[528,512]{1,0:T(8,128)(2,1)}, u32[]{:S(2)}, u32[]{:S(2)}) collective-permute-start(s16[528,512]{1,0:T(8,128)(2,1)} %gate.4), channel_id=1, source_target_pairs={{0,2},{2,4},{4,6},{6,7},{7,5},{5,3},{3,1},{1,0},{8,10},{10,12},{12... | collective-permute-start | bytes 1622024 | tf_op jit(solution)/shard_map/ppermute | solution.py:812
  191.6 11.5 %collective-permute-done.32 = s16[528,512]{1,0:T(8,128)(2,1)} collective-permute-done((s16[528,512]{1,0:T(8,128)(2,1)}, s16[528,512]{1,0:T(8,128)(2,1)}, u32[]{:S(2)}, u32[]{:S(2)}) %collective-permute-start.32) | collective-permute-done | bytes 540704 | tf_op jit(solution)/shard_map/ppermute | solution.py:812
  203.2 2.2 collective-permute-start.33
  205.4 0.7 slice_convert_fusion.5
  206.0 1.6 collective-permute-start.29
  207.8 0.6 pad_add_fusion.4.id_ref
  209.0 7.0 %collective-permute-done.33.refs_2_ = s16[528,512]{1,0:T(8,128)(2,1)S(1)} collective-permute-done((s16[528,512]{1,0:T(8,128)(2,1)}, s16[528,512]{1,0:T(8,128)(2,1)S(1)}, u32[]{:S(2)}, u32[]{:S(2)}) %collective-permute-start.33) | collective-permute-done | bytes 540704 | tf_op jit(solution)/shard_map/ppermute | solution.py:812
  216.0 2.1 collective-permute-start.37
  218.1 0.7 slice_convert_fusion.4
  218.8 3.3 collective-permute-done.36.refs_3_
  222.2 0.7 slice_bitcast_fusion.14
  222.9 6.2 %distribute.1 = (bf16[16,1552,128]{2,1,0:T(8,128)(2,1)}, s32[1]{0:T(128)}) custom-call(s32[28]{0:T(128)} %get-tuple-element.159.refs_0_, s32[28]{0:T(128)} %get-tuple-element.157.refs_1_, s32[28]{0:T(128)} %get-tuple-element.158.refs_2_, s32[28]{0:T(128)} %get-tuple-element.156.refs_3_, bf16[3600,128]{1,0:T(8,128)(2,1)} %get-tuple-element.64.refs_4_, ...), custom_call_target="tpu_custom_call" | custom-call | bytes 4096 | tf_op jit(solution)/shard_map/distribute/pallas_call | solution.py:313
  229.3 8.6 %right_factor.2 = (bf16[512,2048]{1,0:T(8,128)(2,1)}, bf16[512,2048]{1,0:T(8,128)(2,1)}, f32[512,2048]{1,0:T(8,128)}) custom-call(s32[2]{0:T(128)S(1)} %pad_add_fusion.3.flag_ref, s32[4]{0:T(128)} %pad_add_fusion.4.id_ref, f32[512,512]{1,0:T(8,128)S(1)} %copy-done.1, f32[128,2048]{1,0:T(8,128)} %extend_add.3.refs_0_, ...), custom_call_target="tpu_custom_call" | custom-call | bytes 4096 | tf_op jit(solution)/shard_map/right_factor/pallas_call | solution.py:672
  237.9 6.4 %all-to-all-start.2 = ((bf16[16,1552,128]{2,1,0:T(8,128)(2,1)}), bf16[16,1552,128]{2,1,0:T(8,128)(2,1)}, u32[]{:S(2)}, u32[]{:S(2)}) async-start(bf16[16,1552,128]{2,1,0:T(8,128)(2,1)} %gate.5), calls=%async_computation.2 | async-start | bytes 12713984 | tf_op jit(solution)/shard_map/all_to_all | solution.py:903
  244.3 0.7 constant_dynamic-slice_fusion
  245.6 0.6 slice_bitcast_fusion.13.slice_ref
  246.2 1.9 bitcast_dynamic-update-slice_fusion.9
  248.1 1.9 bitcast_dynamic-update-slice_fusion.8
  250.0 0.8 bitcast_dynamic-update-slice_fusion.7.code_ref.scale_ref
  250.8 1.3 pad_add_fusion.2.code_ref.scale_ref
  252.1 26.5 %update_rows.3 = (f32[4096,2048]{1,0:T(8,128)}, f32[8,128]{1,0:T(8,128)}) custom-call(s32[2]{0:T(128)S(1)} %pad_add_fusion.3.flag_ref, s32[5]{0:T(128)} %slice_bitcast_fusion.12.slice_ref, f32[4096,2048]{1,0:T(8,128)} %base_ref.5, s16[5,528,512]{2,1,0:T(8,128)(2,1)} %bitcast_dynamic-update-slice_fusion.7.code_ref.scale_ref, ...), custom_call_target="tpu_custom_call" | custom-call | flops 16106127360 | bytes 41943040 | tf_op jit(solution)/shard_map/update_rows/pallas_call | solution.py:745
  278.7 18.0 %update_rows.4 = (f32[4096,2048]{1,0:T(8,128)}, f32[8,128]{1,0:T(8,128)}) custom-call(s32[2]{0:T(128)S(1)} %pad_add_fusion.3.flag_ref, s32[3]{0:T(128)} %slice_bitcast_fusion.13.slice_ref, f32[4096,2048]{1,0:T(8,128)} %base_ref.5, s16[3,528,512]{2,1,0:T(8,128)(2,1)} %pad_add_fusion.2.code_ref.scale_ref, ...), custom_call_target="tpu_custom_call", output_to_operand_aliasing={{0}: (8, {})} | custom-call | flops 9663676416 | bytes 25165824 | tf_op jit(solution)/shard_map/update_rows/pallas_call | solution.py:745
  296.6 14.0 %touch_tiles.2.base_ref = f32[4096,2048]{1,0:T(8,128)} custom-call(s32[128]{0:T(128)} %get-tuple-element.160.key_ref, f32[4096,2048]{1,0:T(8,128)} %get-tuple-element.73.base_ref, bf16[32,528,128]{2,1,0:T(8,128)(2,1)} %gate.3.arrived_ref), custom_call_target="tpu_custom_call", output_to_operand_aliasing={{}: (1, {})} | custom-call | tf_op jit(solution)/shard_map/touch_tiles/pallas_call | solution.py:497
  310.6 11.7 %all-to-all-done.2.arrived_ref = bf16[16,1552,128]{2,1,0:T(8,128)(2,1)} async-done(((bf16[16,1552,128]{2,1,0:T(8,128)(2,1)}), bf16[16,1552,128]{2,1,0:T(8,128)(2,1)}, u32[]{:S(2)}, u32[]{:S(2)}) %all-to-all-start.2) | async-done | bytes 6357024 | tf_op jit(solution)/shard_map/all_to_all | solution.py:903
  322.3 1.4 fusion.18
  324.2 2.1 collective-permute-start.39
  326.3 0.8 slice_convert_fusion.2
  327.1 0.6 add.150.key_ref
  327.8 13.3 %touch_tiles.3 = f32[4096,2048]{1,0:T(8,128)} custom-call(s32[192]{0:T(256)} %add.150.key_ref, f32[4096,2048]{1,0:T(8,128)} %touch_tiles.2.base_ref, bf16[16,1552,128]{2,1,0:T(8,128)(2,1)} %all-to-all-done.2.arrived_ref), custom_call_target="tpu_custom_call", output_to_operand_aliasing={{}: (1, {})} | custom-call | tf_op jit(solution)/shard_map/touch_tiles/pallas_call | solution.py:497
  341.1 1.1 maximum_reduce_fusion
  (64 shorter events, 3.6 us)
Async XLA Ops:
  13.8 123.7 %all-to-all-start.1 = ((bf16[32,528,128]{2,1,0:T(8,128)(2,1)}), bf16[32,528,128]{2,1,0:T(8,128)(2,1)}, u32[]{:S(2)}, u32[]{:S(2)}) async-start(bf16[32,528,128]{2,1,0:T(8,128)(2,1)} %get-tuple-element.68), calls=%async_computation.1 | async-start | bytes 8650752 | tf_op jit(solution)/shard_map/all_to_all | solution.py:903
  33.5 74.2 %collective-permute-start.18 = (s16[4,528,512]{2,1,0:T(8,128)(2,1)}, s16[4,528,512]{2,1,0:T(8,128)(2,1)S(1)}, u32[]{:S(2)}, u32[]{:S(2)}) collective-permute-start(s16[4,528,512]{2,1,0:T(8,128)(2,1)} %pad_add_fusion.1), channel_id=1, source_target_pairs={{0,1},{8,9},{16,17},{24,25}} | collective-permute-start | bytes 6488072 | tf_op jit(solution)/shard_map/ppermute | solution.py:826
  40.3 70.2 %collective-permute-start.25 = (f32[128,2048]{1,0:T(8,128)}, f32[128,2048]{1,0:T(8,128)S(1)}, u32[]{:S(2)}, u32[]{:S(2)}) collective-permute-start(f32[128,2048]{1,0:T(8,128)} %get-tuple-element.145), channel_id=1, source_target_pairs={{0,24},{1,25},{2,26},{3,27},{4,28},{5,29},{6,30},{7,31}} | collective-permute-start | bytes 3145736 | tf_op jit(solution)/shard_map/ppermute | solution.py:855
  41.6 69.6 %collective-permute-start.26 = (f32[128,2048]{1,0:T(8,128)}, f32[128,2048]{1,0:T(8,128)}, u32[]{:S(2)}, u32[]{:S(2)}) collective-permute-start(f32[128,2048]{1,0:T(8,128)} %get-tuple-element.144), channel_id=1, source_target_pairs={{0,16},{1,17},{2,18},{3,19},{4,20},{5,21},{6,22},{7,23}} | collective-permute-start | bytes 3145736 | tf_op jit(solution)/shard_map/ppermute | solution.py:855
  43.3 68.6 %collective-permute-start.27 = (f32[128,2048]{1,0:T(8,128)}, f32[128,2048]{1,0:T(8,128)}, u32[]{:S(2)}, u32[]{:S(2)}) collective-permute-start(f32[128,2048]{1,0:T(8,128)} %get-tuple-element.143), channel_id=1, source_target_pairs={{0,8},{1,9},{2,10},{3,11},{4,12},{5,13},{6,14},{7,15}} | collective-permute-start | bytes 3145736 | tf_op jit(solution)/shard_map/ppermute | solution.py:855
  45.0 64.2 %collective-permute-start.19 = (s16[528,512]{1,0:T(8,128)(2,1)}, s16[528,512]{1,0:T(8,128)(2,1)}, u32[]{:S(2)}, u32[]{:S(2)}) collective-permute-start(s16[528,512]{1,0:T(8,128)(2,1)} %get-tuple-element.146), channel_id=1, source_target_pairs={{0,2},{8,10},{16,18},{24,26}} | collective-permute-start | bytes 1622024 | tf_op jit(solution)/shard_map/ppermute | solution.py:829
  107.7 7.5 %copy-start.11 = (s16[4,528,512]{2,1,0:T(8,128)(2,1)}, s16[4,528,512]{2,1,0:T(8,128)(2,1)S(1)}, u32[]{:S(2)}) copy-start(s16[4,528,512]{2,1,0:T(8,128)(2,1)S(1)} %collective-permute-done.18) | copy-start | bytes 6488068
  107.8 12.4 %collective-permute-start.20 = (s16[528,512]{1,0:T(8,128)(2,1)}, s16[528,512]{1,0:T(8,128)(2,1)S(1)}, u32[]{:S(2)}, u32[]{:S(2)}) collective-permute-start(s16[528,512]{1,0:T(8,128)(2,1)} %get-tuple-element.148), channel_id=1, source_target_pairs={{0,4},{8,12},{16,20},{24,28}} | collective-permute-start | bytes 1622024 | tf_op jit(solution)/shard_map/ppermute | solution.py:829
  109.2 22.7 %collective-permute-start.21 = (s16[528,512]{1,0:T(8,128)(2,1)}, s16[528,512]{1,0:T(8,128)(2,1)S(1)}, u32[]{:S(2)}, u32[]{:S(2)}) collective-permute-start(s16[528,512]{1,0:T(8,128)(2,1)} %get-tuple-element.147), channel_id=1, source_target_pairs={{0,6},{8,14},{16,22},{24,30}} | collective-permute-start | bytes 1622024 | tf_op jit(solution)/shard_map/ppermute | solution.py:829
  110.5 21.4 %collective-permute-start.22 = (s16[528,512]{1,0:T(8,128)(2,1)S(1)}, s16[528,512]{1,0:T(8,128)(2,1)S(1)}, u32[]{:S(2)}, u32[]{:S(2)}) collective-permute-start(s16[528,512]{1,0:T(8,128)(2,1)S(1)} %get-tuple-element.153), channel_id=1, source_target_pairs={{1,3},{9,11},{17,19},{25,27}} | collective-permute-start | bytes 1622024 | tf_op jit(solution)/shard_map/ppermute | solution.py:830
  111.2 20.6 %collective-permute-start.23 = (s16[528,512]{1,0:T(8,128)(2,1)S(1)}, s16[528,512]{1,0:T(8,128)(2,1)S(1)}, u32[]{:S(2)}, u32[]{:S(2)}) collective-permute-start(s16[528,512]{1,0:T(8,128)(2,1)S(1)} %get-tuple-element.155), channel_id=1, source_target_pairs={{1,5},{9,13},{17,21},{25,29}} | collective-permute-start | bytes 1622024 | tf_op jit(solution)/shard_map/ppermute | solution.py:830
  111.9 19.9 %collective-permute-start.24 = (s16[528,512]{1,0:T(8,128)(2,1)S(1)}, s16[528,512]{1,0:T(8,128)(2,1)S(1)}, u32[]{:S(2)}, u32[]{:S(2)}) collective-permute-start(s16[528,512]{1,0:T(8,128)(2,1)S(1)} %get-tuple-element.154), channel_id=1, source_target_pairs={{1,7},{9,15},{17,23},{25,31}} | collective-permute-start | bytes 1622024 | tf_op jit(solution)/shard_map/ppermute | solution.py:830
  120.3 58.5 %collective-permute-start.17 = (bf16[3600,128]{1,0:T(8,128)(2,1)}, bf16[3600,128]{1,0:T(8,128)(2,1)S(1)}, u32[]{:S(2)}, u32[]{:S(2)}) collective-permute-start(bf16[3600,128]{1,0:T(8,128)(2,1)} %get-tuple-element.65), channel_id=1, source_target_pairs={{0,4},{1,5},{2,6},{3,7},{4,0},{5,1},{6,2},{7,3},{8,12},{9,13},{10,... | collective-permute-start | bytes 2764808 | tf_op jit(solution)/shard_map/ppermute | solution.py:921
  145.4 25.2 %copy-start.13 = (s16[528,512]{1,0:T(8,128)(2,1)S(1)}, s16[528,512]{1,0:T(8,128)(2,1)}, u32[]{:S(2)}) copy-start(s16[528,512]{1,0:T(8,128)(2,1)} %extend_slice.1) | copy-start | bytes 1622020
  145.4 32.5 %collective-permute-start.31 = (s16[528,512]{1,0:T(8,128)(2,1)}, s16[528,512]{1,0:T(8,128)(2,1)S(1)}, u32[]{:S(2)}, u32[]{:S(2)}) collective-permute-start(s16[528,512]{1,0:T(8,128)(2,1)} %extend_slice.1), channel_id=1, source_target_pairs={{0,2},{2,4},{4,6},{6,7},{7,5},{5,3},{3,1},{1,0},{8,10},{10,12},{12... | collective-permute-start | bytes 1622024 | tf_op jit(solution)/shard_map/ppermute | solution.py:812
  170.5 58.7 %copy-start.1 = (f32[512,512]{1,0:T(8,128)S(1)}, f32[512,512]{1,0:T(8,128)}, u32[]{:S(2)}) copy-start(f32[512,512]{1,0:T(8,128)} %pivot_ref.1) | copy-start | bytes 3145732
  170.5 37.1 %collective-permute-start.28 = (f32[128,2048]{1,0:T(8,128)}, f32[128,2048]{1,0:T(8,128)}, u32[]{:S(2)}, u32[]{:S(2)}) collective-permute-start(f32[128,2048]{1,0:T(8,128)} %extend_add.3.refs_0_), channel_id=1, source_target_pairs={{0,16},{8,24},{16,0},{24,8},{1,17},{9,25},{17,1},{25,9},{2,18},{10... | collective-permute-start | bytes 3145736 | tf_op jit(solution)/shard_map/ppermute | solution.py:866
  171.4 20.2 %collective-permute-start.34 = (s16[528,512]{1,0:T(8,128)(2,1)S(1)}, s16[528,512]{1,0:T(8,128)(2,1)}, u32[]{:S(2)}, u32[]{:S(2)}) collective-permute-start(s16[528,512]{1,0:T(8,128)(2,1)S(1)} %copy-done.13), channel_id=1, source_target_pairs={{2,0},{4,2},{6,4},{7,6},{5,7},{3,5},{1,3},{0,1},{10,8},{12,10},{14... | collective-permute-start | bytes 1622024 | tf_op jit(solution)/shard_map/ppermute | solution.py:812
  177.9 1.0 copy-start.12
  178.9 0.9 copy-start.4
  179.8 23.3 %collective-permute-start.32 = (s16[528,512]{1,0:T(8,128)(2,1)}, s16[528,512]{1,0:T(8,128)(2,1)}, u32[]{:S(2)}, u32[]{:S(2)}) collective-permute-start(s16[528,512]{1,0:T(8,128)(2,1)} %gate.4), channel_id=1, source_target_pairs={{0,2},{2,4},{4,6},{6,7},{7,5},{5,3},{3,1},{1,0},{8,10},{10,12},{12... | collective-permute-start | bytes 1622024 | tf_op jit(solution)/shard_map/ppermute | solution.py:812
  191.6 16.1 %collective-permute-start.35 = (s16[528,512]{1,0:T(8,128)(2,1)}, s16[528,512]{1,0:T(8,128)(2,1)S(1)}, u32[]{:S(2)}, u32[]{:S(2)}) collective-permute-start(s16[528,512]{1,0:T(8,128)(2,1)} %collective-permute-done.34), channel_id=1, source_target_pairs={{2,0},{4,2},{6,4},{7,6},{5,7},{3,5},{1,3},{0,1},{10,8},{12,10},{14... | collective-permute-start | bytes 1622024 | tf_op jit(solution)/shard_map/ppermute | solution.py:812
  203.2 12.8 %collective-permute-start.33 = (s16[528,512]{1,0:T(8,128)(2,1)}, s16[528,512]{1,0:T(8,128)(2,1)S(1)}, u32[]{:S(2)}, u32[]{:S(2)}) collective-permute-start(s16[528,512]{1,0:T(8,128)(2,1)} %collective-permute-done.32), channel_id=1, source_target_pairs={{0,2},{2,4},{4,6},{6,7},{7,5},{5,3},{3,1},{1,0},{8,10},{10,12},{12... | collective-permute-start | bytes 1622024 | tf_op jit(solution)/shard_map/ppermute | solution.py:812
  206.0 23.2 %collective-permute-start.29 = (f32[128,2048]{1,0:T(8,128)}, f32[128,2048]{1,0:T(8,128)}, u32[]{:S(2)}, u32[]{:S(2)}) collective-permute-start(f32[128,2048]{1,0:T(8,128)} %extend_add.3.refs_0_), channel_id=1, source_target_pairs={{0,8},{8,0},{16,24},{24,16},{1,9},{9,1},{17,25},{25,17},{2,10},{10... | collective-permute-start | bytes 3145736 | tf_op jit(solution)/shard_map/ppermute | solution.py:866
  207.6 21.6 %collective-permute-start.30 = (f32[128,2048]{1,0:T(8,128)}, f32[128,2048]{1,0:T(8,128)}, u32[]{:S(2)}, u32[]{:S(2)}) collective-permute-start(f32[128,2048]{1,0:T(8,128)} %collective-permute-done.28.refs_1_), channel_id=1, source_target_pairs={{0,8},{8,0},{16,24},{24,16},{1,9},{9,1},{17,25},{25,17},{2,10},{10... | collective-permute-start | bytes 3145736 | tf_op jit(solution)/shard_map/ppermute | solution.py:866
  207.8 14.4 %collective-permute-start.36 = (s16[528,512]{1,0:T(8,128)(2,1)S(1)}, s16[528,512]{1,0:T(8,128)(2,1)S(1)}, u32[]{:S(2)}, u32[]{:S(2)}) collective-permute-start(s16[528,512]{1,0:T(8,128)(2,1)S(1)} %collective-permute-done.35), channel_id=1, source_target_pairs={{2,0},{4,2},{6,4},{7,6},{5,7},{3,5},{1,3},{0,1},{10,8},{12,10},{14... | collective-permute-start | bytes 1622024 | tf_op jit(solution)/shard_map/ppermute | solution.py:812
  216.0 21.9 %copy-start.5 = (s16[528,512]{1,0:T(8,128)(2,1)}, s16[528,512]{1,0:T(8,128)(2,1)S(1)}, u32[]{:S(2)}) copy-start(s16[528,512]{1,0:T(8,128)(2,1)S(1)} %collective-permute-done.33.refs_2_) | copy-start | bytes 1622020
  216.0 13.2 %collective-permute-start.37 = (s16[264,512]{1,0:T(8,128)(2,1)S(1)}, s16[264,512]{1,0:T(8,128)(2,1)S(1)}, u32[]{:S(2)}, u32[]{:S(2)}) collective-permute-start(s16[264,512]{1,0:T(8,128)(2,1)S(1)} %slice.266), channel_id=1, source_target_pairs={{0,2},{2,4},{4,6},{6,7},{7,5},{5,3},{3,1},{1,0},{8,10},{10,12},{12... | collective-permute-start | bytes 811016 | tf_op jit(solution)/shard_map/ppermute | solution.py:818
  222.1 15.8 %copy-start.7 = (s16[528,512]{1,0:T(8,128)(2,1)}, s16[528,512]{1,0:T(8,128)(2,1)S(1)}, u32[]{:S(2)}) copy-start(s16[528,512]{1,0:T(8,128)(2,1)S(1)} %collective-permute-done.36.refs_3_) | copy-start | bytes 1622020
  222.1 7.1 %collective-permute-start.38 = (s16[264,512]{1,0:T(8,128)(2,1)S(1)}, s16[264,512]{1,0:T(8,128)(2,1)S(1)}, u32[]{:S(2)}, u32[]{:S(2)}) collective-permute-start(s16[264,512]{1,0:T(8,128)(2,1)S(1)} %slice.267), channel_id=1, source_target_pairs={{2,0},{4,2},{6,4},{7,6},{5,7},{3,5},{1,3},{0,1},{10,8},{12,10},{14... | collective-permute-start | bytes 811016 | tf_op jit(solution)/shard_map/ppermute | solution.py:818
  229.2 8.7 %copy-start.9 = (s16[528,512]{1,0:T(8,128)(2,1)}, s16[528,512]{1,0:T(8,128)(2,1)S(1)}, u32[]{:S(2)}) copy-start(s16[528,512]{1,0:T(8,128)(2,1)S(1)} %constant_dynamic-update-slice_fusion.refs_4_) | copy-start | bytes 1622020
  237.9 12.9 %copy-start.6 = (s16[528,512]{1,0:T(8,128)(2,1)S(1)}, s16[528,512]{1,0:T(8,128)(2,1)}, u32[]{:S(2)}) copy-start(s16[528,512]{1,0:T(8,128)(2,1)} %copy-done.5) | copy-start | bytes 1622020
  237.9 12.9 %copy-start.8 = (s16[528,512]{1,0:T(8,128)(2,1)S(1)}, s16[528,512]{1,0:T(8,128)(2,1)}, u32[]{:S(2)}) copy-start(s16[528,512]{1,0:T(8,128)(2,1)} %copy-done.7) | copy-start | bytes 1622020
  237.9 12.9 %copy-start.10 = (s16[528,512]{1,0:T(8,128)(2,1)S(1)}, s16[528,512]{1,0:T(8,128)(2,1)}, u32[]{:S(2)}) copy-start(s16[528,512]{1,0:T(8,128)(2,1)} %copy-done.9) | copy-start | bytes 1622020
  237.9 84.3 %all-to-all-start.2 = ((bf16[16,1552,128]{2,1,0:T(8,128)(2,1)}), bf16[16,1552,128]{2,1,0:T(8,128)(2,1)}, u32[]{:S(2)}, u32[]{:S(2)}) async-start(bf16[16,1552,128]{2,1,0:T(8,128)(2,1)} %gate.5), calls=%async_computation.2 | async-start | bytes 12713984 | tf_op jit(solution)/shard_map/all_to_all | solution.py:903
  324.2 16.9 %collective-permute-start.39 = (s32[8,128]{1,0:T(8,128)S(1)}, s32[8,128]{1,0:T(8,128)S(1)}, u32[]{:S(2)}, u32[]{:S(2)}) collective-permute-start(s32[8,128]{1,0:T(8,128)S(1)} %broadcast_in_dim.19), channel_id=1, source_target_pairs={{0,4},{1,5},{2,6},{3,7},{4,0},{5,1},{6,2},{7,3},{8,12},{9,13},{10,... | collective-permute-start | bytes 12296 | tf_op jit(solution)/shard_map/ppermute | solution.py:931
  327.8 14.5 %copy-start.19 = (s32[128]{0:T(128)S(1)}, s32[128]{0:T(128)}, u32[]{:S(2)}) copy-start(s32[128]{0:T(128)} %param.12) | copy-start | bytes 1540
  327.8 14.5 %copy-start.20 = (s32[128,1]{0,1:T(1,128)S(1)}, s32[128,1]{0,1:T(1,128)}, u32[]{:S(2)}) copy-start(s32[128,1]{0,1:T(1,128)} %param.11) | copy-start | bytes 1540

commit v5 on v4

--- a/solution.py
+++ b/solution.py
@@ -808,12 +808,12 @@
     left = right = own
     for step in range(1, count // 2):
         if step in before:
-            left = gate(left, before[step])
+            left = gate(left, *before[step])
         left, right = lax.ppermute(left, axis, ahead), lax.ppermute(right, axis, back)
         pieces += [left, right]
     half = own.shape[0] // 2
     if count // 2 in before:
-        left = gate(left, before[count // 2])
+        left = gate(left, *before[count // 2])
     pieces.append(
         jnp.concatenate([lax.ppermute(left[:half], axis, ahead), lax.ppermute(right[half:], axis, back)], 0)
     )
@@ -919,10 +919,10 @@
     uppers, ids = gather_pieces(pivots, "bulk")
     high, low, upper = right_factor(flags, ids, pivot_inverse, uppers)
     far = lax.ppermute(far, "col", swap)
-    pieces, whose = ring_gather(code, "col", {2: far})
+    late = distribute([near, far], over, groups, plan["late"])
+    pieces, whose = ring_gather(code, "col", {2: [far], column_count // 2 - 1: [late]})
     cut = len(pieces) - 3
-    late = distribute([near, far], over, groups, plan["late"])
-    late = exchange(gate(late, high, *pieces[-3:]), halves)
+    late = exchange(gate(late, *pieces[-3:], *uppers[1:]), halves)
     result, _ = update_rows(flags, whose[:cut], parent, jnp.stack(pieces[:cut]), high, low, upper)
     result, _ = update_rows(flags, whose[cut:], parent, jnp.stack(pieces[cut:]), high, low, upper, into=result)
     result = touch_tiles(result, early, plain_key, width, share)

time: 346 us -> 345 us (level)
  the two profiles are of different devices: /device:TPU:5 before, /device:TPU:0 now
where the time goes in v5:
time: 345 us; the launch traced here: 341 us
  waiting for transfers between devices  115 us (33%)
  Pallas kernels  114 us (33%)
  starting transfers between devices  72.7 us (21%)
  local copies, waits for them, and re-layouts  19.9 us (6%)
  other arithmetic  18.8 us (5%)
    ppermute x1, waiting for transfers between devices, scatter_first(): lax.ppermute(jnp.concatenate([parts[k:k + 1] for k in range(1, count, 2)]...  58.2 us
    pallas_call x2, Pallas kernels, update_rows(): pl.pallas_call(functools.partial(update_kernel, block, per_slice), out_sh...  43.1 us
    ppermute x3, starting transfers between devices, ring_gather(): lax.ppermute(left, axis, ahead)  34.9 us
    pallas_call x2, Pallas kernels, touch_tiles(): pl.pallas_call(functools.partial(touch_kernel, width, capacity), out_shap...  26 us
    ppermute x3, waiting for transfers between devices, scatter_first(): sent = [lax.ppermute(parts[k], axis, [(0, k)]) for k in range(2, count, 2)]  18.5 us
    ppermute x3, waiting for transfers between devices, ring_gather(): lax.ppermute(right, axis, back)  12.6 us
    all_to_all x2, starting transfers between devices, exchange(): lax.all_to_all(blocks, ('bulk', 'col'), split_axis=0, concat_axis=0, axis...  12.2 us
    pallas_call x1, Pallas kernels, sort_children(): pl.pallas_call(functools.partial(sort_kernel, plan), out_shape=[jax.Shape...  11.4 us
  transfers between devices with their start and end apart: 25, of which 11 were waited for; matrix products, arithmetic and copies ran while one was open for 9% of the time, Pallas kernels for 30%

profile of v5, /device:TPU:0, one launch (start us, length us, event | category | flops | bytes accessed | tf_op | source)
XLA Modules:
  0.0 341.3 jit_solution(16660618103359716824)
XLA Ops:
  0.0 1.3 add_select_fusion
  2.4 11.4 %sort_children.1 = (bf16[32,528,128]{2,1,0:T(8,128)(2,1)}, bf16[3600,128]{1,0:T(8,128)(2,1)}, bf16[3600,128]{1,0:T(8,128)(2,1)}, s32[1]{0:T(128)}) custom-call(s32[128]{0:T(128)} %or_select_fusion.kind_ref, s32[128]{0:T(128)} %get-tuple-element.131.dest_ref, s32[128]{0:T(128)} %get-tuple-element.126.code_ref, bf16[128,128,128]{2,1,0:T(8,128)(2,1)} %child_ref.1), custom_call_target="tpu_custom_call" | custom-call | bytes 4096 | tf_op jit(solution)/shard_map/sort_children/pallas_call | solution.py:228
  13.8 7.4 %all-to-all-start.1 = ((bf16[32,528,128]{2,1,0:T(8,128)(2,1)}), bf16[32,528,128]{2,1,0:T(8,128)(2,1)}, u32[]{:S(2)}, u32[]{:S(2)}) async-start(bf16[32,528,128]{2,1,0:T(8,128)(2,1)} %get-tuple-element.68), calls=%async_computation.1 | async-start | bytes 8650752 | tf_op jit(solution)/shard_map/all_to_all | solution.py:903
  21.2 8.4 %encode_panel.1 = s16[8,528,512]{2,1,0:T(8,128)(2,1)} custom-call(f32[4096,2048]{1,0:T(8,128)} %base_ref.5), custom_call_target="tpu_custom_call" | custom-call | bytes 4096 | tf_op jit(solution)/shard_map/encode_panel/pallas_call | solution.py:555
  29.6 3.3 slice_bitcast_fusion.11
  32.9 1.5 pad_add_fusion.1
  34.4 3.7 %collective-permute-start.18 = (s16[4,528,512]{2,1,0:T(8,128)(2,1)}, s16[4,528,512]{2,1,0:T(8,128)(2,1)S(1)}, u32[]{:S(2)}, u32[]{:S(2)}) collective-permute-start(s16[4,528,512]{2,1,0:T(8,128)(2,1)} %pad_add_fusion.1), channel_id=1, source_target_pairs={{0,1},{8,9},{16,17},{24,25}} | collective-permute-start | bytes 6488072 | tf_op jit(solution)/shard_map/ppermute | solution.py:826
  38.2 3.6 %fusion.26 = (f32[128,2048]{1,0:T(8,128)}, f32[128,2048]{1,0:T(8,128)}, f32[128,2048]{1,0:T(8,128)}) fusion(f32[4096,2048]{1,0:T(8,128)} %base_ref.5), kind=kLoop, calls=%fused_computation.122 | loop fusion | bytes 6291456 | tf_op jit(solution)/shard_map/slice | solution.py:855
  41.8 2.8 collective-permute-start.27
  44.5 3.3 collective-permute-start.26
  47.8 2.3 collective-permute-start.25
  50.2 1.3 collective-permute-start.19
  51.5 58.2 %collective-permute-done.18 = s16[4,528,512]{2,1,0:T(8,128)(2,1)S(1)} collective-permute-done((s16[4,528,512]{2,1,0:T(8,128)(2,1)}, s16[4,528,512]{2,1,0:T(8,128)(2,1)S(1)}, u32[]{:S(2)}, u32[]{:S(2)}) %collective-permute-start.18) | collective-permute-done | bytes 2162720 | tf_op jit(solution)/shard_map/ppermute | solution.py:826
  109.8 1.3 collective-permute-start.21
  111.1 1.3 collective-permute-start.20
  112.5 0.7 collective-permute-start.22
  113.2 0.7 collective-permute-start.24
  113.9 0.7 collective-permute-start.23
  114.6 2.6 select_select_fusion.refs_2_.base_ref
  117.2 6.9 %collective-permute-done.21 = s16[528,512]{1,0:T(8,128)(2,1)S(1)} collective-permute-done((s16[528,512]{1,0:T(8,128)(2,1)}, s16[528,512]{1,0:T(8,128)(2,1)S(1)}, u32[]{:S(2)}, u32[]{:S(2)}) %collective-permute-start.21) | collective-permute-done | bytes 540704 | tf_op jit(solution)/shard_map/ppermute | solution.py:829
  124.1 11.6 %collective-permute-done.20 = s16[528,512]{1,0:T(8,128)(2,1)S(1)} collective-permute-done((s16[528,512]{1,0:T(8,128)(2,1)}, s16[528,512]{1,0:T(8,128)(2,1)S(1)}, u32[]{:S(2)}, u32[]{:S(2)}) %collective-permute-start.20) | collective-permute-done | bytes 540704 | tf_op jit(solution)/shard_map/ppermute | solution.py:829
  135.7 2.6 fusion.15.refs_1_.code_ref
  138.3 0.7 all-to-all-done.1.refs_0_
  138.9 0.9 slice_convert_fusion.1
  140.5 6.1 %extend_slice.1 = s16[528,512]{1,0:T(8,128)(2,1)} custom-call(s32[128]{0:T(128)} %get-tuple-element.162.key_ref, s16[528,512]{1,0:T(8,128)(2,1)} %fusion.15.refs_1_.code_ref, bf16[32,528,128]{2,1,0:T(8,128)(2,1)} %gate.4.arrived_ref), custom_call_target="tpu_custom_call" | custom-call | bytes 4096 | tf_op jit(solution)/shard_map/extend_slice/pallas_call | solution.py:582
  146.6 21.0 %collective-permute-start.28 = (s16[528,512]{1,0:T(8,128)(2,1)}, s16[528,512]{1,0:T(8,128)(2,1)S(1)}, u32[]{:S(2)}, u32[]{:S(2)}) collective-permute-start(s16[528,512]{1,0:T(8,128)(2,1)} %extend_slice.1), channel_id=1, source_target_pairs={{0,2},{2,4},{4,6},{6,7},{7,5},{5,3},{3,1},{1,0},{8,10},{10,12},{12... | collective-permute-start | bytes 1622024 | tf_op jit(solution)/shard_map/ppermute | solution.py:812
  167.6 0.7 slice_convert_fusion.5
  168.9 4.4 %extend_add.3.refs_0_ = f32[128,2048]{1,0:T(8,128)} custom-call(s32[128]{0:T(128)} %get-tuple-element.161.key_ref, f32[128,2048]{1,0:T(8,128)} %select_select_fusion.refs_2_.base_ref, bf16[32,528,128]{2,1,0:T(8,128)(2,1)} %gate.4.arrived_ref), custom_call_target="tpu_custom_call" | custom-call | flops 262144 | bytes 3145728 | tf_op jit(solution)/shard_map/extend_add/pallas_call | solution.py:395
  173.3 1.4 collective-permute-start.36
  174.7 0.8 bitcast_dynamic-update-slice_fusion.11
  175.5 3.9 %collective-permute-done.28.refs_0_ = s16[528,512]{1,0:T(8,128)(2,1)S(1)} collective-permute-done((s16[528,512]{1,0:T(8,128)(2,1)}, s16[528,512]{1,0:T(8,128)(2,1)S(1)}, u32[]{:S(2)}, u32[]{:S(2)}) %collective-permute-start.28) | collective-permute-done | bytes 540704 | tf_op jit(solution)/shard_map/ppermute | solution.py:812
  179.4 0.9 bitcast_dynamic-update-slice_fusion.10
  180.4 0.9 copy-done.7
  181.3 11.6 %collective-permute-start.29 = (s16[528,512]{1,0:T(8,128)(2,1)}, s16[528,512]{1,0:T(8,128)(2,1)S(1)}, u32[]{:S(2)}, u32[]{:S(2)}) collective-permute-start(s16[528,512]{1,0:T(8,128)(2,1)} %gate.5), channel_id=1, source_target_pairs={{0,2},{2,4},{4,6},{6,7},{7,5},{5,3},{3,1},{1,0},{8,10},{10,12},{12... | collective-permute-start | bytes 1622024 | tf_op jit(solution)/shard_map/ppermute | solution.py:812
  192.9 0.7 slice_convert_fusion.4
  194.1 5.9 %distribute.1 = (bf16[16,1552,128]{2,1,0:T(8,128)(2,1)}, s32[1]{0:T(128)}) custom-call(s32[28]{0:T(128)} %get-tuple-element.159.refs_0_, s32[28]{0:T(128)} %get-tuple-element.157.refs_1_, s32[28]{0:T(128)} %get-tuple-element.158.refs_2_, s32[28]{0:T(128)} %get-tuple-element.156.refs_3_, bf16[3600,128]{1,0:T(8,128)(2,1)} %get-tuple-element.64.refs_4_, ...), custom_call_target="tpu_custom_call" | custom-call | bytes 4096 | tf_op jit(solution)/shard_map/distribute/pallas_call | solution.py:313
  200.1 1.9 bitcast_dynamic-update-slice_fusion.9
  202.0 2.9 collective-permute-done.29.refs_0_
  205.0 0.9 bitcast_dynamic-update-slice_fusion.8
  205.9 2.4 collective-permute-start.30
  208.8 6.2 %collective-permute-done.32 = s16[528,512]{1,0:T(8,128)(2,1)} collective-permute-done((s16[528,512]{1,0:T(8,128)(2,1)}, s16[528,512]{1,0:T(8,128)(2,1)}, u32[]{:S(2)}, u32[]{:S(2)}) %collective-permute-start.32) | collective-permute-done | bytes 540704 | tf_op jit(solution)/shard_map/ppermute | solution.py:812
  215.1 4.5 %collective-permute-done.30.refs_1_ = s16[528,512]{1,0:T(8,128)(2,1)S(1)} collective-permute-done((s16[528,512]{1,0:T(8,128)(2,1)}, s16[528,512]{1,0:T(8,128)(2,1)S(1)}, u32[]{:S(2)}, u32[]{:S(2)}) %collective-permute-start.30) | collective-permute-done | bytes 540704 | tf_op jit(solution)/shard_map/ppermute | solution.py:812
  219.6 2.5 collective-permute-start.34
  222.1 6.4 %collective-permute-done.33.refs_2_ = s16[528,512]{1,0:T(8,128)(2,1)S(1)} collective-permute-done((s16[528,512]{1,0:T(8,128)(2,1)}, s16[528,512]{1,0:T(8,128)(2,1)S(1)}, u32[]{:S(2)}, u32[]{:S(2)}) %collective-permute-start.33) | collective-permute-done | bytes 540704 | tf_op jit(solution)/shard_map/ppermute | solution.py:812
  228.9 6.2 %collective-permute-done.35 = s16[264,512]{1,0:T(8,128)(2,1)S(1)} collective-permute-done((s16[264,512]{1,0:T(8,128)(2,1)S(1)}, s16[264,512]{1,0:T(8,128)(2,1)S(1)}, u32[]{:S(2)}, u32[]{:S(2)}) %collective-permute-start.35) | collective-permute-done | bytes 270368 | tf_op jit(solution)/shard_map/ppermute | solution.py:818
  235.2 0.8 copy-done.12
  236.0 1.0 copy-done.6
  237.0 4.8 %all-to-all-start.2 = ((bf16[16,1552,128]{2,1,0:T(8,128)(2,1)}), bf16[16,1552,128]{2,1,0:T(8,128)(2,1)}, u32[]{:S(2)}, u32[]{:S(2)}) async-start(bf16[16,1552,128]{2,1,0:T(8,128)(2,1)} %gate.7), calls=%async_computation.2 | async-start | bytes 12713984 | tf_op jit(solution)/shard_map/all_to_all | solution.py:903
  241.9 0.8 constant_dynamic-slice_fusion
  242.7 0.7 pad_add_fusion.4.id_ref
  244.5 1.9 bitcast_dynamic-update-slice_fusion.7.code_ref.scale_ref
  246.5 1.3 pad_add_fusion.2.code_ref.scale_ref
  247.8 8.6 %right_factor.2 = (bf16[512,2048]{1,0:T(8,128)(2,1)}, bf16[512,2048]{1,0:T(8,128)(2,1)}, f32[512,2048]{1,0:T(8,128)}) custom-call(s32[2]{0:T(128)S(1)} %pad_add_fusion.3.flag_ref, s32[4]{0:T(128)} %pad_add_fusion.4.id_ref, f32[512,512]{1,0:T(8,128)S(1)} %copy-done.1, f32[128,2048]{1,0:T(8,128)} %extend_add.3.refs_0_, f32[128,2048]{1,0:T(8,128)} %copy-done.5, ...), custom_call_target="tpu_custom_call" | custom-call | bytes 4096 | tf_op jit(solution)/shard_map/right_factor/pallas_call | solution.py:672
  256.4 25.1 %update_rows.3 = (f32[4096,2048]{1,0:T(8,128)}, f32[8,128]{1,0:T(8,128)}) custom-call(s32[2]{0:T(128)S(1)} %pad_add_fusion.3.flag_ref, s32[5]{0:T(128)} %slice_bitcast_fusion.12.slice_ref, f32[4096,2048]{1,0:T(8,128)} %base_ref.5, s16[5,528,512]{2,1,0:T(8,128)(2,1)} %bitcast_dynamic-update-slice_fusion.7.code_ref.scale_ref, ...), custom_call_target="tpu_custom_call" | custom-call | flops 16106127360 | bytes 41943040 | tf_op jit(solution)/shard_map/update_rows/pallas_call | solution.py:745
  281.5 18.0 %update_rows.4 = (f32[4096,2048]{1,0:T(8,128)}, f32[8,128]{1,0:T(8,128)}) custom-call(s32[2]{0:T(128)S(1)} %pad_add_fusion.3.flag_ref, s32[3]{0:T(128)} %slice_bitcast_fusion.13.slice_ref, f32[4096,2048]{1,0:T(8,128)} %base_ref.5, s16[3,528,512]{2,1,0:T(8,128)(2,1)} %pad_add_fusion.2.code_ref.scale_ref, ...), custom_call_target="tpu_custom_call", output_to_operand_aliasing={{0}: (8, {})} | custom-call | flops 9663676416 | bytes 25165824 | tf_op jit(solution)/shard_map/update_rows/pallas_call | solution.py:745
  299.5 13.8 %touch_tiles.2.base_ref = f32[4096,2048]{1,0:T(8,128)} custom-call(s32[128]{0:T(128)} %get-tuple-element.160.key_ref, f32[4096,2048]{1,0:T(8,128)} %get-tuple-element.73.base_ref, bf16[32,528,128]{2,1,0:T(8,128)(2,1)} %gate.4.arrived_ref), custom_call_target="tpu_custom_call", output_to_operand_aliasing={{}: (1, {})} | custom-call | tf_op jit(solution)/shard_map/touch_tiles/pallas_call | solution.py:497
  313.3 7.3 %all-to-all-done.2.arrived_ref = bf16[16,1552,128]{2,1,0:T(8,128)(2,1)} async-done(((bf16[16,1552,128]{2,1,0:T(8,128)(2,1)}), bf16[16,1552,128]{2,1,0:T(8,128)(2,1)}, u32[]{:S(2)}, u32[]{:S(2)}) %all-to-all-start.2) | async-done | bytes 6357024 | tf_op jit(solution)/shard_map/all_to_all | solution.py:903
  320.5 1.5 fusion.18
  322.0 0.7 broadcast_in_dim.19
  322.7 2.6 collective-permute-start.39
  325.3 0.8 slice_convert_fusion.2
  326.1 0.7 add.150.key_ref
  326.8 12.3 %touch_tiles.3 = f32[4096,2048]{1,0:T(8,128)} custom-call(s32[192]{0:T(256)} %add.150.key_ref, f32[4096,2048]{1,0:T(8,128)} %touch_tiles.2.base_ref, bf16[16,1552,128]{2,1,0:T(8,128)(2,1)} %all-to-all-done.2.arrived_ref), custom_call_target="tpu_custom_call", output_to_operand_aliasing={{}: (1, {})} | custom-call | tf_op jit(solution)/shard_map/touch_tiles/pallas_call | solution.py:497
  339.1 1.4 maximum_reduce_fusion
  (77 shorter events, 6.3 us)
Async XLA Ops:
  13.8 125.2 %all-to-all-start.1 = ((bf16[32,528,128]{2,1,0:T(8,128)(2,1)}), bf16[32,528,128]{2,1,0:T(8,128)(2,1)}, u32[]{:S(2)}, u32[]{:S(2)}) async-start(bf16[32,528,128]{2,1,0:T(8,128)(2,1)} %get-tuple-element.68), calls=%async_computation.1 | async-start | bytes 8650752 | tf_op jit(solution)/shard_map/all_to_all | solution.py:903
  34.4 75.3 %collective-permute-start.18 = (s16[4,528,512]{2,1,0:T(8,128)(2,1)}, s16[4,528,512]{2,1,0:T(8,128)(2,1)S(1)}, u32[]{:S(2)}, u32[]{:S(2)}) collective-permute-start(s16[4,528,512]{2,1,0:T(8,128)(2,1)} %pad_add_fusion.1), channel_id=1, source_target_pairs={{0,1},{8,9},{16,17},{24,25}} | collective-permute-start | bytes 6488072 | tf_op jit(solution)/shard_map/ppermute | solution.py:826
  41.8 70.7 %collective-permute-start.27 = (f32[128,2048]{1,0:T(8,128)}, f32[128,2048]{1,0:T(8,128)}, u32[]{:S(2)}, u32[]{:S(2)}) collective-permute-start(f32[128,2048]{1,0:T(8,128)} %get-tuple-element.143), channel_id=1, source_target_pairs={{0,8},{1,9},{2,10},{3,11},{4,12},{5,13},{6,14},{7,15}} | collective-permute-start | bytes 3145736 | tf_op jit(solution)/shard_map/ppermute | solution.py:855
  44.5 68.7 %collective-permute-start.26 = (f32[128,2048]{1,0:T(8,128)}, f32[128,2048]{1,0:T(8,128)}, u32[]{:S(2)}, u32[]{:S(2)}) collective-permute-start(f32[128,2048]{1,0:T(8,128)} %get-tuple-element.144), channel_id=1, source_target_pairs={{0,16},{1,17},{2,18},{3,19},{4,20},{5,21},{6,22},{7,23}} | collective-permute-start | bytes 3145736 | tf_op jit(solution)/shard_map/ppermute | solution.py:855
  47.8 66.1 %collective-permute-start.25 = (f32[128,2048]{1,0:T(8,128)}, f32[128,2048]{1,0:T(8,128)}, u32[]{:S(2)}, u32[]{:S(2)}) collective-permute-start(f32[128,2048]{1,0:T(8,128)} %get-tuple-element.145), channel_id=1, source_target_pairs={{0,24},{1,25},{2,26},{3,27},{4,28},{5,29},{6,30},{7,31}} | collective-permute-start | bytes 3145736 | tf_op jit(solution)/shard_map/ppermute | solution.py:855
  50.2 60.9 %collective-permute-start.19 = (s16[528,512]{1,0:T(8,128)(2,1)}, s16[528,512]{1,0:T(8,128)(2,1)S(1)}, u32[]{:S(2)}, u32[]{:S(2)}) collective-permute-start(s16[528,512]{1,0:T(8,128)(2,1)} %get-tuple-element.146), channel_id=1, source_target_pairs={{0,2},{8,10},{16,18},{24,26}} | collective-permute-start | bytes 1622024 | tf_op jit(solution)/shard_map/ppermute | solution.py:829
  109.8 14.3 %collective-permute-start.21 = (s16[528,512]{1,0:T(8,128)(2,1)}, s16[528,512]{1,0:T(8,128)(2,1)S(1)}, u32[]{:S(2)}, u32[]{:S(2)}) collective-permute-start(s16[528,512]{1,0:T(8,128)(2,1)} %get-tuple-element.147), channel_id=1, source_target_pairs={{0,6},{8,14},{16,22},{24,30}} | collective-permute-start | bytes 1622024 | tf_op jit(solution)/shard_map/ppermute | solution.py:829
  111.1 12.9 %copy-start.19 = (s16[528,512]{1,0:T(8,128)(2,1)}, s16[528,512]{1,0:T(8,128)(2,1)S(1)}, u32[]{:S(2)}) copy-start(s16[528,512]{1,0:T(8,128)(2,1)S(1)} %collective-permute-done.19) | copy-start | bytes 1622020
  111.1 24.5 %collective-permute-start.20 = (s16[528,512]{1,0:T(8,128)(2,1)}, s16[528,512]{1,0:T(8,128)(2,1)S(1)}, u32[]{:S(2)}, u32[]{:S(2)}) collective-permute-start(s16[528,512]{1,0:T(8,128)(2,1)} %get-tuple-element.148), channel_id=1, source_target_pairs={{0,4},{8,12},{16,20},{24,28}} | collective-permute-start | bytes 1622024 | tf_op jit(solution)/shard_map/ppermute | solution.py:829
  112.5 23.2 %collective-permute-start.22 = (s16[528,512]{1,0:T(8,128)(2,1)S(1)}, s16[528,512]{1,0:T(8,128)(2,1)S(1)}, u32[]{:S(2)}, u32[]{:S(2)}) collective-permute-start(s16[528,512]{1,0:T(8,128)(2,1)S(1)} %get-tuple-element.153), channel_id=1, source_target_pairs={{1,3},{9,11},{17,19},{25,27}} | collective-permute-start | bytes 1622024 | tf_op jit(solution)/shard_map/ppermute | solution.py:830
  113.2 22.5 %collective-permute-start.24 = (s16[528,512]{1,0:T(8,128)(2,1)S(1)}, s16[528,512]{1,0:T(8,128)(2,1)S(1)}, u32[]{:S(2)}, u32[]{:S(2)}) collective-permute-start(s16[528,512]{1,0:T(8,128)(2,1)S(1)} %get-tuple-element.154), channel_id=1, source_target_pairs={{1,7},{9,15},{17,23},{25,31}} | collective-permute-start | bytes 1622024 | tf_op jit(solution)/shard_map/ppermute | solution.py:830
  113.9 21.8 %collective-permute-start.23 = (s16[528,512]{1,0:T(8,128)(2,1)S(1)}, s16[528,512]{1,0:T(8,128)(2,1)S(1)}, u32[]{:S(2)}, u32[]{:S(2)}) collective-permute-start(s16[528,512]{1,0:T(8,128)(2,1)S(1)} %get-tuple-element.155), channel_id=1, source_target_pairs={{1,5},{9,13},{17,21},{25,29}} | collective-permute-start | bytes 1622024 | tf_op jit(solution)/shard_map/ppermute | solution.py:830
  124.1 56.2 %collective-permute-start.17 = (bf16[3600,128]{1,0:T(8,128)(2,1)}, bf16[3600,128]{1,0:T(8,128)(2,1)S(1)}, u32[]{:S(2)}, u32[]{:S(2)}) collective-permute-start(bf16[3600,128]{1,0:T(8,128)(2,1)} %get-tuple-element.65), channel_id=1, source_target_pairs={{0,4},{1,5},{2,6},{3,7},{4,0},{5,1},{6,2},{7,3},{8,12},{9,13},{10,... | collective-permute-start | bytes 2764808 | tf_op jit(solution)/shard_map/ppermute | solution.py:921
  146.6 28.1 %copy-start.16 = (s16[528,512]{1,0:T(8,128)(2,1)S(1)}, s16[528,512]{1,0:T(8,128)(2,1)}, u32[]{:S(2)}) copy-start(s16[528,512]{1,0:T(8,128)(2,1)} %extend_slice.1) | copy-start | bytes 1622020
  146.6 32.8 %collective-permute-start.28 = (s16[528,512]{1,0:T(8,128)(2,1)}, s16[528,512]{1,0:T(8,128)(2,1)S(1)}, u32[]{:S(2)}, u32[]{:S(2)}) collective-permute-start(s16[528,512]{1,0:T(8,128)(2,1)} %extend_slice.1), channel_id=1, source_target_pairs={{0,2},{2,4},{4,6},{6,7},{7,5},{5,3},{3,1},{1,0},{8,10},{10,12},{12... | collective-permute-start | bytes 1622024 | tf_op jit(solution)/shard_map/ppermute | solution.py:812
  168.9 31.2 %collective-permute-start.31 = (s16[528,512]{1,0:T(8,128)(2,1)}, s16[528,512]{1,0:T(8,128)(2,1)}, u32[]{:S(2)}, u32[]{:S(2)}) collective-permute-start(s16[528,512]{1,0:T(8,128)(2,1)} %extend_slice.1), channel_id=1, source_target_pairs={{2,0},{4,2},{6,4},{7,6},{5,7},{3,5},{1,3},{0,1},{10,8},{12,10},{14... | collective-permute-start | bytes 1622024 | tf_op jit(solution)/shard_map/ppermute | solution.py:812
  173.3 35.0 %collective-permute-start.36 = (f32[128,2048]{1,0:T(8,128)}, f32[128,2048]{1,0:T(8,128)S(1)}, u32[]{:S(2)}, u32[]{:S(2)}) collective-permute-start(f32[128,2048]{1,0:T(8,128)} %extend_add.3.refs_0_), channel_id=1, source_target_pairs={{0,16},{8,24},{16,0},{24,8},{1,17},{9,25},{17,1},{25,9},{2,18},{10... | collective-permute-start | bytes 3145736 | tf_op jit(solution)/shard_map/ppermute | solution.py:866
  179.4 1.0 copy-start.15
  180.4 0.9 copy-start.7
  181.3 23.7 %collective-permute-start.29 = (s16[528,512]{1,0:T(8,128)(2,1)}, s16[528,512]{1,0:T(8,128)(2,1)S(1)}, u32[]{:S(2)}, u32[]{:S(2)}) collective-permute-start(s16[528,512]{1,0:T(8,128)(2,1)} %gate.5), channel_id=1, source_target_pairs={{0,2},{2,4},{4,6},{6,7},{7,5},{5,3},{3,1},{1,0},{8,10},{10,12},{12... | collective-permute-start | bytes 1622024 | tf_op jit(solution)/shard_map/ppermute | solution.py:812
  200.1 15.0 %collective-permute-start.32 = (s16[528,512]{1,0:T(8,128)(2,1)}, s16[528,512]{1,0:T(8,128)(2,1)}, u32[]{:S(2)}, u32[]{:S(2)}) collective-permute-start(s16[528,512]{1,0:T(8,128)(2,1)} %collective-permute-done.31), channel_id=1, source_target_pairs={{2,0},{4,2},{6,4},{7,6},{5,7},{3,5},{1,3},{0,1},{10,8},{12,10},{14... | collective-permute-start | bytes 1622024 | tf_op jit(solution)/shard_map/ppermute | solution.py:812
  202.0 6.3 %copy-start.4 = (f32[128,2048]{1,0:T(8,128)S(1)}, f32[128,2048]{1,0:T(8,128)}, u32[]{:S(2)}) copy-start(f32[128,2048]{1,0:T(8,128)} %extend_add.3.refs_0_) | copy-start | bytes 3145732
  205.0 1.0 copy-start.14
  205.9 13.6 %collective-permute-start.30 = (s16[528,512]{1,0:T(8,128)(2,1)}, s16[528,512]{1,0:T(8,128)(2,1)S(1)}, u32[]{:S(2)}, u32[]{:S(2)}) collective-permute-start(s16[528,512]{1,0:T(8,128)(2,1)} %gate.6), channel_id=1, source_target_pairs={{0,2},{2,4},{4,6},{6,7},{7,5},{5,3},{3,1},{1,0},{8,10},{10,12},{12... | collective-permute-start | bytes 1622024 | tf_op jit(solution)/shard_map/ppermute | solution.py:812
  208.3 26.9 %collective-permute-start.37 = (f32[128,2048]{1,0:T(8,128)S(1)}, f32[128,2048]{1,0:T(8,128)S(1)}, u32[]{:S(2)}, u32[]{:S(2)}) collective-permute-start(f32[128,2048]{1,0:T(8,128)S(1)} %copy-done.4), channel_id=1, source_target_pairs={{0,8},{8,0},{16,24},{24,16},{1,9},{9,1},{17,25},{25,17},{2,10},{10... | collective-permute-start | bytes 3145736 | tf_op jit(solution)/shard_map/ppermute | solution.py:866
  208.3 27.7 %copy-start.5 = (f32[128,2048]{1,0:T(8,128)}, f32[128,2048]{1,0:T(8,128)S(1)}, u32[]{:S(2)}) copy-start(f32[128,2048]{1,0:T(8,128)S(1)} %collective-permute-done.36.refs_4_.refs_1_) | copy-start | bytes 3145732
  208.3 27.6 %collective-permute-start.38 = (f32[128,2048]{1,0:T(8,128)S(1)}, f32[128,2048]{1,0:T(8,128)}, u32[]{:S(2)}, u32[]{:S(2)}) collective-permute-start(f32[128,2048]{1,0:T(8,128)S(1)} %collective-permute-done.36.refs_4_.refs_1_), channel_id=1, source_target_pairs={{0,8},{8,0},{16,24},{24,16},{1,9},{9,1},{17,25},{25,17},{2,10},{10... | collective-permute-start | bytes 3145736 | tf_op jit(solution)/shard_map/ppermute | solution.py:866
  215.1 13.5 %collective-permute-start.33 = (s16[528,512]{1,0:T(8,128)(2,1)}, s16[528,512]{1,0:T(8,128)(2,1)S(1)}, u32[]{:S(2)}, u32[]{:S(2)}) collective-permute-start(s16[528,512]{1,0:T(8,128)(2,1)} %collective-permute-done.32), channel_id=1, source_target_pairs={{2,0},{4,2},{6,4},{7,6},{5,7},{3,5},{1,3},{0,1},{10,8},{12,10},{14... | collective-permute-start | bytes 1622024 | tf_op jit(solution)/shard_map/ppermute | solution.py:812
  219.6 15.7 %copy-start.8 = (s16[528,512]{1,0:T(8,128)(2,1)}, s16[528,512]{1,0:T(8,128)(2,1)S(1)}, u32[]{:S(2)}) copy-start(s16[528,512]{1,0:T(8,128)(2,1)S(1)} %collective-permute-done.30.refs_1_) | copy-start | bytes 1622020
  219.6 9.3 %collective-permute-start.34 = (s16[264,512]{1,0:T(8,128)(2,1)S(1)}, s16[264,512]{1,0:T(8,128)(2,1)S(1)}, u32[]{:S(2)}, u32[]{:S(2)}) collective-permute-start(s16[264,512]{1,0:T(8,128)(2,1)S(1)} %slice.266), channel_id=1, source_target_pairs={{0,2},{2,4},{4,6},{6,7},{7,5},{5,3},{3,1},{1,0},{8,10},{10,12},{12... | collective-permute-start | bytes 811016 | tf_op jit(solution)/shard_map/ppermute | solution.py:818
  228.5 6.7 %copy-start.10 = (s16[528,512]{1,0:T(8,128)(2,1)}, s16[528,512]{1,0:T(8,128)(2,1)S(1)}, u32[]{:S(2)}) copy-start(s16[528,512]{1,0:T(8,128)(2,1)S(1)} %collective-permute-done.33.refs_2_) | copy-start | bytes 1622020
  228.6 6.6 %collective-permute-start.35 = (s16[264,512]{1,0:T(8,128)(2,1)S(1)}, s16[264,512]{1,0:T(8,128)(2,1)S(1)}, u32[]{:S(2)}, u32[]{:S(2)}) collective-permute-start(s16[264,512]{1,0:T(8,128)(2,1)S(1)} %slice.267), channel_id=1, source_target_pairs={{2,0},{4,2},{6,4},{7,6},{5,7},{3,5},{1,3},{0,1},{10,8},{12,10},{14... | collective-permute-start | bytes 811016 | tf_op jit(solution)/shard_map/ppermute | solution.py:818
  235.2 0.8 copy-start.12
  236.0 1.0 copy-start.6
  237.0 9.5 %copy-start.9 = (s16[528,512]{1,0:T(8,128)(2,1)S(1)}, s16[528,512]{1,0:T(8,128)(2,1)}, u32[]{:S(2)}) copy-start(s16[528,512]{1,0:T(8,128)(2,1)} %copy-done.8) | copy-start | bytes 1622020
  237.0 9.5 %copy-start.11 = (s16[528,512]{1,0:T(8,128)(2,1)S(1)}, s16[528,512]{1,0:T(8,128)(2,1)}, u32[]{:S(2)}) copy-start(s16[528,512]{1,0:T(8,128)(2,1)} %copy-done.10) | copy-start | bytes 1622020
  237.0 9.5 %copy-start.13 = (s16[528,512]{1,0:T(8,128)(2,1)S(1)}, s16[528,512]{1,0:T(8,128)(2,1)}, u32[]{:S(2)}) copy-start(s16[528,512]{1,0:T(8,128)(2,1)} %copy-done.12) | copy-start | bytes 1622020
  237.0 83.5 %all-to-all-start.2 = ((bf16[16,1552,128]{2,1,0:T(8,128)(2,1)}), bf16[16,1552,128]{2,1,0:T(8,128)(2,1)}, u32[]{:S(2)}, u32[]{:S(2)}) async-start(bf16[16,1552,128]{2,1,0:T(8,128)(2,1)} %gate.7), calls=%async_computation.2 | async-start | bytes 12713984 | tf_op jit(solution)/shard_map/all_to_all | solution.py:903
  241.8 6.0 %copy-start.1 = (f32[512,512]{1,0:T(8,128)S(1)}, f32[512,512]{1,0:T(8,128)}, u32[]{:S(2)}) copy-start(f32[512,512]{1,0:T(8,128)} %pivot_ref.1) | copy-start | bytes 3145732
  241.9 39.6 %copy-start.21 = (s32[2]{0:T(128)}, s32[2]{0:T(128)S(1)}, u32[]{:S(2)}) copy-start(s32[2]{0:T(128)S(1)} %pad_add_fusion.3.flag_ref) | copy-start | bytes 28
  322.7 16.4 %collective-permute-start.39 = (s32[8,128]{1,0:T(8,128)S(1)}, s32[8,128]{1,0:T(8,128)S(1)}, u32[]{:S(2)}, u32[]{:S(2)}) collective-permute-start(s32[8,128]{1,0:T(8,128)S(1)} %broadcast_in_dim.19), channel_id=1, source_target_pairs={{0,4},{1,5},{2,6},{3,7},{4,0},{5,1},{6,2},{7,3},{8,12},{9,13},{10,... | collective-permute-start | bytes 12296 | tf_op jit(solution)/shard_map/ppermute | solution.py:931
  326.8 13.7 %copy-start.22 = (s32[2]{0:T(128)S(1)}, s32[2]{0:T(128)}, u32[]{:S(2)}) copy-start(s32[2]{0:T(128)} %copy-done.21) | copy-start | bytes 28
  326.8 13.7 %copy-start.23 = (s32[128]{0:T(128)S(1)}, s32[128]{0:T(128)}, u32[]{:S(2)}) copy-start(s32[128]{0:T(128)} %param.12) | copy-start | bytes 1540
  326.8 13.7 %copy-start.24 = (s32[128,1]{0,1:T(1,128)S(1)}, s32[128,1]{0,1:T(1,128)}, u32[]{:S(2)}) copy-start(s32[128,1]{0,1:T(1,128)} %param.11) | copy-start | bytes 1540
